TPU v7x, 128 devices: a whole 4x4x4 slice. The times are simulated.
128 devices in a mesh: tile: 32 (over y, x, core), knot: 4 (over z).
Axes of the slice: x: 4, y: 4, z: 4, core: 2. Of those that a mesh axis runs over, the one named last changes fastest.
Arguments:
- images: float32 [32, 32, 65536], P('tile', 'knot'), may hold values from -6 to 6
- gradient: float32 [32, 32, 65536], P('tile', 'knot'), may hold values from -3 to 3
- shifts: int32 [32], P('tile'), may hold values from -4 to 4
- tile_blocks: int32 [32, 2], P('tile'), may hold values from 0 to 127, as said below
- intersections: int32 [32, 3, 8, 5], P('tile'), may hold values from 0 to 57344, as said below
- start_coefficients: float32 [128, 64], P(('tile', 'knot')), may hold values from -0.6 to 0.6
Outputs:
- coefficients: float32 [128, 64], P(('tile', 'knot'))
- warped: float32 [32, 32, 65536], P('tile', 'knot')
Inputs may be any that keep to these rules, and one draw needn't show every extreme that they name: intersections[s, d, m] holds the sending tile's index among the 1 tiles of owner s, its slab offset, the receiving tile's index among the tiles of owner s + d - 1, its slab offset, and a live flag; live slots of one sender and direction come first; no live slot points outside the owners; some owner receives 8 live slots from each of its three senders, and some sender fills 8 slots of a direction. `tile_blocks`: the blocks of a tile held by tile owner i are owned by tile owners i - 1, i or i + 1, block b being owned by device b div 1 in the order of tile and knot joined.
All inputs are finite; a program needn't handle non-finite values.
Results may differ from a plain program's by a relative error of at most 0.0003.
Values sent between devices are 32-bit elements; how exact they have to be, the bound alone decides.
No kernel may reach another device: no remote copies, remote signals or barrier semaphores. Data moves between devices by JAX's collectives and lax.ppermute only.
A program may use at most 576 MiB of HBM per device.

v0:
```python
import jax
import jax.numpy as jnp
from jax import lax
from jax.sharding import PartitionSpec as P

SLAB = 8192
ITERS = 2


shift_step = 0.05
smooth_weight = 20.0
ridge_weight = 1.0


def extended(block, sides, width):
    for axis, dim in sides:
        count = lax.axis_size(axis)
        forward = [(i, i + 1) for i in range(count - 1)]
        backward = [(target, source) for source, target in forward]
        low = lax.ppermute(
            lax.slice_in_dim(block, block.shape[dim] - width, None, axis=dim), axis, forward
        )
        high = lax.ppermute(lax.slice_in_dim(block, 0, width, axis=dim), axis, backward)
        block = jnp.concatenate([low, block, high], axis=dim)
    return block


def from_behind(block, axis, distance):
    devices = range(lax.axis_size(axis))
    route = [(i - distance, i) for i in devices if i - distance in devices]
    return lax.ppermute(block, axis, route)


def spline_basis(plane, knots):
    place = jnp.arange(plane, dtype=jnp.float32) * ((knots - 3) / plane) + 1.0
    offset = place[None, :] - jnp.arange(knots, dtype=jnp.float32)[:, None]
    dist = jnp.abs(offset)
    inner = 2.0 / 3.0 - dist * dist + 0.5 * dist * dist * dist
    outer = (2.0 - dist) * (2.0 - dist) * (2.0 - dist) / 6.0
    return jnp.where(dist < 1.0, inner, jnp.where(dist < 2.0, outer, 0.0))


def smoothing(block):
    rows = jnp.arange(block - 2, dtype=jnp.int32)[:, None]
    cols = jnp.arange(block, dtype=jnp.int32)[None, :]
    second = (
        (cols == rows).astype(jnp.float32)
        - 2.0 * (cols == rows + 1).astype(jnp.float32)
        + (cols == rows + 2).astype(jnp.float32)
    )
    return jnp.dot(second.T, second, precision=lax.Precision.HIGHEST)


def block_update(normal, gradsum, coef, penalty):
    size = normal.shape[-1]
    system = normal + smooth_weight * penalty + ridge_weight * jnp.eye(size, dtype=jnp.float32)
    pull = jnp.einsum("kl,bl->bk", penalty, coef, precision=lax.Precision.HIGHEST)
    target = -(gradsum + smooth_weight * pull)
    factor = lax.linalg.cholesky(system)
    middle = lax.linalg.triangular_solve(factor, target[..., None], left_side=True, lower=True)
    update = lax.linalg.triangular_solve(
        factor, middle, left_side=True, lower=True, transpose_a=True
    )
    return coef + update[..., 0]


def per_device(images, gradient, shifts, tile_blocks, intersections, start_coefficients):
    tile_dev, depth, plane = images.shape
    kb_dev, block = start_coefficients.shape
    slab = SLAB
    basis = spline_basis(plane, 2 * block)
    penalty = smoothing(block)
    knot_count = lax.axis_size("knot")
    here = lax.axis_index("tile")
    links = intersections[0]
    cap = links.shape[1]
    flat = links.reshape(3 * cap, 5)
    rigid = shift_step * shifts.astype(jnp.float32)
    window = kb_dev * knot_count
    owned_tiles = jnp.arange(tile_dev, dtype=jnp.int32)

    def fetch(owned):
        column = lax.all_gather(owned, "knot", axis=0, tiled=True)
        table = extended(column, (("tile", 0),), window)
        first = (here - 1) * window
        wanted = tile_blocks.reshape(-1) - first
        select = (wanted[:, None] == jnp.arange(table.shape[0], dtype=jnp.int32)[None, :]).astype(
            jnp.float32
        )
        return jnp.dot(select, table, precision=lax.Precision.HIGHEST).reshape(tile_dev, 2 * block)

    def warp_tiles(owned):
        local = fetch(owned)
        field = jnp.dot(local, basis, precision=lax.Precision.HIGHEST) + rigid[:, None]
        return images + gradient * field[:, None, :]

    def cut(volume, which, start):
        return lax.dynamic_slice(volume, (which, 0, start), (1, depth, slab))[0]

    def cut_basis(start):
        return lax.dynamic_slice(basis, (0, start), (2 * block, slab))

    coef = start_coefficients
    for step in range(ITERS):
        tiles = warp_tiles(coef)
        slabs = jax.vmap(cut, (None, 0, 0))(tiles, flat[:, 0], flat[:, 1]).reshape(
            3, cap, depth, slab
        )
        labels = flat[:, 2:].astype(jnp.float32).reshape(3, cap, 3)
        below = from_behind((slabs[2], labels[2]), "tile", 1)
        above = from_behind((slabs[0], labels[0]), "tile", -1)
        arrived = jnp.stack([below[0], slabs[1], above[0]])
        arrived_labels = jnp.stack([below[1], labels[1], above[1]])
        arrived = arrived.reshape(3 * cap, depth, slab)
        arrived_labels = arrived_labels.reshape(3 * cap, 3)
        tile_a = arrived_labels[:, 0].astype(jnp.int32)
        off_a = arrived_labels[:, 1].astype(jnp.int32)
        alive = arrived_labels[:, 2]
        near = jax.vmap(cut, (None, 0, 0))(tiles, tile_a, off_a)
        slope = jax.vmap(cut, (None, 0, 0))(gradient, tile_a, off_a)
        misfit = (near - arrived) * alive[:, None, None]
        weight = jnp.sum(slope * slope, axis=1) * alive[:, None]
        project = jnp.sum(slope * misfit, axis=1)
        piece = jax.vmap(cut_basis)(off_a).reshape(3 * cap, 2, block, slab)
        normals = jnp.einsum(
            "pnks,pnls->pnkl",
            piece * weight[:, None, None, :],
            piece,
            precision=lax.Precision.HIGHEST,
        )
        grads = jnp.einsum("pnks,ps->pnk", piece, project, precision=lax.Precision.HIGHEST)
        pick = (tile_a[:, None] == owned_tiles[None, :]).astype(jnp.int32)
        dest = jnp.sum(pick[:, :, None] * tile_blocks[None, :, :], axis=1).reshape(-1)
        normals = normals.reshape(-1, block, block)
        grads = grads.reshape(-1, block)
        rows = dest - (here - 1) * window
        select = (jnp.arange(3 * window, dtype=jnp.int32)[:, None] == rows[None, :]).astype(
            jnp.float32
        )
        normal_term = jnp.einsum(
            "bq,qkl->bkl", select, normals, precision=lax.Precision.HIGHEST
        ).reshape(3, knot_count, kb_dev, block, block)
        grad_term = jnp.dot(select, grads, precision=lax.Precision.HIGHEST).reshape(
            3, knot_count, kb_dev, block
        )
        column_normal, column_grad = (
            lax.psum_scatter(normal_term, "knot", scatter_dimension=1, tiled=True),
            lax.psum_scatter(grad_term, "knot", scatter_dimension=1, tiled=True),
        )
        upper = from_behind((column_normal[0], column_grad[0]), "tile", -1)
        lower = from_behind((column_normal[2], column_grad[2]), "tile", 1)
        normal_sum = (column_normal[1] + upper[0] + lower[0]).reshape(kb_dev, block, block)
        grad_sum = (column_grad[1] + upper[1] + lower[1]).reshape(kb_dev, block)
        coef = block_update(normal_sum, grad_sum, coef, penalty)
    warped = warp_tiles(coef)
    return (coef, warped)


def solution(mesh):
    placed = (
        P("tile", "knot", None),
        P("tile", "knot", None),
        P("tile"),
        P("tile", None),
        P("tile", None, None, None),
        P(("tile", "knot"), None),
    )
    return jax.shard_map(
        per_device,
        mesh=mesh,
        in_specs=placed,
        out_specs=(P(("tile", "knot"), None), P("tile", "knot", None)),
        check_vma=False,
    )
```

profile of v0, /device:TPU:24, one launch (start us, length us, event | category | flops | bytes accessed | tf_op | source)
XLA Modules:
  0.0 1186.2 jit_solution(12496819525911956714)
XLA Ops:
  7.2 11.1 all-gather
  33.6 19.4 %fusion.4 = f32[128,65536]{1,0:T(8,128)} fusion(f32[65536]{0:T(1024)S(1)} %multiply_add_fusion.3), kind=kLoop, calls=%fused_computation.18 | loop fusion | flops 134217728 | bytes 33816576 | tf_op jit(solution)/shard_map/jit(_where)/select_n | solution.py:40
  54.6 155.9 %while.6 = (s32[]{:T(128)}, f32[128,65536]{1,0:T(8,128)}, s32[24,2]{0,1:T(2,128)S(1)}, f32[24,128,8192]{2,1,0:T(8,128)}, s32[]{:T(128)}) while((s32[]{:T(128)}, f32[128,65536]{1,0:T(8,128)}, s32[24,2]{0,1:T(2,128)S(1)}, f32[24,128,8192]{2,1,0:T(8,128)}, s32[]{:T(128)}) %tuple.92), condition=%wide.while_cond, body=%wide.while_body.sunk | while | flops 2 | bytes 8389221 | solution.py:101
  61.6 5.9 bitcast_dynamic-update-slice_fusion.12
  68.2 5.9 bitcast_dynamic-update-slice_fusion.12
  87.6 5.9 bitcast_dynamic-update-slice_fusion.12
  94.1 5.9 bitcast_dynamic-update-slice_fusion.12
  107.1 6.0 bitcast_dynamic-update-slice_fusion.12
  113.6 5.9 bitcast_dynamic-update-slice_fusion.12
  133.1 6.0 bitcast_dynamic-update-slice_fusion.12
  139.6 5.9 bitcast_dynamic-update-slice_fusion.12
  159.1 5.9 bitcast_dynamic-update-slice_fusion.12
  172.1 5.9 bitcast_dynamic-update-slice_fusion.12
  185.0 5.9 bitcast_dynamic-update-slice_fusion.12
  204.5 5.9 bitcast_dynamic-update-slice_fusion.12
  213.7 49.9 %while.7 = (s32[]{:T(128)}, f32[1,8,65536]{2,1,0:T(8,128)S(1)}, s32[24,3]{0,1:T(4,128)S(1)}, f32[24,1,8,8192]{3,2,1,0:T(8,128)}, s32[]{:T(128)}) while((s32[]{:T(128)}, f32[1,8,65536]{2,1,0:T(8,128)S(1)}, s32[24,3]{0,1:T(4,128)S(1)}, f32[24,1,8,8192]{3,2,1,0:T(8,128)}, s32[]{:T(128)}) %tuple.112), condition=%wide.while_cond.1, body=%wide.while_body.1.sunk | while | flops 2 | bytes 524909 | solution.py:98
  264.0 33.4 %fusion.14 = f32[1,65536]{1,0:T(1,128)S(1)} fusion(f32[128,1]{0,1:T(1,128)S(1)} %reshape.516, f32[65536]{0:T(1024)S(1)} %multiply_add_fusion.3), kind=kOutput, calls=%fused_computation.27 | convolution fusion | flops 234881024 | bytes 524800 | tf_op jit(solution)/shard_map/dot_general | solution.py:94
  302.5 69.4 %while.9 = (s32[]{:T(128)}, f32[1,8,65536]{2,1,0:T(8,128)}, s32[24,3]{0,1:T(4,128)S(1)}, f32[24,1,8,8192]{3,2,1,0:T(8,128)}, s32[]{:T(128)}) while((s32[]{:T(128)}, f32[1,8,65536]{2,1,0:T(8,128)}, s32[24,3]{0,1:T(4,128)S(1)}, f32[24,1,8,8192]{3,2,1,0:T(8,128)}, s32[]{:T(128)}) %tuple.95), condition=%wide.while_cond.3, body=%wide.while_body.3.sunk | while | flops 2 | bytes 524909 | solution.py:98
  387.4 74.0 %while.8 = (s32[]{:T(128)}, f32[1,8,65536]{2,1,0:T(8,128)}, s32[24,3]{0,1:T(4,128)S(1)}, f32[24,1,8,8192]{3,2,1,0:T(8,128)}, s32[]{:T(128)}) while((s32[]{:T(128)}, f32[1,8,65536]{2,1,0:T(8,128)}, s32[24,3]{0,1:T(4,128)S(1)}, f32[24,1,8,8192]{3,2,1,0:T(8,128)}, s32[]{:T(128)}) %tuple.115), condition=%wide.while_cond.2, body=%wide.while_body.2.sunk | while | flops 2 | bytes 524909 | solution.py:98
  468.6 12.7 %fusion.21 = (f32[24,8192]{1,0:T(8,128)}, f32[24,8192]{1,0:T(8,128)}) fusion(f32[3,8,8,8192]{3,2,1,0:T(8,128)} %pad_maximum_fusion, f32[24,1,8,8192]{3,2,1,0:T(8,128)} %get-tuple-element.28, f32[24,1,8,8192]{3,2,1,0:T(8,128)} %get-tuple-element.20, f32[24]{0:T(128)S(1)} %slice_bitcast_fusion.7), kind=kLoop, calls=%fused_computation.37 | loop fusion | flops 9043968 | bytes 20447328 | tf_op jit(solution)/shard_map/reduce_sum | solution.py:123
  482.5 102.3 %fusion = f32[24,2,64,64]{3,2,1,0:T(8,128)} fusion(f32[24,2,64,8192]{3,2,1,0:T(8,128)} %bitcast.7, f32[24,8192]{1,0:T(8,128)S(1)} %broadcast_multiply_fusion), kind=kOutput, calls=%fused_computation.12 | convolution fusion | flops 19352518656 | bytes 102236160 | tf_op jit(solution)/shard_map/pnks,pnls->pnkl/dot_general | solution.py:125
  588.7 121.6 %fusion.33 = f32[24,1,2,64]{3,1,2,0:T(1,128)S(1)} fusion(f32[24,2,64,8192]{3,2,1,0:T(8,128)} %bitcast.7, f32[24,8192,1,1]{1,0,2,3:T(8,128)} %bitcast.316), kind=kOutput, calls=%fused_computation.65 | convolution fusion | flops 301989888 | bytes 101462016 | tf_op jit(solution)/shard_map/pnks,ps->pnk/dot_general | solution.py:131
  710.5 7.9 all-reduce.2
  750.5 8.9 all-gather.1
  768.5 33.3 %fusion.12 = f32[1,65536]{1,0:T(1,128)S(1)} fusion(f32[128,1]{0,1:T(1,128)S(1)} %reshape.527, f32[65536]{0:T(1024)S(1)} %multiply_add_fusion.3), kind=kOutput, calls=%fused_computation.26 | convolution fusion | flops 234881024 | bytes 524800 | tf_op jit(solution)/shard_map/dot_general | solution.py:94
  806.8 75.0 %while.11 = (s32[]{:T(128)}, f32[1,8,65536]{2,1,0:T(8,128)}, s32[24,3]{0,1:T(4,128)S(1)}, f32[24,1,8,8192]{3,2,1,0:T(8,128)}, s32[]{:T(128)}) while((s32[]{:T(128)}, f32[1,8,65536]{2,1,0:T(8,128)}, s32[24,3]{0,1:T(4,128)S(1)}, f32[24,1,8,8192]{3,2,1,0:T(8,128)}, s32[]{:T(128)}) %tuple.117), condition=%wide.while_cond.5, body=%wide.while_body.5.sunk | while | flops 2 | bytes 524909 | solution.py:98
  894.0 72.8 %while.10 = (s32[]{:T(128)}, f32[1,8,65536]{2,1,0:T(8,128)}, s32[24,3]{0,1:T(4,128)S(1)}, f32[24,1,8,8192]{3,2,1,0:T(8,128)}, s32[]{:T(128)}) while((s32[]{:T(128)}, f32[1,8,65536]{2,1,0:T(8,128)}, s32[24,3]{0,1:T(4,128)S(1)}, f32[24,1,8,8192]{3,2,1,0:T(8,128)}, s32[]{:T(128)}) %tuple.116), condition=%wide.while_cond.4, body=%wide.while_body.4.sunk | while | flops 2 | bytes 524909 | solution.py:98
  973.9 9.7 fusion.18
  983.7 122.1 %fusion.31 = f32[24,1,2,64]{3,1,2,0:T(1,128)S(1)} fusion(f32[24,2,64,8192]{3,2,1,0:T(8,128)} %bitcast.7, f32[24,8192,1,1]{1,0,2,3:T(8,128)S(1)} %bitcast.317), kind=kOutput, calls=%fused_computation.63 | convolution fusion | flops 301989888 | bytes 101462016 | tf_op jit(solution)/shard_map/pnks,ps->pnk/dot_general | solution.py:131
  1106.0 7.9 all-reduce.3
  1124.5 8.9 all-gather.2
  1144.3 32.9 %fusion.10 = f32[1,65536]{1,0:T(1,128)S(1)} fusion(f32[128,1]{0,1:T(1,128)S(1)} %reshape.538, f32[65536]{0:T(1024)S(1)} %multiply_add_fusion.3), kind=kOutput, calls=%fused_computation.25 | convolution fusion | flops 234881024 | bytes 524800 | tf_op jit(solution)/shard_map/dot_general | solution.py:94
  (551 shorter events, 567.0 us)
Async XLA Ops:
  7.2 711.3 %all-reduce.6.cloned.1.call-start = ((), (), s32[]{:S(2)}) async-start(), calls=%async_computation | async-start | bytes 786432
  18.3 245.4 %collective-permute-start.5 = (f32[4,64]{1,0:T(4,128)S(1)}, f32[4,64]{1,0:T(4,128)S(1)}, u32[]{:S(2)}, u32[]{:S(2)}) collective-permute-start(f32[4,64]{1,0:T(4,128)S(1)} %bitcast.327), channel_id=1, source_target_pairs={{4,0},{8,4},{12,8},{16,12},{20,16},{24,20},{28,24},{32,28},{36,32}... | collective-permute-start | bytes 3080 | tf_op jit(solution)/shard_map/ppermute | solution.py:23
  20.6 243.2 %collective-permute-start.4 = (f32[4,64]{1,0:T(4,128)S(1)}, f32[4,64]{1,0:T(4,128)S(1)}, u32[]{:S(2)}, u32[]{:S(2)}) collective-permute-start(f32[4,64]{1,0:T(4,128)S(1)} %bitcast.328), channel_id=1, source_target_pairs={{0,4},{4,8},{8,12},{12,16},{16,20},{20,24},{24,28},{28,32},{32,36}... | collective-permute-start | bytes 3080 | tf_op jit(solution)/shard_map/ppermute | solution.py:20
  23.5 30.9 %collective-permute-start.1 = (f32[8,3]{0,1:T(4,128)S(1)}, f32[8,3]{0,1:T(4,128)S(1)}, u32[]{:S(2)}, u32[]{:S(2)}) collective-permute-start(f32[8,3]{0,1:T(4,128)S(1)} %get-tuple-element.118), channel_id=1, source_target_pairs={{4,0},{8,4},{12,8},{16,12},{20,16},{24,20},{28,24},{32,28},{36,32}... | collective-permute-start | bytes 296 | tf_op jit(solution)/shard_map/ppermute | solution.py:31
  29.1 25.3 %collective-permute-start = (f32[8,3]{0,1:T(4,128)S(1)}, f32[8,3]{0,1:T(4,128)S(1)}, u32[]{:S(2)}, u32[]{:S(2)}) collective-permute-start(f32[8,3]{0,1:T(4,128)S(1)} %get-tuple-element.117), channel_id=1, source_target_pairs={{0,4},{4,8},{8,12},{12,16},{16,20},{20,24},{24,28},{28,32},{32,36}... | collective-permute-start | bytes 296 | tf_op jit(solution)/shard_map/ppermute | solution.py:31
  31.5 21.5 %copy-start.4 = (f32[64,64]{1,0:T(8,128)}, f32[64,64]{1,0:T(8,128)S(1)}, u32[]{:S(2)}) copy-start(f32[64,64]{1,0:T(8,128)S(1)} %fusion.46) | copy-start | bytes 49156
  33.6 20.1 %copy-start.10 = (s32[1,2]{1,0:T(1,128)S(1)}, s32[1,2]{1,0:T(1,128)}, u32[]{:S(2)}) copy-start(s32[1,2]{1,0:T(1,128)} %param.14) | copy-start | bytes 28
  33.6 20.1 %copy-start.11 = (u32[128]{0:T(128)S(1)}, u32[128]{0:T(128)}, u32[]{:S(2)}) copy-start(u32[128]{0:T(128)} %constant.171) | copy-start | bytes 1540
  54.5 159.2 %copy-start = (f32[1,8,65536]{2,1,0:T(8,128)S(1)}, f32[1,8,65536]{2,1,0:T(8,128)}, u32[]{:S(2)}) copy-start(f32[1,8,65536]{2,1,0:T(8,128)} %param.12) | copy-start | bytes 6291460
  264.0 33.4 %copy-start.1 = (f32[1,8,65536]{2,1,0:T(8,128)S(1)}, f32[1,8,65536]{2,1,0:T(8,128)}, u32[]{:S(2)}) copy-start(f32[1,8,65536]{2,1,0:T(8,128)} %param.11) | copy-start | bytes 6291460
  376.4 86.8 %collective-permute-start.7 = (f32[8,8,8192]{2,1,0:T(8,128)}, f32[8,8,8192]{2,1,0:T(8,128)}, u32[]{:S(2)}, u32[]{:S(2)}) collective-permute-start(f32[8,8,8192]{2,1,0:T(8,128)} %get-tuple-element.106), channel_id=1, source_target_pairs={{4,0},{8,4},{12,8},{16,12},{20,16},{24,20},{28,24},{32,28},{36,32}... | collective-permute-start | bytes 6291464 | tf_op jit(solution)/shard_map/ppermute | solution.py:31
  382.2 81.0 %collective-permute-start.6 = (f32[8,8,8192]{2,1,0:T(8,128)}, f32[8,8,8192]{2,1,0:T(8,128)}, u32[]{:S(2)}, u32[]{:S(2)}) collective-permute-start(f32[8,8,8192]{2,1,0:T(8,128)} %get-tuple-element.105), channel_id=1, source_target_pairs={{0,4},{4,8},{8,12},{12,16},{16,20},{20,24},{24,28},{28,32},{32,36}... | collective-permute-start | bytes 6291464 | tf_op jit(solution)/shard_map/ppermute | solution.py:31
  588.7 147.2 %copy-start.6 = (f32[64,64]{0,1:T(8,128)S(1)}, f32[64,64]{0,1:T(8,128)}, u32[]{:S(2)}) copy-start(f32[64,64]{0,1:T(8,128)} %copy.32) | copy-start | bytes 49156
  588.7 160.8 %copy-start.8 = (f32[64]{0:T(128)S(1)}, f32[64]{0:T(128)}, u32[]{:S(2)}) copy-start(f32[64]{0:T(128)} %fusion.30) | copy-start | bytes 772
  588.7 161.6 %copy-start.7 = (f32[1,64]{1,0:T(1,128)S(1)}, f32[1,64]{1,0:T(1,128)}, u32[]{:S(2)}) copy-start(f32[1,64]{1,0:T(1,128)} %param.16) | copy-start | bytes 772
  719.9 16.0 %collective-permute-start.3 = (f32[1,1,64,64]{2,3,1,0:T(8,128)S(1)}, f32[1,1,64,64]{2,3,1,0:T(8,128)S(1)}, u32[]{:S(2)}, u32[]{:S(2)}) collective-permute-start(f32[1,1,64,64]{2,3,1,0:T(8,128)S(1)} %get-tuple-element.108), channel_id=1, source_target_pairs={{0,4},{4,8},{8,12},{12,16},{16,20},{20,24},{24,28},{28,32},{32,36}... | collective-permute-start | bytes 49160 | tf_op jit(solution)/shard_map/ppermute | solution.py:31
  721.8 14.1 %collective-permute-start.2 = (f32[1,1,64,64]{2,3,1,0:T(8,128)S(1)}, f32[1,1,64,64]{2,3,1,0:T(8,128)S(1)}, u32[]{:S(2)}, u32[]{:S(2)}) collective-permute-start(f32[1,1,64,64]{2,3,1,0:T(8,128)S(1)} %get-tuple-element.107), channel_id=1, source_target_pairs={{4,0},{8,4},{12,8},{16,12},{20,16},{24,20},{28,24},{32,28},{36,32}... | collective-permute-start | bytes 49160 | tf_op jit(solution)/shard_map/ppermute | solution.py:31
  728.2 21.3 %collective-permute-start.9 = (f32[1,1,64]{2,1,0:T(1,128)S(1)}, f32[1,1,64]{2,1,0:T(1,128)S(1)}, u32[]{:S(2)}, u32[]{:S(2)}) collective-permute-start(f32[1,1,64]{2,1,0:T(1,128)S(1)} %get-tuple-element.112), channel_id=1, source_target_pairs={{0,4},{4,8},{8,12},{12,16},{16,20},{20,24},{24,28},{28,32},{32,36}... | collective-permute-start | bytes 776 | tf_op jit(solution)/shard_map/ppermute | solution.py:31
  730.1 19.4 %collective-permute-start.8 = (f32[1,1,64]{2,1,0:T(1,128)S(1)}, f32[1,1,64]{2,1,0:T(1,128)S(1)}, u32[]{:S(2)}, u32[]{:S(2)}) collective-permute-start(f32[1,1,64]{2,1,0:T(1,128)S(1)} %get-tuple-element.111), channel_id=1, source_target_pairs={{4,0},{8,4},{12,8},{16,12},{20,16},{24,20},{28,24},{32,28},{36,32}... | collective-permute-start | bytes 776 | tf_op jit(solution)/shard_map/ppermute | solution.py:31
  759.3 4.3 collective-permute-start.11
  761.2 7.0 collective-permute-start.10
  768.5 33.3 %copy-start.2 = (f32[1,8,65536]{2,1,0:T(8,128)S(1)}, f32[1,8,65536]{2,1,0:T(8,128)}, u32[]{:S(2)}) copy-start(f32[1,8,65536]{2,1,0:T(8,128)} %param.11) | copy-start | bytes 6291460
  886.4 82.1 %collective-permute-start.13 = (f32[8,8,8192]{2,1,0:T(8,128)}, f32[8,8,8192]{2,1,0:T(8,128)}, u32[]{:S(2)}, u32[]{:S(2)}) collective-permute-start(f32[8,8,8192]{2,1,0:T(8,128)} %get-tuple-element.104), channel_id=1, source_target_pairs={{4,0},{8,4},{12,8},{16,12},{20,16},{24,20},{28,24},{32,28},{36,32}... | collective-permute-start | bytes 6291464 | tf_op jit(solution)/shard_map/ppermute | solution.py:31
  888.3 80.2 %collective-permute-start.12 = (f32[8,8,8192]{2,1,0:T(8,128)}, f32[8,8,8192]{2,1,0:T(8,128)}, u32[]{:S(2)}, u32[]{:S(2)}) collective-permute-start(f32[8,8,8192]{2,1,0:T(8,128)} %get-tuple-element.103), channel_id=1, source_target_pairs={{0,4},{4,8},{8,12},{12,16},{16,20},{20,24},{24,28},{28,32},{32,36}... | collective-permute-start | bytes 6291464 | tf_op jit(solution)/shard_map/ppermute | solution.py:31
  983.7 138.6 %copy-start.5 = (f32[64,64]{1,0:T(8,128)S(1)}, f32[64,64]{1,0:T(8,128)}, u32[]{:S(2)}) copy-start(f32[64,64]{1,0:T(8,128)} %copy-done.4) | copy-start | bytes 49156
  1114.6 7.8 collective-permute-start.15
  1116.5 7.0 collective-permute-start.14
  1124.5 52.7 %copy-start.9 = (f32[1,64]{1,0:T(1,128)}, f32[1,64]{1,0:T(1,128)S(1)}, u32[]{:S(2)}) copy-start(f32[1,64]{1,0:T(1,128)S(1)} %convolution_add_fusion) | copy-start | bytes 772
  1133.4 5.6 collective-permute-start.17
  1137.0 7.0 collective-permute-start.16
  1144.3 32.9 %copy-start.3 = (f32[1,8,65536]{2,1,0:T(8,128)S(1)}, f32[1,8,65536]{2,1,0:T(8,128)}, u32[]{:S(2)}) copy-start(f32[1,8,65536]{2,1,0:T(8,128)} %param.11) | copy-start | bytes 6291460
Sparse Core Ops, SparseCore 0:
  588.8 42.1 all-reduce.5
where the time goes:
time: 1200 us; the launch traced here: 1190 us
  local copies, waits for them, and re-layouts  532 us (44%)
  matrix products  453 us (38%)
  other arithmetic  72.7 us (6%)
  starting transfers between devices  56.8 us (5%)
  blocking collectives  44.7 us (4%)
  between operations  15.7 us (1%)
    gather x432, local copies, waits for them, and re-layouts  497 us
    dot_general x2, matrix products, per_device(): jnp.einsum('pnks,ps->pnk', piece, project, precision=lax.Precision.HIGHEST)  244 us
    dot_general x1, matrix products, per_device(): jnp.einsum('pnks,pnls->pnkl', piece * weight[:, None, None, :], piece, pr...  102 us
    dot_general x3, matrix products, warp_tiles(): jnp.dot(local, basis, precision=lax.Precision.HIGHEST) + rigid[:, None]  99.5 us
    ppermute x12, starting transfers between devices, from_behind(): return lax.ppermute(block, axis, route)  42.5 us
    all_gather x3, blocking collectives, fetch(): column = lax.all_gather(owned, 'knot', axis=0, tiled=True)  28.8 us
  transfers between devices with their start and end apart: 19, of which 3 were waited for; matrix products, arithmetic and copies ran while one was open for 44% of the time, Pallas kernels for 0%

commit v1 on v0

v1 whole, which is shorter than its diff:
```python
import functools

import jax
import jax.numpy as jnp
from jax import lax
from jax.experimental import pallas as pl
from jax.experimental.pallas import tpu as pltpu
from jax.sharding import PartitionSpec as P

SLAB = 8192
BLOCK = 64
LANES = 128
ROWS = 512
DEPTH = 8
LEAD = 8
PADDED = LEAD + ROWS + 16
GROUPS = SLAB // (8 * LANES) + 1
SLAB_ROWS = 8 * GROUPS
CAP = 8

shift_step = 0.05
smooth_weight = 20.0
ridge_weight = 1.0

EXACT = lax.Precision.HIGHEST
VMEM_LIMIT = 48 * 1024 * 1024


def iota(shape, dim):
    return lax.broadcasted_iota(jnp.int32, shape, dim)


def dot(a, b):
    return lax.dot_general(
        a, b, (((1,), (0,)), ((), ())), precision=EXACT, preferred_element_type=jnp.float32
    )


def dot_rows(a, b):
    return lax.dot_general(
        a, b, (((1,), (1,)), ((), ())), precision=EXACT, preferred_element_type=jnp.float32
    )


class Spline:
    def __init__(self):
        row = iota((ROWS, LANES), 0)
        lane = iota((ROWS, LANES), 1)
        self.low = (((row * LANES + lane) * 125) >> 16) == ((row * 125) >> 9)
        self.hot = (lane == ((row * 125) >> 9)).astype(jnp.float32)
        sub = iota((8, ROWS), 0)
        col = iota((8, ROWS), 1)
        first = (col * 125) >> 9
        centre = ((col * 256 + 127) * 125).astype(jnp.float32) * (1.0 / 131072.0)
        u = centre - first.astype(jnp.float32) - (sub >= 4).astype(jnp.float32)
        t = 1.0 - u
        k = 64.0 * 125.0 / 65536.0
        which = sub & 3
        def pick(a, b, c, d):
            return jnp.where(which == 0, a, jnp.where(which == 1, b, jnp.where(which == 2, c, d)))
        self.cubic = [
            pick(
                t * t * t / 6.0,
                2.0 / 3.0 - u * u + 0.5 * u * u * u,
                2.0 / 3.0 - t * t + 0.5 * t * t * t,
                u * u * u / 6.0,
            ),
            k * pick(-0.5 * t * t, -2.0 * u + 1.5 * u * u, 2.0 * t - 1.5 * t * t, 0.5 * u * u),
            (k * k) * pick(0.5 * t, 1.5 * u - 1.0, 1.5 * t - 1.0, 0.5 * u),
            (k * k * k) * pick(-1.0 / 6.0, 0.5, -0.5, 1.0 / 6.0),
        ]
        self.sub = sub
        eta = (iota((8, LANES), 1).astype(jnp.float32) - 63.5) * (1.0 / 64.0)
        power = iota((8, LANES), 0)
        q = jnp.ones((8, LANES), jnp.float32)
        for n in range(7):
            q = jnp.where(power > n, q * eta, q)
        self.powers = q

    def field(self, local):
        rows = [pltpu.roll(local, (LANES - s) % LANES, 1) if s else local for s in (0, 1, 2, 3)]
        rows += [pltpu.roll(local, LANES - s, 1) for s in (1, 2, 3, 4)]
        near = dot_rows(jnp.concatenate(rows, axis=0), self.hot)
        terms = jnp.concatenate([c * near for c in self.cubic], axis=0)
        wide = iota((32, 2 * LANES), 1)
        high = (iota((32, 2 * LANES), 0) & 4) != 0
        order = iota((32, 2 * LANES), 0) >> 3
        eta = ((wide & 127).astype(jnp.float32) - 63.5) * (1.0 / 64.0)
        power = jnp.where(
            order == 0, 1.0, jnp.where(order == 1, eta, jnp.where(order == 2, eta * eta, eta * eta * eta))
        )
        power = jnp.where(high == (wide >= LANES), power, 0.0)
        both = dot(terms.T, power)
        return jnp.where(self.low, both[:, :LANES], both[:, LANES:])

    def moments(self, value):
        low = jnp.where(self.low, value, 0.0)
        high = jnp.where(self.low, 0.0, value)
        a = dot_rows(self.powers, low)
        b = dot_rows(self.powers, high)
        return lambda n: jnp.where(self.sub < 4, a[n : n + 1], b[n : n + 1])

    def gather(self, rows):
        total = rows[0:1]
        for s in range(1, 4):
            total = total + pltpu.roll(rows[s : s + 1], s, 1)
        for s in range(4):
            total = total + pltpu.roll(rows[4 + s : 5 + s], s + 1, 1)
        return total

    def adjoint(self, value):
        part = self.moments(value)
        rows = sum(self.cubic[n] * part(n) for n in range(4))
        return self.gather(dot(rows, self.hot))

    def band(self, value):
        part = self.moments(value)
        parts = [part(n) for n in range(7)]
        y = [sum(self.cubic[j] * parts[i + j] for j in range(4)) for i in range(4)]
        stack = []
        for m in range(4):
            moved = [pltpu.roll(v, 8 - m, 0) if m else v for v in y]
            rows = sum(self.cubic[i] * moved[i] for i in range(4))
            stack.append(jnp.where((self.sub & 3) + m < 4, rows, 0.0))
        rows = dot(jnp.concatenate(stack, axis=0), self.hot)
        return [self.gather(rows[8 * m : 8 * m + 8]) for m in range(4)]


def place(pair, p):
    off_b, off_a = pair(p, 1), pair(p, 3)
    row_b = off_b >> 7
    lead = off_b & 127
    start = off_a - lead
    row_a = start >> 7
    turn = start & 127
    return row_b, lead, row_a, turn


def add_moved(accs, row_a, turn, i, value):
    lane = iota((8, LANES), 1)
    moved = pltpu.roll(value, turn, 1)
    keep = lane >= turn
    at = pl.ds(row_a + (LEAD + 8 * i), 8)
    accs[0][at, :] += jnp.where(keep, moved, 0.0)
    accs[1][at, :] += jnp.where(keep, 0.0, moved)


def live_count(pair):
    total = pair(0, 4)
    for p in range(1, CAP):
        total = total + pair(p, 4)
    return total


def pair_reader(ref, direction):
    return lambda p, field: ref[(direction * CAP + p) * 5 + field]


def slabs(pair, base, far, grad, image, field, cross, accs):
    lane = iota((8, LANES), 1)
    sub = iota((8, LANES), 0)

    def body(p, carry):
        row_b, lead, row_a, turn = place(pair, p)
        back = (LANES - turn) & 127
        keep = lane >= turn
        for i in range(GROUPS):
            c = jnp.zeros((8, LANES), jnp.float32)
            x = jnp.zeros((8, LANES), jnp.float32)
            for z in range(DEPTH):
                at_a = (row_a + (LEAD + 8 * i)) * 8 + z
                at_b = (row_b + (LEAD + 8 * i)) * 8 + z
                first = far[pl.ds(at_a, 8, stride=8), :]
                second = far[pl.ds(at_a + 8, 8, stride=8), :]
                slope = pltpu.roll(jnp.where(keep, first, second), back, 1)
                c = c + slope * grad[pl.ds(at_b, 8, stride=8), :]
                x = x + slope * image[pl.ds(at_b, 8, stride=8), :]
            if i in (0, GROUPS - 1):
                s = (sub + 8 * i) * LANES + lane - lead
                valid = (s >= 0) & (s < SLAB)
                c = jnp.where(valid, c, 0.0)
                x = jnp.where(valid, x, 0.0)
            cross[base + p, 8 * i : 8 * i + 8, :] = c
            value = x + c * field[pl.ds(row_b + (LEAD + 8 * i), 8), :]
            add_moved(accs, row_a, turn, i, value)
        return carry

    lax.fori_loop(0, live_count(pair), body, 0)


def slab_steps(pair, base, field, cross, accs):
    def body(p, carry):
        row_b, lead, row_a, turn = place(pair, p)
        for i in range(GROUPS):
            c = cross[base + p, 8 * i : 8 * i + 8, :]
            value = c * field[pl.ds(row_b + (LEAD + 8 * i), 8), :]
            add_moved(accs, row_a, turn, i, value)
        return carry

    lax.fori_loop(0, live_count(pair), body, 0)


def collected(accs):
    return accs[0][LEAD : LEAD + ROWS, :] + accs[1][LEAD - 1 : LEAD + ROWS - 1, :]


def clear(refs):
    for ref in refs:
        ref[...] = jnp.zeros(ref.shape, jnp.float32)


def clear_ends(ref, step):
    ref[0 : LEAD * step, :] = jnp.zeros((LEAD * step, LANES), jnp.float32)
    ref[(LEAD + ROWS) * step :, :] = jnp.zeros(((PADDED - LEAD - ROWS) * step, LANES), jnp.float32)


def local_values(place_ref, own, side_a, side_b):
    here = place_ref[0]
    lane = iota((1, LANES), 1)
    out = []
    for n in range(2):
        block = place_ref[1 + n]
        col, slot = block >> 2, block & 3
        table = jnp.where(
            col == here, own[0:2, :], jnp.where(col == (here ^ 1), side_a[0:2, :], side_b[0:2, :])
        )
        row = jnp.where((slot >> 1) == 0, table[0:1], table[1:2])
        row = jnp.where((slot & 1) == 0, row, pltpu.roll(row, BLOCK, 1))
        out.append(row)
    return jnp.where(lane < BLOCK, out[0], pltpu.roll(out[1], BLOCK, 1))


def padded_copy(source, target, sem):
    return pltpu.make_async_copy(source, target.at[pl.ds(LEAD * 8, ROWS * 8)], sem)


def directions(place_ref):
    odd = place_ref[0] & 1
    return jnp.where(odd == 0, 2, 0), jnp.where(odd == 0, 0, 2)


def early_kernel(
    place_ref, meta_own, meta_a, meta_b, own, side_a, side_b, grad_in, image_in, far_in,
    cross, weight_out, field_out, part_out,
    grad, image, far, acc0, acc1, acc2, acc3, count, sems,
):
    copies = [
        padded_copy(s, t, sems.at[n])
        for n, (s, t) in enumerate(((grad_in, grad), (image_in, image), (far_in, far)))
    ]
    for c in copies:
        c.start()
    for ref in (grad, image, far):
        clear_ends(ref, 8)
    clear((acc0, acc1, acc2, acc3, count))
    clear_ends(field_out, 1)
    spline = Spline()
    local = local_values(place_ref, own, side_a, side_b)
    rigid = shift_step * place_ref[3].astype(jnp.float32)
    field_out[LEAD : LEAD + ROWS, :] = spline.field(local) + rigid

    dir_a, dir_b = directions(place_ref)
    lane = iota((8, LANES), 1)
    sub = iota((8, LANES), 0)

    def cover(pair):
        def body(p, carry):
            off = pair(p, 3)
            row = off >> 7
            for i in range(GROUPS):
                s = (sub + 8 * i) * LANES + lane - (off & 127)
                inside = (s >= 0) & (s < SLAB)
                count[pl.ds(row + (LEAD + 8 * i), 8), :] += jnp.where(inside, 1.0, 0.0)
            return carry

        lax.fori_loop(0, live_count(pair), body, 0)

    own_pairs = pair_reader(meta_own, 1)
    cover(own_pairs)
    cover(pair_reader(meta_a, 2 - dir_a))
    cover(pair_reader(meta_b, 2 - dir_b))
    for c in copies:
        c.wait()
    slabs(own_pairs, 0, grad, grad, image, field_out, cross, (acc0, acc1))
    slabs(pair_reader(meta_own, dir_a), CAP, far, grad, image, field_out, cross, (acc2, acc3))

    def rows(g, carry):
        w = jnp.zeros((8, LANES), jnp.float32)
        v = jnp.zeros((8, LANES), jnp.float32)
        for z in range(DEPTH):
            at = pl.ds((LEAD + 8 * g) * 8 + z, 8, stride=8)
            slope = grad[at, :]
            w = w + slope * slope
            v = v + slope * image[at, :]
        at = pl.ds(pl.multiple_of(LEAD + 8 * g, 8), 8)
        n = count[at, :]
        w = w * n
        weight_out[pl.ds(pl.multiple_of(8 * g, 8), 8), :] = w
        count[at, :] = v * n + w * field_out[at, :]
        return carry

    lax.fori_loop(0, ROWS // 8, rows, 0)
    part_out[0:1, :] = spline.adjoint(count[LEAD : LEAD + ROWS, :] - collected((acc0, acc1)))
    part_out[1:2, :] = -spline.adjoint(collected((acc2, acc3)))
    part_out[2:3, :] = jnp.zeros((1, LANES), jnp.float32)
    half = iota((1, LANES), 1) < BLOCK
    first = jnp.where(place_ref[4] == 0, 1.0, 0.0)
    part_out[3:4, :] = first * jnp.where(half, place_ref[1], place_ref[2]).astype(jnp.float32)
    for m, row in enumerate(spline.band(weight_out[...])):
        part_out[4 + m : 5 + m, :] = row


def late_kernel(
    place_ref, meta_own, field, part, grad_in, image_in, far_in,
    cross, part_out, grad, image, far, acc0, acc1, sems,
):
    copies = [
        padded_copy(s, t, sems.at[n])
        for n, (s, t) in enumerate(((grad_in, grad), (image_in, image), (far_in, far)))
    ]
    for c in copies:
        c.start()
    for ref in (grad, image, far):
        clear_ends(ref, 8)
    clear((acc0, acc1))
    spline = Spline()
    _, dir_b = directions(place_ref)
    for c in copies:
        c.wait()
    slabs(pair_reader(meta_own, dir_b), 0, far, grad, image, field, cross, (acc0, acc1))
    part_out[...] = part[...]
    part_out[2:3, :] = -spline.adjoint(collected((acc0, acc1)))


def block_ids(place_ref):
    return [
        place_ref[1].astype(jnp.float32),
        place_ref[2].astype(jnp.float32),
        (place_ref[0] * 4 + place_ref[4]).astype(jnp.float32),
    ]


def near_tiles(me, a, b, c, d, sb, sd):
    return [
        (me, me[0:1, :] + a[1:2, :] + b[2:3, :]),
        (a, a[0:1, :] + me[1:2, :] + sb[2:3, :]),
        (b, b[0:1, :] + d[1:2, :] + me[2:3, :]),
        (d, d[0:1, :] + b[1:2, :] + c[2:3, :]),
        (sb, sb[0:1, :] + sd[1:2, :] + a[2:3, :]),
    ]


def folded(rows):
    return rows + pltpu.roll(rows, BLOCK, 1)


def block_sums(tiles, block):
    total = jnp.zeros((1, LANES), jnp.float32)
    for ref, grad in tiles:
        total = total + jnp.where(ref[3:4, :] == block, grad, 0.0)
    lane = iota((1, LANES), 1)
    return jnp.where(lane < BLOCK, folded(total), 0.0)


def pulled(coef):
    lane = iota((1, LANES), 1)
    y = coef - 2.0 * pltpu.roll(coef, LANES - 1, 1) + pltpu.roll(coef, LANES - 2, 1)
    y = jnp.where(lane < BLOCK - 2, y, 0.0)
    return jnp.where(lane < BLOCK, y - 2.0 * pltpu.roll(y, 1, 1) + pltpu.roll(y, 2, 1), 0.0)


def solve(target, factor, steps):
    y = []
    for i in range(BLOCK):
        v = target[i : i + 1, :]
        for j in range(1, 4):
            if i >= j:
                v = v - factor[j * BLOCK + i - j : j * BLOCK + i - j + 1, :] * y[i - j]
        y.append(v)
    x = [None] * BLOCK
    for i in reversed(range(BLOCK)):
        v = y[i] * factor[i : i + 1, :]
        for j in range(3, 0, -1):
            if i + j < BLOCK:
                v = v - factor[j * BLOCK + i : j * BLOCK + i + 1, :] * x[i + j]
        x[i] = v
        steps[i : i + 1, :] = v


def across(rows):
    block = jnp.concatenate(rows + [jnp.zeros((LANES - len(rows), LANES), jnp.float32)], axis=0)
    return block.T


def joined(coefs):
    lane = iota((1, LANES), 1)
    return jnp.where(lane < BLOCK, coefs[0], pltpu.roll(coefs[1], BLOCK, 1))


def step_kernel(
    place_ref, meta_own, me, a, b, c, d, sb, sd, own, side_a, side_b, start, weight,
    cross_early, cross_late,
    part_out, state, factor,
    field, steps, work, acc0, acc1, acc2, acc3, acc4, acc5,
):
    clear((acc0, acc1, acc2, acc3, acc4, acc5, steps))
    clear_ends(field, 1)
    lane = iota((1, LANES), 1)
    zero = jnp.zeros((1, LANES), jnp.float32)
    tiles = near_tiles(me, a, b, c, d, sb, sd)
    both = local_values(place_ref, own, side_a, side_b)
    coefs = [
        jnp.where(lane < BLOCK, both, 0.0),
        jnp.where(lane < BLOCK, pltpu.roll(both, BLOCK, 1), 0.0),
        start[0:1, :],
    ]
    sums = []
    rows = []
    for q, block in enumerate(block_ids(place_ref)):
        gradsum = block_sums(tiles, block)
        sums.append(gradsum)
        bands = []
        for m in range(4):
            total = zero
            for ref, _ in tiles:
                total = total + jnp.where(ref[3:4, :] == block, ref[4 + m : 5 + m, :], 0.0)
            total = jnp.where((lane & (BLOCK - 1)) + m < BLOCK, total, 0.0)
            bands.append(folded(total))
        inside = lambda cond: jnp.where(cond, 1.0, 0.0)
        upper, lower = inside(lane < BLOCK - 2), inside(lane >= 2)
        middle = inside((lane >= 1) & (lane < BLOCK - 1))
        bands[0] = bands[0] + smooth_weight * (upper + 4.0 * middle + lower) + ridge_weight
        bands[1] = bands[1] - smooth_weight * 2.0 * (
            upper + inside((lane >= 1) & (lane < BLOCK - 1))
        )
        bands[2] = bands[2] + smooth_weight * upper
        target = -(gradsum + smooth_weight * pulled(coefs[q]))
        rows += bands + [target, zero, zero, zero]
    work[...] = across(rows)
    turned = [work[0:BLOCK, :]] + [pltpu.roll(work[0:BLOCK, :], LANES - m, 1) for m in range(1, 5)]
    band = [[turned[m][i : i + 1, :] for i in range(BLOCK)] for m in range(4)]
    for i in range(BLOCK):
        r = 1.0 / band[0][i]
        factor[i : i + 1, :] = r
        cs = [band[m][i] for m in range(1, 4)]
        ls = [v * r for v in cs]
        for j in range(1, 4):
            factor[j * BLOCK + i : j * BLOCK + i + 1, :] = ls[j - 1]
            if i + j < BLOCK:
                for m in range(0, 4 - j):
                    band[m][i + j] = band[m][i + j] - ls[j - 1] * cs[j - 1 + m]
    solve(turned[4], factor, steps)
    moved = steps[...].T
    change = [moved[8 * q : 8 * q + 1, :] for q in range(3)]
    state[...] = jnp.concatenate(
        [coefs[q] + change[q] for q in range(3)] + [zero] + sums + [zero], axis=0
    )
    spline = Spline()
    field[LEAD : LEAD + ROWS, :] = spline.field(joined(change))
    dir_a, dir_b = directions(place_ref)
    slab_steps(pair_reader(meta_own, 1), 0, field, cross_early, (acc0, acc1))
    slab_steps(pair_reader(meta_own, dir_a), CAP, field, cross_early, (acc2, acc3))
    slab_steps(pair_reader(meta_own, dir_b), 0, field, cross_late, (acc4, acc5))
    part_out[0:1, :] = spline.adjoint(
        weight[...] * field[LEAD : LEAD + ROWS, :] - collected((acc0, acc1))
    )
    part_out[1:2, :] = -spline.adjoint(collected((acc2, acc3)))
    part_out[2:3, :] = -spline.adjoint(collected((acc4, acc5)))
    first = jnp.where(place_ref[4] == 0, 1.0, 0.0)
    half = iota((1, LANES), 1) < BLOCK
    part_out[3:4, :] = first * jnp.where(half, place_ref[1], place_ref[2]).astype(jnp.float32)
    part_out[4:8, :] = jnp.zeros((4, LANES), jnp.float32)


CHUNKS = 8


def final_kernel(
    place_ref, me, a, b, c, d, sb, sd, state, factor, grad_in, image_in,
    coef_out, warped_out,
    grad, image, field, steps, sems, out_sems,
):
    size = ROWS * 8 // CHUNKS
    at = [pl.ds(n * size, size) for n in range(CHUNKS)]
    loads = []
    for n in range(CHUNKS):
        loads.append(pltpu.make_async_copy(grad_in.at[at[n]], grad.at[at[n]], sems.at[0, n]))
        loads.append(pltpu.make_async_copy(image_in.at[at[n]], image.at[at[n]], sems.at[1, n]))
    for copy in loads:
        copy.start()
    steps[...] = jnp.zeros((LANES, LANES), jnp.float32)
    tiles = near_tiles(me, a, b, c, d, sb, sd)
    zero = jnp.zeros((1, LANES), jnp.float32)
    coefs = [state[q : q + 1, :] for q in range(3)]
    rows = []
    for q, block in enumerate(block_ids(place_ref)):
        gradsum = state[4 + q : 5 + q, :] + block_sums(tiles, block)
        rows += [-(gradsum + smooth_weight * pulled(coefs[q]))] + [zero] * 7
    solve(across(rows)[0:BLOCK, :], factor, steps)
    moved = steps[...].T
    coefs = [coefs[q] + moved[8 * q : 8 * q + 1, :] for q in range(3)]
    coef_out[...] = coefs[2][:, :BLOCK]
    spline = Spline()
    rigid = shift_step * place_ref[3].astype(jnp.float32)
    field[...] = spline.field(joined(coefs)) + rigid
    stores = []
    for n in range(CHUNKS):
        loads[2 * n].wait()
        loads[2 * n + 1].wait()

        def body(g, carry):
            for r in range(8):
                row = g * 8 + r
                rows = pl.ds(pl.multiple_of(row * 8, 8), 8)
                image[rows, :] = image[rows, :] + grad[rows, :] * field[pl.ds(row, 1), :]
            return carry

        lax.fori_loop(n * size // 64, (n + 1) * size // 64, body, 0)
        stores.append(pltpu.make_async_copy(image.at[at[n]], warped_out.at[at[n]], out_sems.at[n]))
        stores[-1].start()
    for copy in stores:
        copy.wait()


SMEM = pl.BlockSpec(memory_space=pltpu.SMEM)
VMEM = pl.BlockSpec(memory_space=pltpu.VMEM)
ANY = pl.BlockSpec(memory_space=pl.ANY)


def f32(*shape):
    return jax.ShapeDtypeStruct(shape, jnp.float32)


def call(kernel, name, in_specs, out_specs, out_shape, scratch):
    return pl.pallas_call(
        kernel,
        name=name,
        in_specs=in_specs,
        out_specs=out_specs,
        out_shape=out_shape,
        scratch_shapes=scratch,
        compiler_params=pltpu.CompilerParams(vmem_limit_bytes=VMEM_LIMIT),
    )


def whole():
    return pltpu.VMEM((PADDED * 8, LANES), jnp.float32)


def acc():
    return pltpu.VMEM((PADDED, LANES), jnp.float32)


def square():
    return pltpu.VMEM((LANES, LANES), jnp.float32)


def viewed(block):
    return block.reshape(DEPTH, ROWS, LANES).transpose(1, 0, 2).reshape(ROWS * DEPTH, LANES)


def per_device(images, gradient, shifts, tile_blocks, intersections, start_coefficients):
    tiles = lax.axis_size("tile")
    here = lax.axis_index("tile").astype(jnp.int32)
    knot = lax.axis_index("knot").astype(jnp.int32)
    ids = range(tiles)
    swap_a = [(i, i ^ 1) for i in ids]
    swap_b = [(i, ((i - 1) ^ 1) + 1) for i in ids if 0 < i < tiles - 1]
    swap_c = [(i, i + 3 if i % 2 else i - 3) for i in ids]
    swap_c = [(i, j) for i, j in swap_c if 0 <= j < tiles]
    same_d = [(i, i + 2 if i % 2 == 0 else i - 2) for i in ids]
    same_d = [(i, j) for i, j in same_d if 0 <= j < tiles]

    def move(value, route):
        return lax.ppermute(value, "tile", route)

    meta = intersections.reshape(-1)
    far_b = move(gradient, swap_b)
    far_a = move(gradient, swap_a)
    meta_a = move(meta, swap_a)
    meta_b = move(meta, swap_b)
    start = jnp.pad(start_coefficients, ((0, 7), (0, LANES - BLOCK)))
    slot = jnp.arange(4, dtype=jnp.int32)[:, None] == knot
    own = jnp.where(slot, start_coefficients, 0.0).reshape(2, LANES)
    own = lax.psum(jnp.pad(own, ((0, 6), (0, 0))), "knot")
    side_a = move(own, swap_a)
    side_b = move(own, swap_b)
    where = jnp.stack([here, tile_blocks[0, 0], tile_blocks[0, 1], shifts[0], knot])

    grad = viewed(gradient)
    image = viewed(images)
    cross_early, weight, field, part = call(
        early_kernel, "early_pairs",
        [SMEM] * 4 + [VMEM] * 3 + [ANY] * 3,
        [VMEM] * 4,
        [f32(2 * CAP, SLAB_ROWS, LANES), f32(ROWS, LANES), f32(PADDED, LANES), f32(8, LANES)],
        [whole()] * 3 + [acc()] * 5 + [pltpu.SemaphoreType.DMA((3,))],
    )(where, meta, meta_a, meta_b, own, side_a, side_b, grad, image, viewed(far_a))
    cross_late, part = call(
        late_kernel, "late_pairs",
        [SMEM] * 2 + [VMEM] * 2 + [ANY] * 3,
        [VMEM] * 2,
        [f32(CAP, SLAB_ROWS, LANES), f32(8, LANES)],
        [whole()] * 3 + [acc()] * 2 + [pltpu.SemaphoreType.DMA((3,))],
    )(where, meta, field, part, grad, image, viewed(far_b))

    def exchange(value):
        me = lax.psum(value, "knot")
        a = move(me, swap_a)
        b = move(me, swap_b)
        d = move(me, same_d)
        c = move(me, swap_c)
        sb = move(b, swap_a)
        sd = move(d, swap_a)
        return me, a, b, c, d, sb, sd

    part, state, factor = call(
        step_kernel, "first_step",
        [SMEM] * 2 + [VMEM] * 14,
        [VMEM] * 3,
        [f32(8, LANES), f32(8, LANES), f32(4 * BLOCK, LANES)],
        [acc(), square(), square()] + [acc()] * 6,
    )(where, meta, *exchange(part), own, side_a, side_b, start, weight, cross_early, cross_late)
    coef, warped = call(
        final_kernel, "second_step",
        [SMEM] + [VMEM] * 9 + [ANY] * 2,
        [VMEM, ANY],
        [f32(1, BLOCK), f32(ROWS * DEPTH, LANES)],
        [pltpu.VMEM((ROWS * DEPTH, LANES), jnp.float32)] * 2
        + [pltpu.VMEM((ROWS, LANES), jnp.float32), square()]
        + [pltpu.SemaphoreType.DMA((2, CHUNKS)), pltpu.SemaphoreType.DMA((CHUNKS,))],
    )(where, *exchange(part), state, factor, grad, image)
    warped = warped.reshape(ROWS, DEPTH, LANES).transpose(1, 0, 2).reshape(1, DEPTH, ROWS * LANES)
    return coef, warped


def solution(mesh):
    placed = (
        P("tile", "knot", None),
        P("tile", "knot", None),
        P("tile"),
        P("tile", None),
        P("tile", None, None, None),
        P(("tile", "knot"), None),
    )
    return jax.shard_map(
        per_device,
        mesh=mesh,
        in_specs=placed,
        out_specs=(P(("tile", "knot"), None), P("tile", "knot", None)),
        check_vma=False,
    )
```

time: 1200 us -> 113 us (0.09); the launches traced: 1190 us -> 113 us
  local copies, waits for them, and re-layouts: 532 us -> 10.6 us
  matrix products: 453 us -> 0 us
  other arithmetic: 72.7 us -> 0.02 us
  Pallas kernels: 0 us -> 26.1 us
  starting transfers between devices: 56.8 us -> 33.1 us
  between operations: 15.7 us -> 1.49 us
  blocking collectives: 44.7 us -> 31.2 us
    gather x432 -> x0, local copies, waits for them, and re-layouts: 497 us -> none
    dot_general x15 -> x0, matrix products: 451 us -> none  [the longest x2 244 us: per_device(): jnp.einsum('pnks,ps->pnk', piece, project, precision=lax.Precision.HIGHEST)]
    psum x0 -> x3, blocking collectives: none -> 31.2 us  [the longest x2 19.4 us: exchange(): me = lax.psum(value, 'knot')]
    all_gather x3 -> x0, blocking collectives: 28.8 us -> none  [fetch(): column = lax.all_gather(owned, 'knot', axis=0, tiled=True)]
    pallas_call x0 -> x4, Pallas kernels: none -> 26.1 us  [the longest x1 9.6 us: per_device(): call(early_kernel, 'early_pairs', [SMEM] * 4 + [VMEM] * 3 + [ANY] * 3, [V...]
    ppermute x18, starting transfers between devices: 56.7 us -> 33.1 us  [move(): return lax.ppermute(value, 'tile', route)]
    another operation x8 -> x0, other arithmetic: 22.8 us -> none  [the longest x2 10.7 us: per_device(): arrived = jnp.stack([below[0], slabs[1], above[0]])]
    reduce_sum x2 -> x0, other arithmetic: 22.4 us -> none  [per_device(): project = jnp.sum(slope * misfit, axis=1)]
  transfers between devices with their start and end apart: 19 -> 18, of which waited for: 3 -> 4; matrix products, arithmetic and copies ran while one was open for 44% -> 4% of each run, Pallas kernels for 0% -> 9%
where the time goes in v1:
time: 113 us
  starting transfers between devices  33.1 us (29%)
  blocking collectives  31.2 us (28%)
  Pallas kernels  26.1 us (23%)
  local copies, waits for them, and re-layouts  10.6 us (9%)
  waiting for transfers between devices  10.3 us (9%)
  between operations  1.49 us (1%)
    ppermute x18, starting transfers between devices, move(): return lax.ppermute(value, 'tile', route)  33.1 us
    psum x2, blocking collectives, exchange(): me = lax.psum(value, 'knot')  19.4 us
    psum x1, blocking collectives, per_device(): own = lax.psum(jnp.pad(own, ((0, 6), (0, 0))), 'knot')  11.8 us
    ppermute x18, waiting for transfers between devices, move(): return lax.ppermute(value, 'tile', route)  10.3 us
    pallas_call x1, Pallas kernels, per_device(): call(early_kernel, 'early_pairs', [SMEM] * 4 + [VMEM] * 3 + [ANY] * 3, [V...  9.6 us
    pallas_call x1, Pallas kernels, per_device(): call(step_kernel, 'first_step', [SMEM] * 2 + [VMEM] * 14, [VMEM] * 3, [f3...  7.26 us
    unnamed x15, local copies, waits for them, and re-layouts  6.88 us
    pallas_call x1, Pallas kernels, per_device(): call(final_kernel, 'second_step', [SMEM] + [VMEM] * 9 + [ANY] * 2, [VMEM,...  4.92 us
  transfers between devices with their start and end apart: 18, of which 4 were waited for; matrix products, arithmetic and copies ran while one was open for 4% of the time, Pallas kernels for 9%

profile of v1, /device:TPU:24, one launch (start us, length us, event | category | flops | bytes accessed | tf_op | source)
XLA Modules:
  0.0 112.7 jit_solution(6727620434014153323)
XLA Ops:
  0.7 4.9 %collective-permute-start.5 = (f32[1,8,65536]{2,1,0:T(8,128)}, f32[1,8,65536]{2,1,0:T(8,128)}, u32[]{:S(2)}, u32[]{:S(2)}) collective-permute-start(f32[1,8,65536]{2,1,0:T(8,128)} %param.7), channel_id=1, source_target_pairs={{4,8},{8,4},{12,16},{16,12},{20,24},{24,20},{28,32},{32,28},{36,40... | collective-permute-start | bytes 6291464 | tf_op jit(solution)/shard_map/ppermute | solution.py:575
  5.8 0.7 broadcast_in_dim.32
  6.6 11.8 %psum.21.own = f32[8,128]{1,0:T(8,128)S(1)} all-reduce(f32[8,128]{1,0:T(8,128)S(1)} %pad.8), channel_id=1, replica_groups=mesh['tile'=32,'knot'=4] {'knot'}, use_global_device_ids=true, to_apply=%region_0.1 | all-reduce | flops 1024 | bytes 8192 | tf_op jit(solution)/shard_map/psum | solution.py:585
  18.5 2.8 %collective-permute-start.3 = (f32[8,128]{1,0:T(8,128)S(1)}, f32[8,128]{1,0:T(8,128)S(1)}, u32[]{:S(2)}, u32[]{:S(2)}) collective-permute-start(f32[8,128]{1,0:T(8,128)S(1)} %psum.21.own), channel_id=1, source_target_pairs={{4,8},{8,4},{12,16},{16,12},{20,24},{24,20},{28,32},{32,28},{36,40... | collective-permute-start | bytes 12296 | tf_op jit(solution)/shard_map/ppermute | solution.py:575
  21.3 0.8 copy.9
  22.3 1.3 %fusion = (s32[1,1]{1,0:T(1,128)}, s32[1,1]{1,0:T(1,128)}) fusion(s32[1,2]{1,0:T(1,128)} %param.9), kind=kLoop, calls=%fused_computation.2 | loop fusion | bytes 16 | tf_op jit(solution)/shard_map/slice | solution.py:588
  23.6 4.8 %collective-permute-start.1 = (s32[120]{0:T(128)S(1)}, s32[120]{0:T(128)S(1)}, u32[]{:S(2)}, u32[]{:S(2)}) collective-permute-start(s32[120]{0:T(128)S(1)} %reshape.47.meta_own), channel_id=1, source_target_pairs={{4,8},{8,4},{12,16},{16,12},{20,24},{24,20},{28,32},{32,28},{36,40... | collective-permute-start | bytes 1448 | tf_op jit(solution)/shard_map/ppermute | solution.py:575
  29.1 1.4 %stack.11.place_ref = s32[5]{0:T(128)S(1)} concatenate(s32[1]{0:T(128)} %bitcast, s32[1]{0:T(128)} %bitcast.1, s32[1]{0:T(128)} %bitcast.2, s32[1]{0:T(128)S(6)} %copy.10, s32[1]{0:T(128)} %bitcast.3), dimensions={0} | concatenate | bytes 40 | tf_op jit(solution)/shard_map/stack | solution.py:588
  30.4 0.2 collective-permute-done.1.meta_b
  30.6 1.3 %copy-done.5 = f32[1,8,65536]{2,1,0:T(8,128)} copy-done((f32[1,8,65536]{2,1,0:T(8,128)}, f32[1,8,65536]{2,1,0:T(8,128)S(1)}, u32[]{:S(2)}) %copy-start.5) | copy-done | bytes 2097176
  32.0 1.6 %copy-done = f32[1,8,65536]{2,1,0:T(8,128)S(1)} copy-done((f32[1,8,65536]{2,1,0:T(8,128)S(1)}, f32[1,8,65536]{2,1,0:T(8,128)}, u32[]{:S(2)}) %copy-start) | copy-done | bytes 2097176
  33.6 1.6 %copy-done.2 = f32[1,8,65536]{2,1,0:T(8,128)S(1)} copy-done((f32[1,8,65536]{2,1,0:T(8,128)S(1)}, f32[1,8,65536]{2,1,0:T(8,128)}, u32[]{:S(2)}) %copy-start.2) | copy-done | bytes 2097176
  35.1 9.6 %early_pairs.1 = (f32[16,72,128]{2,1,0:T(8,128)S(1)}, f32[512,128]{1,0:T(8,128)S(1)}, f32[536,128]{1,0:T(8,128)S(1)}, f32[8,128]{1,0:T(8,128)S(1)}) custom-call(s32[5]{0:T(128)S(1)} %stack.11.place_ref, s32[120]{0:T(128)S(1)} %reshape.47.meta_own, s32[120]{0:T(128)S(1)} %collective-permute-done.meta_a, s32[120]{0:T(128)S(1)} %collective-permute-done.1.meta_b, ...), custom_call_target="tpu_custom_call" | custom-call | tf_op jit(solution)/shard_map/early_pairs/pallas_call | solution.py:592
  44.8 4.3 %late_pairs.1 = (f32[8,72,128]{2,1,0:T(8,128)S(1)}, f32[8,128]{1,0:T(8,128)S(1)}) custom-call(s32[5]{0:T(128)S(1)} %stack.11.place_ref, s32[120]{0:T(128)S(1)} %reshape.47.meta_own, f32[536,128]{1,0:T(8,128)S(1)} %get-tuple-element.13.field, f32[8,128]{1,0:T(8,128)S(1)} %get-tuple-element.14.part, f32[4096,128]{1,0:T(8,128)S(1)} %bitcast.33, ...), custom_call_target="tpu_custom_call" | custom-call | tf_op jit(solution)/shard_map/late_pairs/pallas_call | solution.py:599
  49.2 11.7 %psum.22.me = f32[8,128]{1,0:T(8,128)S(1)} all-reduce(f32[8,128]{1,0:T(8,128)S(1)} %get-tuple-element.15), channel_id=1, replica_groups=mesh['tile'=32,'knot'=4] {'knot'}, use_global_device_ids=true, to_apply=%region_1.2 | all-reduce | flops 1024 | bytes 8192 | tf_op jit(solution)/shard_map/psum | solution.py:608
  60.8 3.0 %collective-permute-start.7 = (f32[8,128]{1,0:T(8,128)S(1)}, f32[8,128]{1,0:T(8,128)S(1)}, u32[]{:S(2)}, u32[]{:S(2)}) collective-permute-start(f32[8,128]{1,0:T(8,128)S(1)} %psum.22.me), channel_id=1, source_target_pairs={{4,8},{8,4},{12,16},{16,12},{20,24},{24,20},{28,32},{32,28},{36,40... | collective-permute-start | bytes 12296 | tf_op jit(solution)/shard_map/ppermute | solution.py:575
  63.8 1.9 %collective-permute-start.9 = (f32[8,128]{1,0:T(8,128)S(1)}, f32[8,128]{1,0:T(8,128)S(1)}, u32[]{:S(2)}, u32[]{:S(2)}) collective-permute-start(f32[8,128]{1,0:T(8,128)S(1)} %psum.22.me), channel_id=1, source_target_pairs={{0,8},{8,16},{12,4},{16,24},{20,12},{24,32},{28,20},{32,40},{36,28... | collective-permute-start | bytes 12296 | tf_op jit(solution)/shard_map/ppermute | solution.py:575
  65.7 3.0 %collective-permute-start.6 = (f32[8,128]{1,0:T(8,128)S(1)}, f32[8,128]{1,0:T(8,128)S(1)}, u32[]{:S(2)}, u32[]{:S(2)}) collective-permute-start(f32[8,128]{1,0:T(8,128)S(1)} %psum.22.me), channel_id=1, source_target_pairs={{0,4},{4,0},{8,12},{12,8},{16,20},{20,16},{24,28},{28,24},{32,36},... | collective-permute-start | bytes 12296 | tf_op jit(solution)/shard_map/ppermute | solution.py:575
  68.7 1.9 %collective-permute-start.8 = (f32[8,128]{1,0:T(8,128)S(1)}, f32[8,128]{1,0:T(8,128)S(1)}, u32[]{:S(2)}, u32[]{:S(2)}) collective-permute-start(f32[8,128]{1,0:T(8,128)S(1)} %psum.22.me), channel_id=1, source_target_pairs={{4,16},{12,24},{16,4},{20,32},{24,12},{28,40},{32,20},{36,48},{40,... | collective-permute-start | bytes 12296 | tf_op jit(solution)/shard_map/ppermute | solution.py:575
  70.7 0.7 collective-permute-done.9.d
  71.4 4.6 %collective-permute-done.8.c = f32[8,128]{1,0:T(8,128)S(1)} collective-permute-done((f32[8,128]{1,0:T(8,128)S(1)}, f32[8,128]{1,0:T(8,128)S(1)}, u32[]{:S(2)}, u32[]{:S(2)}) %collective-permute-start.8) | collective-permute-done | bytes 4128 | tf_op jit(solution)/shard_map/ppermute | solution.py:575
  76.0 7.3 %first_step.1 = (f32[8,128]{1,0:T(8,128)S(1)}, f32[8,128]{1,0:T(8,128)S(1)}, f32[256,128]{1,0:T(8,128)S(1)}) custom-call(s32[5]{0:T(128)S(1)} %stack.11.place_ref, s32[120]{0:T(128)S(1)} %reshape.47.meta_own, f32[8,128]{1,0:T(8,128)S(1)} %psum.22.me, f32[8,128]{1,0:T(8,128)S(1)} %collective-permute-done.6.a, f32[8,128]{1,0:T(8,128)S(1)} %collective-permute-done.7.b, ...), custom_call_target="tpu_custom_call" | custom-call | tf_op jit(solution)/shard_map/first_step/pallas_call | solution.py:617
  83.3 7.8 %psum.23.me = f32[8,128]{1,0:T(8,128)S(1)} all-reduce(f32[8,128]{1,0:T(8,128)S(1)} %get-tuple-element.19), channel_id=1, replica_groups=mesh['tile'=32,'knot'=4] {'knot'}, use_global_device_ids=true, to_apply=%region_2.3 | all-reduce | flops 1024 | bytes 8192 | tf_op jit(solution)/shard_map/psum | solution.py:608
  91.0 1.9 %collective-permute-start.13 = (f32[8,128]{1,0:T(8,128)S(1)}, f32[8,128]{1,0:T(8,128)S(1)}, u32[]{:S(2)}, u32[]{:S(2)}) collective-permute-start(f32[8,128]{1,0:T(8,128)S(1)} %psum.23.me), channel_id=1, source_target_pairs={{4,8},{8,4},{12,16},{16,12},{20,24},{24,20},{28,32},{32,28},{36,40... | collective-permute-start | bytes 12296 | tf_op jit(solution)/shard_map/ppermute | solution.py:575
  92.9 1.9 %collective-permute-start.15 = (f32[8,128]{1,0:T(8,128)S(1)}, f32[8,128]{1,0:T(8,128)S(1)}, u32[]{:S(2)}, u32[]{:S(2)}) collective-permute-start(f32[8,128]{1,0:T(8,128)S(1)} %psum.23.me), channel_id=1, source_target_pairs={{0,8},{8,16},{12,4},{16,24},{20,12},{24,32},{28,20},{32,40},{36,28... | collective-permute-start | bytes 12296 | tf_op jit(solution)/shard_map/ppermute | solution.py:575
  94.9 4.0 %collective-permute-start.12 = (f32[8,128]{1,0:T(8,128)S(1)}, f32[8,128]{1,0:T(8,128)S(1)}, u32[]{:S(2)}, u32[]{:S(2)}) collective-permute-start(f32[8,128]{1,0:T(8,128)S(1)} %psum.23.me), channel_id=1, source_target_pairs={{0,4},{4,0},{8,12},{12,8},{16,20},{20,16},{24,28},{28,24},{32,36},... | collective-permute-start | bytes 12296 | tf_op jit(solution)/shard_map/ppermute | solution.py:575
  98.9 1.9 %collective-permute-start.14 = (f32[8,128]{1,0:T(8,128)S(1)}, f32[8,128]{1,0:T(8,128)S(1)}, u32[]{:S(2)}, u32[]{:S(2)}) collective-permute-start(f32[8,128]{1,0:T(8,128)S(1)} %psum.23.me), channel_id=1, source_target_pairs={{4,16},{12,24},{16,4},{20,32},{24,12},{28,40},{32,20},{36,48},{40,... | collective-permute-start | bytes 12296 | tf_op jit(solution)/shard_map/ppermute | solution.py:575
  100.8 0.1 collective-permute-start.16
  100.9 0.5 collective-permute-start.17
  101.4 4.8 %collective-permute-done.14.c = f32[8,128]{1,0:T(8,128)S(1)} collective-permute-done((f32[8,128]{1,0:T(8,128)S(1)}, f32[8,128]{1,0:T(8,128)S(1)}, u32[]{:S(2)}, u32[]{:S(2)}) %collective-permute-start.14) | collective-permute-done | bytes 4128 | tf_op jit(solution)/shard_map/ppermute | solution.py:575
  106.2 1.6 %copy-done.4 = f32[1,8,65536]{2,1,0:T(8,128)S(1)} copy-done((f32[1,8,65536]{2,1,0:T(8,128)S(1)}, f32[1,8,65536]{2,1,0:T(8,128)}, u32[]{:S(2)}) %copy-start.4) | copy-done | bytes 2097176
  107.8 4.9 %second_step.1 = (f32[1,64]{1,0:T(1,128)}, f32[4096,128]{1,0:T(8,128)}) custom-call(s32[5]{0:T(128)S(1)} %stack.11.place_ref, f32[8,128]{1,0:T(8,128)S(1)} %psum.23.me, f32[8,128]{1,0:T(8,128)S(1)} %collective-permute-done.12.a, f32[8,128]{1,0:T(8,128)S(1)} %collective-permute-done.13.b, f32[8,128]{1,0:T(8,128)S(1)} %collective-permute-done.14.c, ...), custom_call_target="tpu_custom_call" | custom-call | tf_op jit(solution)/shard_map/second_step/pallas_call | solution.py:624
  (37 shorter events, 0.8 us)
Async XLA Ops:
  0.6 30.0 %collective-permute-start.4 = (f32[1,8,65536]{2,1,0:T(8,128)}, f32[1,8,65536]{2,1,0:T(8,128)S(1)}, u32[]{:S(2)}, u32[]{:S(2)}) collective-permute-start(f32[1,8,65536]{2,1,0:T(8,128)} %param.7), channel_id=1, source_target_pairs={{0,4},{4,0},{8,12},{12,8},{16,20},{20,16},{24,28},{28,24},{32,36},... | collective-permute-start | bytes 6291464 | tf_op jit(solution)/shard_map/ppermute | solution.py:575
  0.7 44.0 %collective-permute-start.5 = (f32[1,8,65536]{2,1,0:T(8,128)}, f32[1,8,65536]{2,1,0:T(8,128)}, u32[]{:S(2)}, u32[]{:S(2)}) collective-permute-start(f32[1,8,65536]{2,1,0:T(8,128)} %param.7), channel_id=1, source_target_pairs={{4,8},{8,4},{12,16},{16,12},{20,24},{24,20},{28,32},{32,28},{36,40... | collective-permute-start | bytes 6291464 | tf_op jit(solution)/shard_map/ppermute | solution.py:575
  18.4 12.3 %collective-permute-start.2 = (f32[8,128]{1,0:T(8,128)S(1)}, f32[8,128]{1,0:T(8,128)S(1)}, u32[]{:S(2)}, u32[]{:S(2)}) collective-permute-start(f32[8,128]{1,0:T(8,128)S(1)} %psum.21.own), channel_id=1, source_target_pairs={{0,4},{4,0},{8,12},{12,8},{16,20},{20,16},{24,28},{28,24},{32,36},... | collective-permute-start | bytes 12296 | tf_op jit(solution)/shard_map/ppermute | solution.py:575
  18.5 12.2 %collective-permute-start.3 = (f32[8,128]{1,0:T(8,128)S(1)}, f32[8,128]{1,0:T(8,128)S(1)}, u32[]{:S(2)}, u32[]{:S(2)}) collective-permute-start(f32[8,128]{1,0:T(8,128)S(1)} %psum.21.own), channel_id=1, source_target_pairs={{4,8},{8,4},{12,16},{16,12},{20,24},{24,20},{28,32},{32,28},{36,40... | collective-permute-start | bytes 12296 | tf_op jit(solution)/shard_map/ppermute | solution.py:575
  22.2 1.4 %collective-permute-start = (s32[120]{0:T(128)S(1)}, s32[120]{0:T(128)S(1)}, u32[]{:S(2)}, u32[]{:S(2)}) collective-permute-start(s32[120]{0:T(128)S(1)} %reshape.47.meta_own), channel_id=1, source_target_pairs={{0,4},{4,0},{8,12},{12,8},{16,20},{20,16},{24,28},{28,24},{32,36},... | collective-permute-start | bytes 1448 | tf_op jit(solution)/shard_map/ppermute | solution.py:575
  23.6 7.0 %collective-permute-start.1 = (s32[120]{0:T(128)S(1)}, s32[120]{0:T(128)S(1)}, u32[]{:S(2)}, u32[]{:S(2)}) collective-permute-start(s32[120]{0:T(128)S(1)} %reshape.47.meta_own), channel_id=1, source_target_pairs={{4,8},{8,4},{12,16},{16,12},{20,24},{24,20},{28,32},{32,28},{36,40... | collective-permute-start | bytes 1448 | tf_op jit(solution)/shard_map/ppermute | solution.py:575
  30.6 1.3 %copy-start.5 = (f32[1,8,65536]{2,1,0:T(8,128)}, f32[1,8,65536]{2,1,0:T(8,128)S(1)}, u32[]{:S(2)}) copy-start(f32[1,8,65536]{2,1,0:T(8,128)S(1)} %collective-permute-done.4) | copy-start | bytes 6291460
  32.0 1.6 %copy-start = (f32[1,8,65536]{2,1,0:T(8,128)S(1)}, f32[1,8,65536]{2,1,0:T(8,128)}, u32[]{:S(2)}) copy-start(f32[1,8,65536]{2,1,0:T(8,128)} %param.7) | copy-start | bytes 6291460
  33.6 1.6 %copy-start.2 = (f32[1,8,65536]{2,1,0:T(8,128)S(1)}, f32[1,8,65536]{2,1,0:T(8,128)}, u32[]{:S(2)}) copy-start(f32[1,8,65536]{2,1,0:T(8,128)} %param.6) | copy-start | bytes 6291460
  35.1 9.6 %copy-start.1 = (f32[1,8,65536]{2,1,0:T(8,128)S(1)}, f32[1,8,65536]{2,1,0:T(8,128)}, u32[]{:S(2)}) copy-start(f32[1,8,65536]{2,1,0:T(8,128)} %param.7) | copy-start | bytes 6291460
  35.1 9.6 %copy-start.3 = (f32[1,8,65536]{2,1,0:T(8,128)S(1)}, f32[1,8,65536]{2,1,0:T(8,128)}, u32[]{:S(2)}) copy-start(f32[1,8,65536]{2,1,0:T(8,128)} %param.6) | copy-start | bytes 6291460
  44.8 26.6 %copy-start.6 = (f32[1,64]{1,0:T(1,128)S(1)}, f32[1,64]{1,0:T(1,128)}, u32[]{:S(2)}) copy-start(f32[1,64]{1,0:T(1,128)} %param.11) | copy-start | bytes 772
  60.8 9.8 %collective-permute-start.7 = (f32[8,128]{1,0:T(8,128)S(1)}, f32[8,128]{1,0:T(8,128)S(1)}, u32[]{:S(2)}, u32[]{:S(2)}) collective-permute-start(f32[8,128]{1,0:T(8,128)S(1)} %psum.22.me), channel_id=1, source_target_pairs={{4,8},{8,4},{12,16},{16,12},{20,24},{24,20},{28,32},{32,28},{36,40... | collective-permute-start | bytes 12296 | tf_op jit(solution)/shard_map/ppermute | solution.py:575
  63.8 7.6 %collective-permute-start.9 = (f32[8,128]{1,0:T(8,128)S(1)}, f32[8,128]{1,0:T(8,128)S(1)}, u32[]{:S(2)}, u32[]{:S(2)}) collective-permute-start(f32[8,128]{1,0:T(8,128)S(1)} %psum.22.me), channel_id=1, source_target_pairs={{0,8},{8,16},{12,4},{16,24},{20,12},{24,32},{28,20},{32,40},{36,28... | collective-permute-start | bytes 12296 | tf_op jit(solution)/shard_map/ppermute | solution.py:575
  65.7 5.7 %collective-permute-start.6 = (f32[8,128]{1,0:T(8,128)S(1)}, f32[8,128]{1,0:T(8,128)S(1)}, u32[]{:S(2)}, u32[]{:S(2)}) collective-permute-start(f32[8,128]{1,0:T(8,128)S(1)} %psum.22.me), channel_id=1, source_target_pairs={{0,4},{4,0},{8,12},{12,8},{16,20},{20,16},{24,28},{28,24},{32,36},... | collective-permute-start | bytes 12296 | tf_op jit(solution)/shard_map/ppermute | solution.py:575
  68.7 7.3 %collective-permute-start.8 = (f32[8,128]{1,0:T(8,128)S(1)}, f32[8,128]{1,0:T(8,128)S(1)}, u32[]{:S(2)}, u32[]{:S(2)}) collective-permute-start(f32[8,128]{1,0:T(8,128)S(1)} %psum.22.me), channel_id=1, source_target_pairs={{4,16},{12,24},{16,4},{20,32},{24,12},{28,40},{32,20},{36,48},{40,... | collective-permute-start | bytes 12296 | tf_op jit(solution)/shard_map/ppermute | solution.py:575
  70.6 5.4 %collective-permute-start.10 = (f32[8,128]{1,0:T(8,128)S(1)}, f32[8,128]{1,0:T(8,128)S(1)}, u32[]{:S(2)}, u32[]{:S(2)}) collective-permute-start(f32[8,128]{1,0:T(8,128)S(1)} %collective-permute-done.7.b), channel_id=1, source_target_pairs={{0,4},{4,0},{8,12},{12,8},{16,20},{20,16},{24,28},{28,24},{32,36},... | collective-permute-start | bytes 12296 | tf_op jit(solution)/shard_map/ppermute | solution.py:575
  71.4 4.6 %collective-permute-start.11 = (f32[8,128]{1,0:T(8,128)S(1)}, f32[8,128]{1,0:T(8,128)S(1)}, u32[]{:S(2)}, u32[]{:S(2)}) collective-permute-start(f32[8,128]{1,0:T(8,128)S(1)} %collective-permute-done.9.d), channel_id=1, source_target_pairs={{0,4},{4,0},{8,12},{12,8},{16,20},{20,16},{24,28},{28,24},{32,36},... | collective-permute-start | bytes 12296 | tf_op jit(solution)/shard_map/ppermute | solution.py:575
  91.0 9.8 %collective-permute-start.13 = (f32[8,128]{1,0:T(8,128)S(1)}, f32[8,128]{1,0:T(8,128)S(1)}, u32[]{:S(2)}, u32[]{:S(2)}) collective-permute-start(f32[8,128]{1,0:T(8,128)S(1)} %psum.23.me), channel_id=1, source_target_pairs={{4,8},{8,4},{12,16},{16,12},{20,24},{24,20},{28,32},{32,28},{36,40... | collective-permute-start | bytes 12296 | tf_op jit(solution)/shard_map/ppermute | solution.py:575
  92.9 8.0 %collective-permute-start.15 = (f32[8,128]{1,0:T(8,128)S(1)}, f32[8,128]{1,0:T(8,128)S(1)}, u32[]{:S(2)}, u32[]{:S(2)}) collective-permute-start(f32[8,128]{1,0:T(8,128)S(1)} %psum.23.me), channel_id=1, source_target_pairs={{0,8},{8,16},{12,4},{16,24},{20,12},{24,32},{28,20},{32,40},{36,28... | collective-permute-start | bytes 12296 | tf_op jit(solution)/shard_map/ppermute | solution.py:575
  94.9 6.5 %collective-permute-start.12 = (f32[8,128]{1,0:T(8,128)S(1)}, f32[8,128]{1,0:T(8,128)S(1)}, u32[]{:S(2)}, u32[]{:S(2)}) collective-permute-start(f32[8,128]{1,0:T(8,128)S(1)} %psum.23.me), channel_id=1, source_target_pairs={{0,4},{4,0},{8,12},{12,8},{16,20},{20,16},{24,28},{28,24},{32,36},... | collective-permute-start | bytes 12296 | tf_op jit(solution)/shard_map/ppermute | solution.py:575
  98.9 7.3 %collective-permute-start.14 = (f32[8,128]{1,0:T(8,128)S(1)}, f32[8,128]{1,0:T(8,128)S(1)}, u32[]{:S(2)}, u32[]{:S(2)}) collective-permute-start(f32[8,128]{1,0:T(8,128)S(1)} %psum.23.me), channel_id=1, source_target_pairs={{4,16},{12,24},{16,4},{20,32},{24,12},{28,40},{32,20},{36,48},{40,... | collective-permute-start | bytes 12296 | tf_op jit(solution)/shard_map/ppermute | solution.py:575
  100.8 5.4 %collective-permute-start.16 = (f32[8,128]{1,0:T(8,128)S(1)}, f32[8,128]{1,0:T(8,128)S(1)}, u32[]{:S(2)}, u32[]{:S(2)}) collective-permute-start(f32[8,128]{1,0:T(8,128)S(1)} %collective-permute-done.13.b), channel_id=1, source_target_pairs={{0,4},{4,0},{8,12},{12,8},{16,20},{20,16},{24,28},{28,24},{32,36},... | collective-permute-start | bytes 12296 | tf_op jit(solution)/shard_map/ppermute | solution.py:575
  100.9 5.3 %collective-permute-start.17 = (f32[8,128]{1,0:T(8,128)S(1)}, f32[8,128]{1,0:T(8,128)S(1)}, u32[]{:S(2)}, u32[]{:S(2)}) collective-permute-start(f32[8,128]{1,0:T(8,128)S(1)} %collective-permute-done.15.d), channel_id=1, source_target_pairs={{0,4},{4,0},{8,12},{12,8},{16,20},{20,16},{24,28},{28,24},{32,36},... | collective-permute-start | bytes 12296 | tf_op jit(solution)/shard_map/ppermute | solution.py:575
  106.2 1.6 %copy-start.4 = (f32[1,8,65536]{2,1,0:T(8,128)S(1)}, f32[1,8,65536]{2,1,0:T(8,128)}, u32[]{:S(2)}) copy-start(f32[1,8,65536]{2,1,0:T(8,128)} %param.6) | copy-start | bytes 6291460

commit v2 on v1

--- a/solution.py
+++ b/solution.py
@@ -12,7 +12,7 @@
 LANES = 128
 ROWS = 512
 DEPTH = 8
-LEAD = 8
+LEAD = 16
 PADDED = LEAD + ROWS + 16
 GROUPS = SLAB // (8 * LANES) + 1
 SLAB_ROWS = 8 * GROUPS
@@ -23,7 +23,7 @@
 ridge_weight = 1.0
 
 EXACT = lax.Precision.HIGHEST
-VMEM_LIMIT = 48 * 1024 * 1024
+VMEM_LIMIT = 24 * 1024 * 1024
 
 
 def iota(shape, dim):
@@ -126,14 +126,37 @@
         return [self.gather(rows[8 * m : 8 * m + 8]) for m in range(4)]
 
 
+LAST_ROW = ROWS - SLAB_ROWS
+
+
+class Here:
+    def __init__(self, blocks=None, shifts=None):
+        self.tile = lax.axis_index("tile").astype(jnp.int32)
+        self.knot = lax.axis_index("knot").astype(jnp.int32)
+        odd = self.tile & 1
+        self.to_a = jnp.where(odd == 0, 2, 0)
+        self.to_b = 2 - self.to_a
+        if blocks is not None:
+            self.blocks = [blocks[0, 0], blocks[0, 1]]
+        if shifts is not None:
+            self.rigid = shift_step * shifts[0].astype(jnp.float32)
+
+    def block_row(self):
+        lane = iota((1, LANES), 1)
+        row = jnp.where(lane < BLOCK, self.blocks[0], self.blocks[1]).astype(jnp.float32)
+        return jnp.where(self.knot == 0, 1.0, 0.0) * row
+
+    def block_ids(self):
+        owned = self.tile * 4 + self.knot
+        return [b.astype(jnp.float32) for b in self.blocks + [owned]]
+
+
 def place(pair, p):
     off_b, off_a = pair(p, 1), pair(p, 3)
-    row_b = off_b >> 7
-    lead = off_b & 127
+    row_b = jnp.minimum(off_b >> 7, LAST_ROW)
+    lead = off_b - row_b * LANES
     start = off_a - lead
-    row_a = start >> 7
-    turn = start & 127
-    return row_b, lead, row_a, turn
+    return row_b, lead, start >> 7, start & 127
 
 
 def add_moved(accs, row_a, turn, i, value):
@@ -153,10 +176,10 @@
 
 
 def pair_reader(ref, direction):
-    return lambda p, field: ref[(direction * CAP + p) * 5 + field]
-
-
-def slabs(pair, base, far, grad, image, field, cross, accs):
+    return lambda p, field: ref[0, direction, p, field]
+
+
+def slabs(pair, base, far, grad, image, cross, accs, field=None):
     lane = iota((8, LANES), 1)
     sub = iota((8, LANES), 0)
 
@@ -169,20 +192,22 @@
             x = jnp.zeros((8, LANES), jnp.float32)
             for z in range(DEPTH):
                 at_a = (row_a + (LEAD + 8 * i)) * 8 + z
-                at_b = (row_b + (LEAD + 8 * i)) * 8 + z
+                at_b = (row_b + 8 * i) * 8 + z
+                at_g = at_b + LEAD * 8
                 first = far[pl.ds(at_a, 8, stride=8), :]
                 second = far[pl.ds(at_a + 8, 8, stride=8), :]
                 slope = pltpu.roll(jnp.where(keep, first, second), back, 1)
-                c = c + slope * grad[pl.ds(at_b, 8, stride=8), :]
+                c = c + slope * grad[pl.ds(at_g, 8, stride=8), :]
                 x = x + slope * image[pl.ds(at_b, 8, stride=8), :]
-            if i in (0, GROUPS - 1):
+            if i in (0, 1, GROUPS - 1):
                 s = (sub + 8 * i) * LANES + lane - lead
                 valid = (s >= 0) & (s < SLAB)
                 c = jnp.where(valid, c, 0.0)
                 x = jnp.where(valid, x, 0.0)
             cross[base + p, 8 * i : 8 * i + 8, :] = c
-            value = x + c * field[pl.ds(row_b + (LEAD + 8 * i), 8), :]
-            add_moved(accs, row_a, turn, i, value)
+            if field is not None:
+                x = x + c * field[pl.ds(row_b + 8 * i, 8), :]
+            add_moved(accs, row_a, turn, i, x)
         return carry
 
     lax.fori_loop(0, live_count(pair), body, 0)
@@ -193,7 +218,7 @@
         row_b, lead, row_a, turn = place(pair, p)
         for i in range(GROUPS):
             c = cross[base + p, 8 * i : 8 * i + 8, :]
-            value = c * field[pl.ds(row_b + (LEAD + 8 * i), 8), :]
+            value = c * field[pl.ds(row_b + 8 * i, 8), :]
             add_moved(accs, row_a, turn, i, value)
         return carry
 
@@ -209,144 +234,134 @@
         ref[...] = jnp.zeros(ref.shape, jnp.float32)
 
 
-def clear_ends(ref, step):
-    ref[0 : LEAD * step, :] = jnp.zeros((LEAD * step, LANES), jnp.float32)
-    ref[(LEAD + ROWS) * step :, :] = jnp.zeros(((PADDED - LEAD - ROWS) * step, LANES), jnp.float32)
-
-
-def local_values(place_ref, own, side_a, side_b):
-    here = place_ref[0]
-    lane = iota((1, LANES), 1)
+def clear_ends(ref):
+    ref[0 : LEAD * 8, :] = jnp.zeros((LEAD * 8, LANES), jnp.float32)
+    ref[(LEAD + ROWS) * 8 :, :] = jnp.zeros(((PADDED - LEAD - ROWS) * 8, LANES), jnp.float32)
+
+
+def local_values(here, own, side_a, side_b):
     out = []
-    for n in range(2):
-        block = place_ref[1 + n]
+    for block in here.blocks:
         col, slot = block >> 2, block & 3
+        back = (here.knot - slot) & 3
         table = jnp.where(
-            col == here, own[0:2, :], jnp.where(col == (here ^ 1), side_a[0:2, :], side_b[0:2, :])
+            col == here.tile,
+            own[...],
+            jnp.where(col == (here.tile ^ 1), side_a[...], side_b[...]),
         )
-        row = jnp.where((slot >> 1) == 0, table[0:1], table[1:2])
-        row = jnp.where((slot & 1) == 0, row, pltpu.roll(row, BLOCK, 1))
-        out.append(row)
-    return jnp.where(lane < BLOCK, out[0], pltpu.roll(out[1], BLOCK, 1))
+        out.append(
+            jnp.where(
+                back == 0,
+                table[0:1],
+                jnp.where(back == 1, table[1:2], jnp.where(back == 2, table[2:3], table[3:4])),
+            )
+        )
+    return jnp.concatenate(out, axis=1)
 
 
 def padded_copy(source, target, sem):
     return pltpu.make_async_copy(source, target.at[pl.ds(LEAD * 8, ROWS * 8)], sem)
 
 
-def directions(place_ref):
-    odd = place_ref[0] & 1
-    return jnp.where(odd == 0, 2, 0), jnp.where(odd == 0, 0, 2)
+def cover(pair, count):
+    lane = iota((8, LANES), 1)
+    sub = iota((8, LANES), 0)
+
+    def body(p, carry):
+        off = pair(p, 3)
+        for i in range(GROUPS):
+            s = (sub + 8 * i) * LANES + lane - (off & 127)
+            inside = (s >= 0) & (s < SLAB)
+            count[pl.ds((off >> 7) + (LEAD + 8 * i), 8), :] += jnp.where(inside, 1.0, 0.0)
+        return carry
+
+    lax.fori_loop(0, live_count(pair), body, 0)
 
 
 def early_kernel(
-    place_ref, meta_own, meta_a, meta_b, own, side_a, side_b, grad_in, image_in, far_in,
-    cross, weight_out, field_out, part_out,
-    grad, image, far, acc0, acc1, acc2, acc3, count, sems,
+    meta, meta_a, grad_in, image_in, far_in,
+    cross, weight_out, value_out, own_out, side_out, count, near, image,
+    far, acc0, acc1, acc2, acc3, sems,
 ):
     copies = [
-        padded_copy(s, t, sems.at[n])
-        for n, (s, t) in enumerate(((grad_in, grad), (image_in, image), (far_in, far)))
+        padded_copy(grad_in, near, sems.at[0]),
+        pltpu.make_async_copy(image_in, image, sems.at[1]),
+        padded_copy(far_in, far, sems.at[2]),
     ]
     for c in copies:
         c.start()
-    for ref in (grad, image, far):
-        clear_ends(ref, 8)
+    for ref in (near, far):
+        clear_ends(ref)
     clear((acc0, acc1, acc2, acc3, count))
-    clear_ends(field_out, 1)
-    spline = Spline()
-    local = local_values(place_ref, own, side_a, side_b)
-    rigid = shift_step * place_ref[3].astype(jnp.float32)
-    field_out[LEAD : LEAD + ROWS, :] = spline.field(local) + rigid
-
-    dir_a, dir_b = directions(place_ref)
-    lane = iota((8, LANES), 1)
-    sub = iota((8, LANES), 0)
-
-    def cover(pair):
-        def body(p, carry):
-            off = pair(p, 3)
-            row = off >> 7
-            for i in range(GROUPS):
-                s = (sub + 8 * i) * LANES + lane - (off & 127)
-                inside = (s >= 0) & (s < SLAB)
-                count[pl.ds(row + (LEAD + 8 * i), 8), :] += jnp.where(inside, 1.0, 0.0)
-            return carry
-
-        lax.fori_loop(0, live_count(pair), body, 0)
-
-    own_pairs = pair_reader(meta_own, 1)
-    cover(own_pairs)
-    cover(pair_reader(meta_a, 2 - dir_a))
-    cover(pair_reader(meta_b, 2 - dir_b))
-    for c in copies:
-        c.wait()
-    slabs(own_pairs, 0, grad, grad, image, field_out, cross, (acc0, acc1))
-    slabs(pair_reader(meta_own, dir_a), CAP, far, grad, image, field_out, cross, (acc2, acc3))
+    here = Here()
+    cover(pair_reader(meta, 1), count)
+    cover(pair_reader(meta_a, 2 - here.to_a), count)
 
     def rows(g, carry):
         w = jnp.zeros((8, LANES), jnp.float32)
         v = jnp.zeros((8, LANES), jnp.float32)
         for z in range(DEPTH):
-            at = pl.ds((LEAD + 8 * g) * 8 + z, 8, stride=8)
-            slope = grad[at, :]
+            slope = near[pl.ds(64 * g + (LEAD * 8 + z), 8, stride=8), :]
             w = w + slope * slope
-            v = v + slope * image[at, :]
-        at = pl.ds(pl.multiple_of(LEAD + 8 * g, 8), 8)
-        n = count[at, :]
-        w = w * n
-        weight_out[pl.ds(pl.multiple_of(8 * g, 8), 8), :] = w
-        count[at, :] = v * n + w * field_out[at, :]
+            v = v + slope * image[pl.ds(64 * g + z, 8, stride=8), :]
+        at = pl.ds(pl.multiple_of(8 * g, 8), 8)
+        weight_out[at, :] = w
+        value_out[at, :] = v
         return carry
 
+    copies[0].wait()
+    copies[1].wait()
     lax.fori_loop(0, ROWS // 8, rows, 0)
-    part_out[0:1, :] = spline.adjoint(count[LEAD : LEAD + ROWS, :] - collected((acc0, acc1)))
-    part_out[1:2, :] = -spline.adjoint(collected((acc2, acc3)))
-    part_out[2:3, :] = jnp.zeros((1, LANES), jnp.float32)
-    half = iota((1, LANES), 1) < BLOCK
-    first = jnp.where(place_ref[4] == 0, 1.0, 0.0)
-    part_out[3:4, :] = first * jnp.where(half, place_ref[1], place_ref[2]).astype(jnp.float32)
-    for m, row in enumerate(spline.band(weight_out[...])):
+    slabs(pair_reader(meta, 1), 0, near, near, image, cross, (acc0, acc1))
+    copies[2].wait()
+    slabs(pair_reader(meta, here.to_a), CAP, far, near, image, cross, (acc2, acc3))
+    own_out[...] = collected((acc0, acc1))
+    side_out[...] = collected((acc2, acc3))
+
+
+def late_kernel(
+    meta, meta_b, blocks, shifts, column, side_a, side_b,
+    near, image, cross_early, weight, value, own, side, counted, far_in,
+    cross, weight_out, part_out,
+    far, field, count, acc0, acc1, acc2, acc3, acc4, acc5, sems,
+):
+    copy = padded_copy(far_in, far, sems.at[0])
+    copy.start()
+    here = Here(blocks, shifts)
+    clear_ends(far)
+    clear((acc0, acc1, acc2, acc3, acc4, acc5))
+    count[...] = counted[...]
+    cover(pair_reader(meta_b, 2 - here.to_b), count)
+    spline = Spline()
+    field[...] = spline.field(local_values(here, column, side_a, side_b)) + here.rigid
+    slab_steps(pair_reader(meta, 1), 0, field, cross_early, (acc0, acc1))
+    slab_steps(pair_reader(meta, here.to_a), CAP, field, cross_early, (acc2, acc3))
+    copy.wait()
+    slabs(pair_reader(meta, here.to_b), 0, far, near, image, cross, (acc4, acc5), field)
+    n = count[LEAD : LEAD + ROWS, :]
+    w = weight[...] * n
+    weight_out[...] = w
+    part_out[0:1, :] = spline.adjoint(
+        value[...] * n + w * field[...] - own[...] - collected((acc0, acc1))
+    )
+    part_out[1:2, :] = -spline.adjoint(side[...] + collected((acc2, acc3)))
+    part_out[2:3, :] = -spline.adjoint(collected((acc4, acc5)))
+    part_out[3:4, :] = here.block_row()
+    for m, row in enumerate(spline.band(w)):
         part_out[4 + m : 5 + m, :] = row
 
 
-def late_kernel(
-    place_ref, meta_own, field, part, grad_in, image_in, far_in,
-    cross, part_out, grad, image, far, acc0, acc1, sems,
-):
-    copies = [
-        padded_copy(s, t, sems.at[n])
-        for n, (s, t) in enumerate(((grad_in, grad), (image_in, image), (far_in, far)))
-    ]
-    for c in copies:
-        c.start()
-    for ref in (grad, image, far):
-        clear_ends(ref, 8)
-    clear((acc0, acc1))
-    spline = Spline()
-    _, dir_b = directions(place_ref)
-    for c in copies:
-        c.wait()
-    slabs(pair_reader(meta_own, dir_b), 0, far, grad, image, field, cross, (acc0, acc1))
-    part_out[...] = part[...]
-    part_out[2:3, :] = -spline.adjoint(collected((acc0, acc1)))
-
-
-def block_ids(place_ref):
+def near_tiles(both, ahead, third, behind):
+    me, a = both[0:8, :], both[8:16, :]
+    d, b = ahead[0:8, :], ahead[8:16, :]
+    sd, sb = behind[0:8, :], behind[8:16, :]
+    c = third[...]
     return [
-        place_ref[1].astype(jnp.float32),
-        place_ref[2].astype(jnp.float32),
-        (place_ref[0] * 4 + place_ref[4]).astype(jnp.float32),
-    ]
-
-
-def near_tiles(me, a, b, c, d, sb, sd):
-    return [
-        (me, me[0:1, :] + a[1:2, :] + b[2:3, :]),
-        (a, a[0:1, :] + me[1:2, :] + sb[2:3, :]),
-        (b, b[0:1, :] + d[1:2, :] + me[2:3, :]),
-        (d, d[0:1, :] + b[1:2, :] + c[2:3, :]),
-        (sb, sb[0:1, :] + sd[1:2, :] + a[2:3, :]),
+        (me, me[0:1] + a[1:2] + b[2:3]),
+        (a, a[0:1] + me[1:2] + sb[2:3]),
+        (b, b[0:1] + d[1:2] + me[2:3]),
+        (d, d[0:1] + b[1:2] + c[2:3]),
+        (sb, sb[0:1] + sd[1:2] + a[2:3]),
     ]
 
 
@@ -357,7 +372,7 @@
 def block_sums(tiles, block):
     total = jnp.zeros((1, LANES), jnp.float32)
     for ref, grad in tiles:
-        total = total + jnp.where(ref[3:4, :] == block, grad, 0.0)
+        total = total + jnp.where(ref[3:4] == block, grad, 0.0)
     lane = iota((1, LANES), 1)
     return jnp.where(lane < BLOCK, folded(total), 0.0)
 
@@ -398,32 +413,32 @@
 
 
 def step_kernel(
-    place_ref, meta_own, me, a, b, c, d, sb, sd, own, side_a, side_b, start, weight,
+    meta, blocks, both, ahead, third, behind, column, side_a, side_b, start, weight,
     cross_early, cross_late,
     part_out, state, factor,
     field, steps, work, acc0, acc1, acc2, acc3, acc4, acc5,
 ):
+    here = Here(blocks)
     clear((acc0, acc1, acc2, acc3, acc4, acc5, steps))
-    clear_ends(field, 1)
     lane = iota((1, LANES), 1)
     zero = jnp.zeros((1, LANES), jnp.float32)
-    tiles = near_tiles(me, a, b, c, d, sb, sd)
-    both = local_values(place_ref, own, side_a, side_b)
+    tiles = near_tiles(both, ahead, third, behind)
+    knots = local_values(here, column, side_a, side_b)
     coefs = [
-        jnp.where(lane < BLOCK, both, 0.0),
-        jnp.where(lane < BLOCK, pltpu.roll(both, BLOCK, 1), 0.0),
-        start[0:1, :],
+        jnp.where(lane < BLOCK, knots, 0.0),
+        jnp.where(lane < BLOCK, pltpu.roll(knots, BLOCK, 1), 0.0),
+        jnp.concatenate([start[...], jnp.zeros((1, LANES - BLOCK), jnp.float32)], axis=1),
     ]
     sums = []
     rows = []
-    for q, block in enumerate(block_ids(place_ref)):
+    for q, block in enumerate(here.block_ids()):
         gradsum = block_sums(tiles, block)
         sums.append(gradsum)
         bands = []
         for m in range(4):
             total = zero
             for ref, _ in tiles:
-                total = total + jnp.where(ref[3:4, :] == block, ref[4 + m : 5 + m, :], 0.0)
+                total = total + jnp.where(ref[3:4] == block, ref[4 + m : 5 + m], 0.0)
             total = jnp.where((lane & (BLOCK - 1)) + m < BLOCK, total, 0.0)
             bands.append(folded(total))
         inside = lambda cond: jnp.where(cond, 1.0, 0.0)
@@ -456,19 +471,14 @@
         [coefs[q] + change[q] for q in range(3)] + [zero] + sums + [zero], axis=0
     )
     spline = Spline()
-    field[LEAD : LEAD + ROWS, :] = spline.field(joined(change))
-    dir_a, dir_b = directions(place_ref)
-    slab_steps(pair_reader(meta_own, 1), 0, field, cross_early, (acc0, acc1))
-    slab_steps(pair_reader(meta_own, dir_a), CAP, field, cross_early, (acc2, acc3))
-    slab_steps(pair_reader(meta_own, dir_b), 0, field, cross_late, (acc4, acc5))
-    part_out[0:1, :] = spline.adjoint(
-        weight[...] * field[LEAD : LEAD + ROWS, :] - collected((acc0, acc1))
-    )
+    field[...] = spline.field(joined(change))
+    slab_steps(pair_reader(meta, 1), 0, field, cross_early, (acc0, acc1))
+    slab_steps(pair_reader(meta, here.to_a), CAP, field, cross_early, (acc2, acc3))
+    slab_steps(pair_reader(meta, here.to_b), 0, field, cross_late, (acc4, acc5))
+    part_out[0:1, :] = spline.adjoint(weight[...] * field[...] - collected((acc0, acc1)))
     part_out[1:2, :] = -spline.adjoint(collected((acc2, acc3)))
     part_out[2:3, :] = -spline.adjoint(collected((acc4, acc5)))
-    first = jnp.where(place_ref[4] == 0, 1.0, 0.0)
-    half = iota((1, LANES), 1) < BLOCK
-    part_out[3:4, :] = first * jnp.where(half, place_ref[1], place_ref[2]).astype(jnp.float32)
+    part_out[3:4, :] = here.block_row()
     part_out[4:8, :] = jnp.zeros((4, LANES), jnp.float32)
 
 
@@ -476,7 +486,7 @@
 
 
 def final_kernel(
-    place_ref, me, a, b, c, d, sb, sd, state, factor, grad_in, image_in,
+    blocks, shifts, both, ahead, third, behind, state, factor, grad_in, image_in,
     coef_out, warped_out,
     grad, image, field, steps, sems, out_sems,
 ):
@@ -488,12 +498,13 @@
         loads.append(pltpu.make_async_copy(image_in.at[at[n]], image.at[at[n]], sems.at[1, n]))
     for copy in loads:
         copy.start()
+    here = Here(blocks, shifts)
     steps[...] = jnp.zeros((LANES, LANES), jnp.float32)
-    tiles = near_tiles(me, a, b, c, d, sb, sd)
+    tiles = near_tiles(both, ahead, third, behind)
     zero = jnp.zeros((1, LANES), jnp.float32)
     coefs = [state[q : q + 1, :] for q in range(3)]
     rows = []
-    for q, block in enumerate(block_ids(place_ref)):
+    for q, block in enumerate(here.block_ids()):
         gradsum = state[4 + q : 5 + q, :] + block_sums(tiles, block)
         rows += [-(gradsum + smooth_weight * pulled(coefs[q]))] + [zero] * 7
     solve(across(rows)[0:BLOCK, :], factor, steps)
@@ -501,8 +512,7 @@
     coefs = [coefs[q] + moved[8 * q : 8 * q + 1, :] for q in range(3)]
     coef_out[...] = coefs[2][:, :BLOCK]
     spline = Spline()
-    rigid = shift_step * place_ref[3].astype(jnp.float32)
-    field[...] = spline.field(joined(coefs)) + rigid
+    field[...] = spline.field(joined(coefs)) + here.rigid
     stores = []
     for n in range(CHUNKS):
         loads[2 * n].wait()
@@ -561,8 +571,7 @@
 
 def per_device(images, gradient, shifts, tile_blocks, intersections, start_coefficients):
     tiles = lax.axis_size("tile")
-    here = lax.axis_index("tile").astype(jnp.int32)
-    knot = lax.axis_index("knot").astype(jnp.int32)
+    knots = lax.axis_size("knot")
     ids = range(tiles)
     swap_a = [(i, i ^ 1) for i in ids]
     swap_b = [(i, ((i - 1) ^ 1) + 1) for i in ids if 0 < i < tiles - 1]
@@ -574,62 +583,71 @@
     def move(value, route):
         return lax.ppermute(value, "tile", route)
 
-    meta = intersections.reshape(-1)
+    def over_knot(value):
+        return [value] + [
+            lax.ppermute(value, "knot", [(i, (i + s) % knots) for i in range(knots)])
+            for s in range(1, knots)
+        ]
+
     far_b = move(gradient, swap_b)
     far_a = move(gradient, swap_a)
-    meta_a = move(meta, swap_a)
-    meta_b = move(meta, swap_b)
-    start = jnp.pad(start_coefficients, ((0, 7), (0, LANES - BLOCK)))
-    slot = jnp.arange(4, dtype=jnp.int32)[:, None] == knot
-    own = jnp.where(slot, start_coefficients, 0.0).reshape(2, LANES)
-    own = lax.psum(jnp.pad(own, ((0, 6), (0, 0))), "knot")
-    side_a = move(own, swap_a)
-    side_b = move(own, swap_b)
-    where = jnp.stack([here, tile_blocks[0, 0], tile_blocks[0, 1], shifts[0], knot])
+    meta_a = move(intersections, swap_a)
+    meta_b = move(intersections, swap_b)
+    column = jnp.concatenate(over_knot(start_coefficients), axis=0)
+    tables = (column, move(column, swap_a), move(column, swap_b))
 
     grad = viewed(gradient)
     image = viewed(images)
-    cross_early, weight, field, part = call(
+    cross_early, *sums, near, held = call(
         early_kernel, "early_pairs",
-        [SMEM] * 4 + [VMEM] * 3 + [ANY] * 3,
-        [VMEM] * 4,
-        [f32(2 * CAP, SLAB_ROWS, LANES), f32(ROWS, LANES), f32(PADDED, LANES), f32(8, LANES)],
-        [whole()] * 3 + [acc()] * 5 + [pltpu.SemaphoreType.DMA((3,))],
-    )(where, meta, meta_a, meta_b, own, side_a, side_b, grad, image, viewed(far_a))
-    cross_late, part = call(
+        [SMEM] * 2 + [ANY] * 3,
+        [VMEM] * 8,
+        [f32(2 * CAP, SLAB_ROWS, LANES)]
+        + [f32(ROWS, LANES)] * 4
+        + [f32(PADDED, LANES), f32(PADDED * DEPTH, LANES), f32(ROWS * DEPTH, LANES)],
+        [whole()] + [acc()] * 4 + [pltpu.SemaphoreType.DMA((3,))],
+    )(intersections, meta_a, grad, image, viewed(far_a))
+    cross_late, weight, part = call(
         late_kernel, "late_pairs",
-        [SMEM] * 2 + [VMEM] * 2 + [ANY] * 3,
-        [VMEM] * 2,
-        [f32(CAP, SLAB_ROWS, LANES), f32(8, LANES)],
-        [whole()] * 3 + [acc()] * 2 + [pltpu.SemaphoreType.DMA((3,))],
-    )(where, meta, field, part, grad, image, viewed(far_b))
+        [SMEM] * 4 + [VMEM] * 11 + [ANY],
+        [VMEM] * 3,
+        [f32(CAP, SLAB_ROWS, LANES), f32(ROWS, LANES), f32(8, LANES)],
+        [whole(), pltpu.VMEM((ROWS, LANES), jnp.float32)]
+        + [acc()] * 7
+        + [pltpu.SemaphoreType.DMA((1,))],
+    )(
+        intersections, meta_b, tile_blocks, shifts, *tables, near, held, cross_early, *sums,
+        viewed(far_b),
+    )
 
     def exchange(value):
-        me = lax.psum(value, "knot")
-        a = move(me, swap_a)
-        b = move(me, swap_b)
-        d = move(me, same_d)
-        c = move(me, swap_c)
-        sb = move(b, swap_a)
-        sd = move(d, swap_a)
-        return me, a, b, c, d, sb, sd
+        v = over_knot(value)
+        me = (v[0] + v[1]) + (v[2] + v[3])
+        both = jnp.concatenate([me, move(me, swap_a)], axis=0)
+        next_up = move(both, same_d)
+        third = move(me, swap_c)
+        next_up, third = lax.optimization_barrier((next_up, third))
+        return both, next_up, third, move(next_up, swap_a)
 
     part, state, factor = call(
         step_kernel, "first_step",
-        [SMEM] * 2 + [VMEM] * 14,
+        [SMEM] * 2 + [VMEM] * 11,
         [VMEM] * 3,
         [f32(8, LANES), f32(8, LANES), f32(4 * BLOCK, LANES)],
-        [acc(), square(), square()] + [acc()] * 6,
-    )(where, meta, *exchange(part), own, side_a, side_b, start, weight, cross_early, cross_late)
+        [pltpu.VMEM((ROWS, LANES), jnp.float32), square(), square()] + [acc()] * 6,
+    )(
+        intersections, tile_blocks, *exchange(part), *tables, start_coefficients, weight,
+        cross_early, cross_late,
+    )
     coef, warped = call(
         final_kernel, "second_step",
-        [SMEM] + [VMEM] * 9 + [ANY] * 2,
+        [SMEM] * 2 + [VMEM] * 6 + [ANY] * 2,
         [VMEM, ANY],
         [f32(1, BLOCK), f32(ROWS * DEPTH, LANES)],
         [pltpu.VMEM((ROWS * DEPTH, LANES), jnp.float32)] * 2
         + [pltpu.VMEM((ROWS, LANES), jnp.float32), square()]
         + [pltpu.SemaphoreType.DMA((2, CHUNKS)), pltpu.SemaphoreType.DMA((CHUNKS,))],
-    )(where, *exchange(part), state, factor, grad, image)
+    )(tile_blocks, shifts, *exchange(part), state, factor, grad, image)
     warped = warped.reshape(ROWS, DEPTH, LANES).transpose(1, 0, 2).reshape(1, DEPTH, ROWS * LANES)
     return coef, warped
 

time: 113 us -> 93.1 us (0.82)
  blocking collectives: 31.2 us -> 0 us
  waiting for transfers between devices: 10.3 us -> 20.4 us
  local copies, waits for them, and re-layouts: 10.6 us -> 3.98 us
  starting transfers between devices: 33.1 us -> 39 us
    psum x3 -> x0, blocking collectives: 31.2 us -> none  [the longest x2 19.4 us: exchange(): me = lax.psum(value, 'knot')]
    ppermute x0 -> x9, starting transfers between devices: none -> 14.5 us  [over_knot(): lax.ppermute(value, 'knot', [(i, (i + s) % knots) for i in range(knots)])]
    ppermute x18 -> x14, starting transfers between devices: 33.1 us -> 24.6 us  [move(): return lax.ppermute(value, 'tile', route)]
    ppermute x0 -> x9, waiting for transfers between devices: none -> 7.32 us  [over_knot(): lax.ppermute(value, 'knot', [(i, (i + s) % knots) for i in range(knots)])]
    unnamed x15 -> x13, local copies, waits for them, and re-layouts: 6.88 us -> 3.98 us
    ppermute x18 -> x14, waiting for transfers between devices: 10.3 us -> 13.1 us  [move(): return lax.ppermute(value, 'tile', route)]
    another operation x1 -> x0, local copies, waits for them, and re-layouts: 1.35 us -> none  [per_device(): jnp.stack([here, tile_blocks[0, 0], tile_blocks[0, 1], shifts[0], knot])]
    slice x1 -> x0, local copies, waits for them, and re-layouts: 1.31 us -> none  [per_device(): tile_blocks[0, 1]]
  transfers between devices with their start and end apart: 18 -> 23, of which waited for: 4 -> 12; matrix products, arithmetic and copies ran while one was open for 4% -> 2% of each run, Pallas kernels for 9% -> 7%
where the time goes in v2:
time: 93.1 us; the launch traced here: 93 us
  starting transfers between devices  39 us (42%)
  Pallas kernels  27.2 us (29%)
  waiting for transfers between devices  20.4 us (22%)
  local copies, waits for them, and re-layouts  3.98 us (4%)
  between operations  1.66 us (2%)
    ppermute x14, starting transfers between devices, move(): return lax.ppermute(value, 'tile', route)  24.6 us
    ppermute x9, starting transfers between devices, over_knot(): lax.ppermute(value, 'knot', [(i, (i + s) % knots) for i in range(knots)])  14.5 us
    ppermute x14, waiting for transfers between devices, move(): return lax.ppermute(value, 'tile', route)  13.1 us
    pallas_call x1, Pallas kernels, per_device(): call(late_kernel, 'late_pairs', [SMEM] * 4 + [VMEM] * 11 + [ANY], [VMEM]...  8.59 us
    pallas_call x1, Pallas kernels, per_device(): call(step_kernel, 'first_step', [SMEM] * 2 + [VMEM] * 11, [VMEM] * 3, [f3...  7.64 us
    ppermute x9, waiting for transfers between devices, over_knot(): lax.ppermute(value, 'knot', [(i, (i + s) % knots) for i in range(knots)])  7.32 us
    pallas_call x1, Pallas kernels, per_device(): call(early_kernel, 'early_pairs', [SMEM] * 2 + [ANY] * 3, [VMEM] * 8, [f3...  6.08 us
    pallas_call x1, Pallas kernels, per_device(): call(final_kernel, 'second_step', [SMEM] * 2 + [VMEM] * 6 + [ANY] * 2, [V...  4.92 us
  transfers between devices with their start and end apart: 23, of which 12 were waited for; matrix products, arithmetic and copies ran while one was open for 2% of the time, Pallas kernels for 7%

profile of v2, /device:TPU:24, one launch (start us, length us, event | category | flops | bytes accessed | tf_op | source)
XLA Modules:
  0.0 93.0 jit_solution(3462151026959093575)
XLA Ops:
  0.7 4.9 %collective-permute-start.8 = (f32[1,8,65536]{2,1,0:T(8,128)}, f32[1,8,65536]{2,1,0:T(8,128)}, u32[]{:S(2)}, u32[]{:S(2)}) collective-permute-start(f32[1,8,65536]{2,1,0:T(8,128)} %param.7), channel_id=1, source_target_pairs={{4,8},{8,4},{12,16},{16,12},{20,24},{24,20},{28,32},{32,28},{36,40... | collective-permute-start | bytes 6291464 | tf_op jit(solution)/shard_map/ppermute | solution.py:584
  5.7 2.0 %collective-permute-start.1 = (f32[1,64]{1,0:T(1,128)}, f32[1,64]{1,0:T(1,128)S(1)}, u32[]{:S(2)}, u32[]{:S(2)}) collective-permute-start(f32[1,64]{1,0:T(1,128)} %start.1), channel_id=1, source_target_pairs={{0,1},{1,2},{2,3},{3,0},{4,5},{5,6},{6,7},{7,4},{8,9},{9,10},{10,1... | collective-permute-start | bytes 776 | tf_op jit(solution)/shard_map/ppermute | solution.py:588
  7.7 3.6 %collective-permute-start.2 = (f32[1,64]{1,0:T(1,128)}, f32[1,64]{1,0:T(1,128)S(1)}, u32[]{:S(2)}, u32[]{:S(2)}) collective-permute-start(f32[1,64]{1,0:T(1,128)} %start.1), channel_id=1, source_target_pairs={{0,2},{1,3},{2,0},{3,1},{4,6},{5,7},{6,4},{7,5},{8,10},{9,11},{10,... | collective-permute-start | bytes 776 | tf_op jit(solution)/shard_map/ppermute | solution.py:588
  11.2 1.0 %collective-permute-start.3 = (f32[1,64]{1,0:T(1,128)}, f32[1,64]{1,0:T(1,128)S(1)}, u32[]{:S(2)}, u32[]{:S(2)}) collective-permute-start(f32[1,64]{1,0:T(1,128)} %start.1), channel_id=1, source_target_pairs={{0,3},{1,0},{2,1},{3,2},{4,7},{5,4},{6,5},{7,6},{8,11},{9,8},{10,9... | collective-permute-start | bytes 776 | tf_op jit(solution)/shard_map/ppermute | solution.py:588
  12.2 0.8 copy.12.meta
  13.1 1.8 %collective-permute-done.3 = f32[1,64]{1,0:T(1,128)S(1)} collective-permute-done((f32[1,64]{1,0:T(1,128)}, f32[1,64]{1,0:T(1,128)S(1)}, u32[]{:S(2)}, u32[]{:S(2)}) %collective-permute-start.3) | collective-permute-done | bytes 288 | tf_op jit(solution)/shard_map/ppermute | solution.py:588
  15.6 2.8 %collective-permute-start.5 = (f32[4,64]{1,0:T(4,128)S(1)}, f32[4,64]{1,0:T(4,128)S(1)}, u32[]{:S(2)}, u32[]{:S(2)}) collective-permute-start(f32[4,64]{1,0:T(4,128)S(1)} %pad_maximum_fusion.2.column), channel_id=1, source_target_pairs={{4,8},{8,4},{12,16},{16,12},{20,24},{24,20},{28,32},{32,28},{36,40... | collective-permute-start | bytes 3080 | tf_op jit(solution)/shard_map/ppermute | solution.py:584
  18.4 4.8 %collective-permute-start = (s32[1,3,8,5]{3,2,1,0:T(8,128)S(1)}, s32[1,3,8,5]{3,2,1,0:T(8,128)S(1)}, u32[]{:S(2)}, u32[]{:S(2)}) collective-permute-start(s32[1,3,8,5]{3,2,1,0:T(8,128)S(1)} %copy.12.meta), channel_id=1, source_target_pairs={{4,8},{8,4},{12,16},{16,12},{20,24},{24,20},{28,32},{32,28},{36,40... | collective-permute-start | bytes 1448 | tf_op jit(solution)/shard_map/ppermute | solution.py:584
  24.0 1.6 %copy-done = f32[1,8,65536]{2,1,0:T(8,128)S(1)} copy-done((f32[1,8,65536]{2,1,0:T(8,128)S(1)}, f32[1,8,65536]{2,1,0:T(8,128)}, u32[]{:S(2)}) %copy-start) | copy-done | bytes 2097176
  25.5 1.6 %copy-done.2 = f32[1,8,65536]{2,1,0:T(8,128)S(1)} copy-done((f32[1,8,65536]{2,1,0:T(8,128)S(1)}, f32[1,8,65536]{2,1,0:T(8,128)}, u32[]{:S(2)}) %copy-start.2) | copy-done | bytes 2097176
  27.1 6.1 %early_pairs.1 = (f32[16,72,128]{2,1,0:T(8,128)S(1)}, f32[512,128]{1,0:T(8,128)S(1)}, f32[512,128]{1,0:T(8,128)S(1)}, f32[512,128]{1,0:T(8,128)S(1)}, f32[512,12...) custom-call(s32[1,3,8,5]{3,2,1,0:T(8,128)S(1)} %copy.12.meta, ...), custom_call_target="tpu_custom_call" | custom-call | tf_op jit(solution)/shard_map/early_pairs/pallas_call | solution.py:601
  33.3 8.6 %late_pairs.1 = (f32[8,72,128]{2,1,0:T(8,128)S(1)}, f32[512,128]{1,0:T(8,128)S(1)}, f32[8,128]{1,0:T(8,128)S(1)}) custom-call(s32[1,3,8,5]{3,2,1,0:T(8,128)S(1)} %copy.12.meta, s32[1,3,8,5]{3,2,1,0:T(8,128)S(1)} %collective-permute-done.meta_b, s32[1,2]{1,0:T(1,128)S(1)} %copy-done.4, s32[1]{0:T(128)S(6)} %copy.13.shifts, ...), custom_call_target="tpu_custom_call" | custom-call | tf_op jit(solution)/shard_map/late_pairs/pallas_call | solution.py:610
  41.9 1.6 %collective-permute-start.10 = (f32[8,128]{1,0:T(8,128)S(1)}, f32[8,128]{1,0:T(8,128)S(1)}, u32[]{:S(2)}, u32[]{:S(2)}) collective-permute-start(f32[8,128]{1,0:T(8,128)S(1)} %get-tuple-element.30), channel_id=1, source_target_pairs={{0,2},{1,3},{2,0},{3,1},{4,6},{5,7},{6,4},{7,5},{8,10},{9,11},{10,... | collective-permute-start | bytes 12296 | tf_op jit(solution)/shard_map/ppermute | solution.py:588
  43.5 1.0 %collective-permute-start.11 = (f32[8,128]{1,0:T(8,128)S(1)}, f32[8,128]{1,0:T(8,128)S(1)}, u32[]{:S(2)}, u32[]{:S(2)}) collective-permute-start(f32[8,128]{1,0:T(8,128)S(1)} %get-tuple-element.30), channel_id=1, source_target_pairs={{0,3},{1,0},{2,1},{3,2},{4,7},{5,4},{6,5},{7,6},{8,11},{9,8},{10,9... | collective-permute-start | bytes 12296 | tf_op jit(solution)/shard_map/ppermute | solution.py:588
  44.5 1.0 %collective-permute-start.9 = (f32[8,128]{1,0:T(8,128)S(1)}, f32[8,128]{1,0:T(8,128)S(1)}, u32[]{:S(2)}, u32[]{:S(2)}) collective-permute-start(f32[8,128]{1,0:T(8,128)S(1)} %get-tuple-element.30), channel_id=1, source_target_pairs={{0,1},{1,2},{2,3},{3,0},{4,5},{5,6},{6,7},{7,4},{8,9},{9,10},{10,1... | collective-permute-start | bytes 12296 | tf_op jit(solution)/shard_map/ppermute | solution.py:588
  45.5 1.6 %collective-permute-done.10 = f32[8,128]{1,0:T(8,128)S(1)} collective-permute-done((f32[8,128]{1,0:T(8,128)S(1)}, f32[8,128]{1,0:T(8,128)S(1)}, u32[]{:S(2)}, u32[]{:S(2)}) %collective-permute-start.10) | collective-permute-done | bytes 4128 | tf_op jit(solution)/shard_map/ppermute | solution.py:588
  47.1 2.2 %collective-permute-done.9 = f32[8,128]{1,0:T(8,128)S(1)} collective-permute-done((f32[8,128]{1,0:T(8,128)S(1)}, f32[8,128]{1,0:T(8,128)S(1)}, u32[]{:S(2)}, u32[]{:S(2)}) %collective-permute-start.9) | collective-permute-done | bytes 4128 | tf_op jit(solution)/shard_map/ppermute | solution.py:588
  49.3 1.2 %collective-permute-done.12 = f32[8,128]{1,0:T(8,128)S(1)} collective-permute-done((f32[8,128]{1,0:T(8,128)S(1)}, f32[8,128]{1,0:T(8,128)S(1)}, u32[]{:S(2)}, u32[]{:S(2)}) %collective-permute-start.12) | collective-permute-done | bytes 4128 | tf_op jit(solution)/shard_map/ppermute | solution.py:584
  50.5 1.9 %collective-permute-start.13 = (f32[16,128]{1,0:T(8,128)S(1)}, f32[16,128]{1,0:T(8,128)S(1)}, u32[]{:S(2)}, u32[]{:S(2)}) collective-permute-start(f32[16,128]{1,0:T(8,128)S(1)} %pad_maximum_fusion.both), channel_id=1, source_target_pairs={{0,8},{8,16},{12,4},{16,24},{20,12},{24,32},{28,20},{32,40},{36,28... | collective-permute-start | bytes 24584 | tf_op jit(solution)/shard_map/ppermute | solution.py:584
  52.4 2.2 %collective-permute-start.14 = (f32[8,128]{1,0:T(8,128)S(1)}, f32[8,128]{1,0:T(8,128)S(1)}, u32[]{:S(2)}, u32[]{:S(2)}) collective-permute-start(f32[8,128]{1,0:T(8,128)S(1)} %add_add_fusion.1), channel_id=1, source_target_pairs={{4,16},{12,24},{16,4},{20,32},{24,12},{28,40},{32,20},{36,48},{40,... | collective-permute-start | bytes 12296 | tf_op jit(solution)/shard_map/ppermute | solution.py:584
  54.6 5.1 %collective-permute-done.14.third = f32[8,128]{1,0:T(8,128)S(1)} collective-permute-done((f32[8,128]{1,0:T(8,128)S(1)}, f32[8,128]{1,0:T(8,128)S(1)}, u32[]{:S(2)}, u32[]{:S(2)}) %collective-permute-start.14) | collective-permute-done | bytes 4128 | tf_op jit(solution)/shard_map/ppermute | solution.py:584
  59.9 1.1 %collective-permute-done.15.behind = f32[16,128]{1,0:T(8,128)S(1)} collective-permute-done((f32[16,128]{1,0:T(8,128)S(1)}, f32[16,128]{1,0:T(8,128)S(1)}, u32[]{:S(2)}, u32[]{:S(2)}) %collective-permute-start.15) | collective-permute-done | bytes 8224 | tf_op jit(solution)/shard_map/ppermute | solution.py:584
  60.9 7.6 %first_step.1 = (f32[8,128]{1,0:T(8,128)S(1)}, f32[8,128]{1,0:T(8,128)S(1)}, f32[256,128]{1,0:T(8,128)S(1)}) custom-call(s32[1,3,8,5]{3,2,1,0:T(8,128)S(1)} %copy.12.meta, s32[1,2]{1,0:T(1,128)S(1)} %copy-done.4, f32[16,128]{1,0:T(8,128)S(1)} %pad_maximum_fusion.both, f32[16,128]{1,0:T(8,128)S(1)} %collective-permute-done.13.ahead, ...), custom_call_target="tpu_custom_call" | custom-call | tf_op jit(solution)/shard_map/first_step/pallas_call | solution.py:632
  68.8 1.8 %collective-permute-start.17 = (f32[8,128]{1,0:T(8,128)S(1)}, f32[8,128]{1,0:T(8,128)S(1)}, u32[]{:S(2)}, u32[]{:S(2)}) collective-permute-start(f32[8,128]{1,0:T(8,128)S(1)} %get-tuple-element.35), channel_id=1, source_target_pairs={{0,2},{1,3},{2,0},{3,1},{4,6},{5,7},{6,4},{7,5},{8,10},{9,11},{10,... | collective-permute-start | bytes 12296 | tf_op jit(solution)/shard_map/ppermute | solution.py:588
  70.6 2.2 %collective-permute-start.18 = (f32[8,128]{1,0:T(8,128)S(1)}, f32[8,128]{1,0:T(8,128)S(1)}, u32[]{:S(2)}, u32[]{:S(2)}) collective-permute-start(f32[8,128]{1,0:T(8,128)S(1)} %get-tuple-element.35), channel_id=1, source_target_pairs={{0,3},{1,0},{2,1},{3,2},{4,7},{5,4},{6,5},{7,6},{8,11},{9,8},{10,9... | collective-permute-start | bytes 12296 | tf_op jit(solution)/shard_map/ppermute | solution.py:588
  74.5 1.2 %collective-permute-done.19 = f32[8,128]{1,0:T(8,128)S(1)} collective-permute-done((f32[8,128]{1,0:T(8,128)S(1)}, f32[8,128]{1,0:T(8,128)S(1)}, u32[]{:S(2)}, u32[]{:S(2)}) %collective-permute-start.19) | collective-permute-done | bytes 4128 | tf_op jit(solution)/shard_map/ppermute | solution.py:584
  75.7 2.2 %collective-permute-start.20 = (f32[16,128]{1,0:T(8,128)S(1)}, f32[16,128]{1,0:T(8,128)S(1)}, u32[]{:S(2)}, u32[]{:S(2)}) collective-permute-start(f32[16,128]{1,0:T(8,128)S(1)} %pad_maximum_fusion.1.both), channel_id=1, source_target_pairs={{0,8},{8,16},{12,4},{16,24},{20,12},{24,32},{28,20},{32,40},{36,28... | collective-permute-start | bytes 24584 | tf_op jit(solution)/shard_map/ppermute | solution.py:584
  77.9 3.6 %collective-permute-start.21 = (f32[8,128]{1,0:T(8,128)S(1)}, f32[8,128]{1,0:T(8,128)S(1)}, u32[]{:S(2)}, u32[]{:S(2)}) collective-permute-start(f32[8,128]{1,0:T(8,128)S(1)} %add_add_fusion), channel_id=1, source_target_pairs={{4,16},{12,24},{16,4},{20,32},{24,12},{28,40},{32,20},{36,48},{40,... | collective-permute-start | bytes 12296 | tf_op jit(solution)/shard_map/ppermute | solution.py:584
  81.5 3.7 %collective-permute-done.21.third = f32[8,128]{1,0:T(8,128)S(1)} collective-permute-done((f32[8,128]{1,0:T(8,128)S(1)}, f32[8,128]{1,0:T(8,128)S(1)}, u32[]{:S(2)}, u32[]{:S(2)}) %collective-permute-start.21) | collective-permute-done | bytes 4128 | tf_op jit(solution)/shard_map/ppermute | solution.py:584
  85.3 1.8 %collective-permute-start.22 = (f32[16,128]{1,0:T(8,128)S(1)}, f32[16,128]{1,0:T(8,128)S(1)}, u32[]{:S(2)}, u32[]{:S(2)}) collective-permute-start(f32[16,128]{1,0:T(8,128)S(1)} %collective-permute-done.20.ahead), channel_id=1, source_target_pairs={{0,4},{4,0},{8,12},{12,8},{16,20},{20,16},{24,28},{28,24},{32,36},... | collective-permute-start | bytes 24584 | tf_op jit(solution)/shard_map/ppermute | solution.py:584
  87.1 0.8 collective-permute-done.22.behind
  87.9 4.9 %second_step.1 = (f32[1,64]{1,0:T(1,128)}, f32[4096,128]{1,0:T(8,128)}) custom-call(s32[1,2]{1,0:T(1,128)S(1)} %copy-done.4, s32[1]{0:T(128)S(6)} %copy.13.shifts, f32[16,128]{1,0:T(8,128)S(1)} %pad_maximum_fusion.1.both, f32[16,128]{1,0:T(8,128)S(1)} %collective-permute-done.20.ahead, f32[8,128]{1,0:T(8,128)S(1)} %collective-permute-done.21.third, ...), custom_call_target="tpu_custom_call" | custom-call | tf_op jit(solution)/shard_map/second_step/pallas_call | solution.py:642
  (36 shorter events, 2.9 us)
Async XLA Ops:
  0.6 23.3 %collective-permute-start.7 = (f32[1,8,65536]{2,1,0:T(8,128)}, f32[1,8,65536]{2,1,0:T(8,128)S(1)}, u32[]{:S(2)}, u32[]{:S(2)}) collective-permute-start(f32[1,8,65536]{2,1,0:T(8,128)} %param.7), channel_id=1, source_target_pairs={{0,4},{4,0},{8,12},{12,8},{16,20},{20,16},{24,28},{28,24},{32,36},... | collective-permute-start | bytes 6291464 | tf_op jit(solution)/shard_map/ppermute | solution.py:584
  0.7 32.5 %collective-permute-start.8 = (f32[1,8,65536]{2,1,0:T(8,128)}, f32[1,8,65536]{2,1,0:T(8,128)}, u32[]{:S(2)}, u32[]{:S(2)}) collective-permute-start(f32[1,8,65536]{2,1,0:T(8,128)} %param.7), channel_id=1, source_target_pairs={{4,8},{8,4},{12,16},{16,12},{20,24},{24,20},{28,32},{32,28},{36,40... | collective-permute-start | bytes 6291464 | tf_op jit(solution)/shard_map/ppermute | solution.py:584
  5.7 7.4 %collective-permute-start.1 = (f32[1,64]{1,0:T(1,128)}, f32[1,64]{1,0:T(1,128)S(1)}, u32[]{:S(2)}, u32[]{:S(2)}) collective-permute-start(f32[1,64]{1,0:T(1,128)} %start.1), channel_id=1, source_target_pairs={{0,1},{1,2},{2,3},{3,0},{4,5},{5,6},{6,7},{7,4},{8,9},{9,10},{10,1... | collective-permute-start | bytes 776 | tf_op jit(solution)/shard_map/ppermute | solution.py:588
  7.7 5.4 %collective-permute-start.2 = (f32[1,64]{1,0:T(1,128)}, f32[1,64]{1,0:T(1,128)S(1)}, u32[]{:S(2)}, u32[]{:S(2)}) collective-permute-start(f32[1,64]{1,0:T(1,128)} %start.1), channel_id=1, source_target_pairs={{0,2},{1,3},{2,0},{3,1},{4,6},{5,7},{6,4},{7,5},{8,10},{9,11},{10,... | collective-permute-start | bytes 776 | tf_op jit(solution)/shard_map/ppermute | solution.py:588
  11.2 3.7 %collective-permute-start.3 = (f32[1,64]{1,0:T(1,128)}, f32[1,64]{1,0:T(1,128)S(1)}, u32[]{:S(2)}, u32[]{:S(2)}) collective-permute-start(f32[1,64]{1,0:T(1,128)} %start.1), channel_id=1, source_target_pairs={{0,3},{1,0},{2,1},{3,2},{4,7},{5,4},{6,5},{7,6},{8,11},{9,8},{10,9... | collective-permute-start | bytes 776 | tf_op jit(solution)/shard_map/ppermute | solution.py:588
  13.0 5.4 %collective-permute-start.6 = (s32[1,3,8,5]{3,2,1,0:T(8,128)S(1)}, s32[1,3,8,5]{3,2,1,0:T(8,128)S(1)}, u32[]{:S(2)}, u32[]{:S(2)}) collective-permute-start(s32[1,3,8,5]{3,2,1,0:T(8,128)S(1)} %copy.12.meta), channel_id=1, source_target_pairs={{0,4},{4,0},{8,12},{12,8},{16,20},{20,16},{24,28},{28,24},{32,36},... | collective-permute-start | bytes 1448 | tf_op jit(solution)/shard_map/ppermute | solution.py:584
  15.6 17.7 %collective-permute-start.4 = (f32[4,64]{1,0:T(4,128)S(1)}, f32[4,64]{1,0:T(4,128)S(1)}, u32[]{:S(2)}, u32[]{:S(2)}) collective-permute-start(f32[4,64]{1,0:T(4,128)S(1)} %pad_maximum_fusion.2.column), channel_id=1, source_target_pairs={{0,4},{4,0},{8,12},{12,8},{16,20},{20,16},{24,28},{28,24},{32,36},... | collective-permute-start | bytes 3080 | tf_op jit(solution)/shard_map/ppermute | solution.py:584
  15.6 17.7 %collective-permute-start.5 = (f32[4,64]{1,0:T(4,128)S(1)}, f32[4,64]{1,0:T(4,128)S(1)}, u32[]{:S(2)}, u32[]{:S(2)}) collective-permute-start(f32[4,64]{1,0:T(4,128)S(1)} %pad_maximum_fusion.2.column), channel_id=1, source_target_pairs={{4,8},{8,4},{12,16},{16,12},{20,24},{24,20},{28,32},{32,28},{36,40... | collective-permute-start | bytes 3080 | tf_op jit(solution)/shard_map/ppermute | solution.py:584
  18.4 14.8 %collective-permute-start = (s32[1,3,8,5]{3,2,1,0:T(8,128)S(1)}, s32[1,3,8,5]{3,2,1,0:T(8,128)S(1)}, u32[]{:S(2)}, u32[]{:S(2)}) collective-permute-start(s32[1,3,8,5]{3,2,1,0:T(8,128)S(1)} %copy.12.meta), channel_id=1, source_target_pairs={{4,8},{8,4},{12,16},{16,12},{20,24},{24,20},{28,32},{32,28},{36,40... | collective-permute-start | bytes 1448 | tf_op jit(solution)/shard_map/ppermute | solution.py:584
  23.9 1.6 %copy-start = (f32[1,8,65536]{2,1,0:T(8,128)S(1)}, f32[1,8,65536]{2,1,0:T(8,128)}, u32[]{:S(2)}) copy-start(f32[1,8,65536]{2,1,0:T(8,128)} %param.7) | copy-start | bytes 6291460
  25.5 1.6 %copy-start.2 = (f32[1,8,65536]{2,1,0:T(8,128)S(1)}, f32[1,8,65536]{2,1,0:T(8,128)}, u32[]{:S(2)}) copy-start(f32[1,8,65536]{2,1,0:T(8,128)} %param.6) | copy-start | bytes 6291460
  27.1 6.1 %copy-start.4 = (s32[1,2]{1,0:T(1,128)S(1)}, s32[1,2]{1,0:T(1,128)}, u32[]{:S(2)}) copy-start(s32[1,2]{1,0:T(1,128)} %blocks.5) | copy-start | bytes 28
  33.3 27.7 %copy-start.5 = (f32[1,64]{1,0:T(1,128)S(1)}, f32[1,64]{1,0:T(1,128)}, u32[]{:S(2)}) copy-start(f32[1,64]{1,0:T(1,128)} %start.1) | copy-start | bytes 772
  33.3 54.6 %copy-start.1 = (f32[1,8,65536]{2,1,0:T(8,128)S(1)}, f32[1,8,65536]{2,1,0:T(8,128)}, u32[]{:S(2)}) copy-start(f32[1,8,65536]{2,1,0:T(8,128)} %param.7) | copy-start | bytes 6291460
  33.3 54.6 %copy-start.3 = (f32[1,8,65536]{2,1,0:T(8,128)S(1)}, f32[1,8,65536]{2,1,0:T(8,128)}, u32[]{:S(2)}) copy-start(f32[1,8,65536]{2,1,0:T(8,128)} %param.6) | copy-start | bytes 6291460
  41.9 5.2 %collective-permute-start.10 = (f32[8,128]{1,0:T(8,128)S(1)}, f32[8,128]{1,0:T(8,128)S(1)}, u32[]{:S(2)}, u32[]{:S(2)}) collective-permute-start(f32[8,128]{1,0:T(8,128)S(1)} %get-tuple-element.30), channel_id=1, source_target_pairs={{0,2},{1,3},{2,0},{3,1},{4,6},{5,7},{6,4},{7,5},{8,10},{9,11},{10,... | collective-permute-start | bytes 12296 | tf_op jit(solution)/shard_map/ppermute | solution.py:588
  43.5 3.6 %collective-permute-start.11 = (f32[8,128]{1,0:T(8,128)S(1)}, f32[8,128]{1,0:T(8,128)S(1)}, u32[]{:S(2)}, u32[]{:S(2)}) collective-permute-start(f32[8,128]{1,0:T(8,128)S(1)} %get-tuple-element.30), channel_id=1, source_target_pairs={{0,3},{1,0},{2,1},{3,2},{4,7},{5,4},{6,5},{7,6},{8,11},{9,8},{10,9... | collective-permute-start | bytes 12296 | tf_op jit(solution)/shard_map/ppermute | solution.py:588
  44.5 4.8 %collective-permute-start.9 = (f32[8,128]{1,0:T(8,128)S(1)}, f32[8,128]{1,0:T(8,128)S(1)}, u32[]{:S(2)}, u32[]{:S(2)}) collective-permute-start(f32[8,128]{1,0:T(8,128)S(1)} %get-tuple-element.30), channel_id=1, source_target_pairs={{0,1},{1,2},{2,3},{3,0},{4,5},{5,6},{6,7},{7,4},{8,9},{9,10},{10,1... | collective-permute-start | bytes 12296 | tf_op jit(solution)/shard_map/ppermute | solution.py:588
  49.3 1.2 %collective-permute-start.12 = (f32[8,128]{1,0:T(8,128)S(1)}, f32[8,128]{1,0:T(8,128)S(1)}, u32[]{:S(2)}, u32[]{:S(2)}) collective-permute-start(f32[8,128]{1,0:T(8,128)S(1)} %add_add_fusion.1), channel_id=1, source_target_pairs={{0,4},{4,0},{8,12},{12,8},{16,20},{20,16},{24,28},{28,24},{32,36},... | collective-permute-start | bytes 12296 | tf_op jit(solution)/shard_map/ppermute | solution.py:584
  50.5 9.2 %collective-permute-start.13 = (f32[16,128]{1,0:T(8,128)S(1)}, f32[16,128]{1,0:T(8,128)S(1)}, u32[]{:S(2)}, u32[]{:S(2)}) collective-permute-start(f32[16,128]{1,0:T(8,128)S(1)} %pad_maximum_fusion.both), channel_id=1, source_target_pairs={{0,8},{8,16},{12,4},{16,24},{20,12},{24,32},{28,20},{32,40},{36,28... | collective-permute-start | bytes 24584 | tf_op jit(solution)/shard_map/ppermute | solution.py:584
  52.4 7.3 %collective-permute-start.14 = (f32[8,128]{1,0:T(8,128)S(1)}, f32[8,128]{1,0:T(8,128)S(1)}, u32[]{:S(2)}, u32[]{:S(2)}) collective-permute-start(f32[8,128]{1,0:T(8,128)S(1)} %add_add_fusion.1), channel_id=1, source_target_pairs={{4,16},{12,24},{16,4},{20,32},{24,12},{28,40},{32,20},{36,48},{40,... | collective-permute-start | bytes 12296 | tf_op jit(solution)/shard_map/ppermute | solution.py:584
  59.7 1.2 %collective-permute-start.15 = (f32[16,128]{1,0:T(8,128)S(1)}, f32[16,128]{1,0:T(8,128)S(1)}, u32[]{:S(2)}, u32[]{:S(2)}) collective-permute-start(f32[16,128]{1,0:T(8,128)S(1)} %collective-permute-done.13.ahead), channel_id=1, source_target_pairs={{0,4},{4,0},{8,12},{12,8},{16,20},{20,16},{24,28},{28,24},{32,36},... | collective-permute-start | bytes 24584 | tf_op jit(solution)/shard_map/ppermute | solution.py:584
  68.6 5.1 %collective-permute-start.16 = (f32[8,128]{1,0:T(8,128)S(1)}, f32[8,128]{1,0:T(8,128)S(1)}, u32[]{:S(2)}, u32[]{:S(2)}) collective-permute-start(f32[8,128]{1,0:T(8,128)S(1)} %get-tuple-element.35), channel_id=1, source_target_pairs={{0,1},{1,2},{2,3},{3,0},{4,5},{5,6},{6,7},{7,4},{8,9},{9,10},{10,1... | collective-permute-start | bytes 12296 | tf_op jit(solution)/shard_map/ppermute | solution.py:588
  68.8 5.2 %collective-permute-start.17 = (f32[8,128]{1,0:T(8,128)S(1)}, f32[8,128]{1,0:T(8,128)S(1)}, u32[]{:S(2)}, u32[]{:S(2)}) collective-permute-start(f32[8,128]{1,0:T(8,128)S(1)} %get-tuple-element.35), channel_id=1, source_target_pairs={{0,2},{1,3},{2,0},{3,1},{4,6},{5,7},{6,4},{7,5},{8,10},{9,11},{10,... | collective-permute-start | bytes 12296 | tf_op jit(solution)/shard_map/ppermute | solution.py:588
  70.6 3.9 %collective-permute-start.18 = (f32[8,128]{1,0:T(8,128)S(1)}, f32[8,128]{1,0:T(8,128)S(1)}, u32[]{:S(2)}, u32[]{:S(2)}) collective-permute-start(f32[8,128]{1,0:T(8,128)S(1)} %get-tuple-element.35), channel_id=1, source_target_pairs={{0,3},{1,0},{2,1},{3,2},{4,7},{5,4},{6,5},{7,6},{8,11},{9,8},{10,9... | collective-permute-start | bytes 12296 | tf_op jit(solution)/shard_map/ppermute | solution.py:588
  74.5 1.2 %collective-permute-start.19 = (f32[8,128]{1,0:T(8,128)S(1)}, f32[8,128]{1,0:T(8,128)S(1)}, u32[]{:S(2)}, u32[]{:S(2)}) collective-permute-start(f32[8,128]{1,0:T(8,128)S(1)} %add_add_fusion), channel_id=1, source_target_pairs={{0,4},{4,0},{8,12},{12,8},{16,20},{20,16},{24,28},{28,24},{32,36},... | collective-permute-start | bytes 12296 | tf_op jit(solution)/shard_map/ppermute | solution.py:584
  75.7 9.6 %collective-permute-start.20 = (f32[16,128]{1,0:T(8,128)S(1)}, f32[16,128]{1,0:T(8,128)S(1)}, u32[]{:S(2)}, u32[]{:S(2)}) collective-permute-start(f32[16,128]{1,0:T(8,128)S(1)} %pad_maximum_fusion.1.both), channel_id=1, source_target_pairs={{0,8},{8,16},{12,4},{16,24},{20,12},{24,32},{28,20},{32,40},{36,28... | collective-permute-start | bytes 24584 | tf_op jit(solution)/shard_map/ppermute | solution.py:584
  77.9 7.3 %collective-permute-start.21 = (f32[8,128]{1,0:T(8,128)S(1)}, f32[8,128]{1,0:T(8,128)S(1)}, u32[]{:S(2)}, u32[]{:S(2)}) collective-permute-start(f32[8,128]{1,0:T(8,128)S(1)} %add_add_fusion), channel_id=1, source_target_pairs={{4,16},{12,24},{16,4},{20,32},{24,12},{28,40},{32,20},{36,48},{40,... | collective-permute-start | bytes 12296 | tf_op jit(solution)/shard_map/ppermute | solution.py:584
  85.3 2.6 %collective-permute-start.22 = (f32[16,128]{1,0:T(8,128)S(1)}, f32[16,128]{1,0:T(8,128)S(1)}, u32[]{:S(2)}, u32[]{:S(2)}) collective-permute-start(f32[16,128]{1,0:T(8,128)S(1)} %collective-permute-done.20.ahead), channel_id=1, source_target_pairs={{0,4},{4,0},{8,12},{12,8},{16,20},{20,16},{24,28},{28,24},{32,36},... | collective-permute-start | bytes 24584 | tf_op jit(solution)/shard_map/ppermute | solution.py:584

commit v3 on v2

--- a/solution.py
+++ b/solution.py
@@ -22,8 +22,7 @@
 smooth_weight = 20.0
 ridge_weight = 1.0
 
-EXACT = lax.Precision.HIGHEST
-VMEM_LIMIT = 24 * 1024 * 1024
+EXACT = lax.Precision.HIGH
 
 
 def iota(shape, dim):
@@ -136,19 +135,23 @@
         odd = self.tile & 1
         self.to_a = jnp.where(odd == 0, 2, 0)
         self.to_b = 2 - self.to_a
+        self.side_b = self.tile + jnp.where(odd == 0, -1, 1)
         if blocks is not None:
-            self.blocks = [blocks[0, 0], blocks[0, 1]]
+            both = blocks[...].astype(jnp.float32)
+            self.blocks = [jnp.broadcast_to(both[:, n : n + 1], (1, LANES)) for n in range(2)]
         if shifts is not None:
-            self.rigid = shift_step * shifts[0].astype(jnp.float32)
+            self.rigid = shift_step * jnp.broadcast_to(
+                shifts[...].astype(jnp.float32), (1, LANES)
+            )
 
     def block_row(self):
         lane = iota((1, LANES), 1)
-        row = jnp.where(lane < BLOCK, self.blocks[0], self.blocks[1]).astype(jnp.float32)
+        row = jnp.where(lane < BLOCK, self.blocks[0], self.blocks[1])
         return jnp.where(self.knot == 0, 1.0, 0.0) * row
 
     def block_ids(self):
-        owned = self.tile * 4 + self.knot
-        return [b.astype(jnp.float32) for b in self.blocks + [owned]]
+        owned = (self.tile * 4 + self.knot).astype(jnp.float32)
+        return self.blocks + [jnp.full((1, LANES), owned)]
 
 
 def place(pair, p):
@@ -159,13 +162,37 @@
     return row_b, lead, start >> 7, start & 127
 
 
-def add_moved(accs, row_a, turn, i, value):
-    lane = iota((8, LANES), 1)
-    moved = pltpu.roll(value, turn, 1)
-    keep = lane >= turn
-    at = pl.ds(row_a + (LEAD + 8 * i), 8)
-    accs[0][at, :] += jnp.where(keep, moved, 0.0)
-    accs[1][at, :] += jnp.where(keep, 0.0, moved)
+def window(ref, row, rows=SLAB_ROWS):
+    return ref.at[pl.ds(pl.multiple_of((row + LEAD) * 8, 8), rows * 8)]
+
+
+def rows_at(row, plane):
+    return pl.ds(row * 8 + plane, 8, stride=8)
+
+
+def all_rows(plane, back=0):
+    return pl.ds((LEAD - back) * 8 + plane, ROWS, stride=8)
+
+
+def moved_sums(planes, plane, row_a, turn, values):
+    keep = iota((8, LANES), 1) >= turn
+    out = window(planes, row_a)
+    sums = []
+    for i, value in enumerate(values):
+        moved = pltpu.roll(value, turn, 1)
+        sums.append(
+            (
+                out[rows_at(8 * i, plane), :] + jnp.where(keep, moved, 0.0),
+                out[rows_at(8 * i, plane + 1), :] + jnp.where(keep, 0.0, moved),
+            )
+        )
+
+    def store():
+        for i, (kept, passed) in enumerate(sums):
+            out[rows_at(8 * i, plane), :] = kept
+            out[rows_at(8 * i, plane + 1), :] = passed
+
+    return store
 
 
 def live_count(pair):
@@ -175,11 +202,18 @@
     return total
 
 
-def pair_reader(ref, direction):
-    return lambda p, field: ref[0, direction, p, field]
-
-
-def slabs(pair, base, far, grad, image, cross, accs, field=None):
+def sent_reader(ref, direction):
+    def read(p, field):
+        at = (direction * CAP + p) * 5 + field
+        return ref[4 + (at >> 6), at & 63].astype(jnp.int32)
+
+    return read
+
+
+FIELD, COUNT = 6, 7
+
+
+def slabs(pair, base, far, grad, image, cross, planes, plane, with_field):
     lane = iota((8, LANES), 1)
     sub = iota((8, LANES), 0)
 
@@ -187,46 +221,63 @@
         row_b, lead, row_a, turn = place(pair, p)
         back = (LANES - turn) & 127
         keep = lane >= turn
+        values = []
+        far_rows = window(far, row_a, SLAB_ROWS + 8)
+        grad_rows = window(grad, row_b)
+        image_rows = window(image, row_b)
+        field_rows = window(planes, row_b)
         for i in range(GROUPS):
             c = jnp.zeros((8, LANES), jnp.float32)
             x = jnp.zeros((8, LANES), jnp.float32)
             for z in range(DEPTH):
-                at_a = (row_a + (LEAD + 8 * i)) * 8 + z
-                at_b = (row_b + 8 * i) * 8 + z
-                at_g = at_b + LEAD * 8
-                first = far[pl.ds(at_a, 8, stride=8), :]
-                second = far[pl.ds(at_a + 8, 8, stride=8), :]
+                first = far_rows[rows_at(8 * i, z), :]
+                second = far_rows[rows_at(8 * i + 1, z), :]
                 slope = pltpu.roll(jnp.where(keep, first, second), back, 1)
-                c = c + slope * grad[pl.ds(at_g, 8, stride=8), :]
-                x = x + slope * image[pl.ds(at_b, 8, stride=8), :]
+                c = c + slope * grad_rows[rows_at(8 * i, z), :]
+                x = x + slope * image_rows[rows_at(8 * i, z), :]
             if i in (0, 1, GROUPS - 1):
                 s = (sub + 8 * i) * LANES + lane - lead
                 valid = (s >= 0) & (s < SLAB)
                 c = jnp.where(valid, c, 0.0)
                 x = jnp.where(valid, x, 0.0)
             cross[base + p, 8 * i : 8 * i + 8, :] = c
-            if field is not None:
-                x = x + c * field[pl.ds(row_b + 8 * i, 8), :]
-            add_moved(accs, row_a, turn, i, x)
+            if with_field:
+                x = x + c * field_rows[rows_at(8 * i, FIELD), :]
+            values.append(x)
+        moved_sums(planes, plane, row_a, turn, values)()
         return carry
 
     lax.fori_loop(0, live_count(pair), body, 0)
 
 
-def slab_steps(pair, base, field, cross, accs):
+def slab_steps(groups, planes):
+    counts = [live_count(pair) for pair, _, _, _ in groups]
+    total = functools.reduce(jnp.maximum, counts)
+
     def body(p, carry):
-        row_b, lead, row_a, turn = place(pair, p)
-        for i in range(GROUPS):
-            c = cross[base + p, 8 * i : 8 * i + 8, :]
-            value = c * field[pl.ds(row_b + 8 * i, 8), :]
-            add_moved(accs, row_a, turn, i, value)
+        done = []
+        for (pair, base, cross, plane), count in zip(groups, counts):
+            row_b, _, row_a, turn = place(pair, p)
+            field_rows = window(planes, row_b)
+            live = p < count
+            values = [
+                jnp.where(
+                    live,
+                    cross[base + p, 8 * i : 8 * i + 8, :] * field_rows[rows_at(8 * i, FIELD), :],
+                    0.0,
+                )
+                for i in range(GROUPS)
+            ]
+            done.append(moved_sums(planes, plane, row_a, turn, values))
+        for store in done:
+            store()
         return carry
 
-    lax.fori_loop(0, live_count(pair), body, 0)
-
-
-def collected(accs):
-    return accs[0][LEAD : LEAD + ROWS, :] + accs[1][LEAD - 1 : LEAD + ROWS - 1, :]
+    lax.fori_loop(0, total, body, 0)
+
+
+def collected(planes, plane):
+    return planes[all_rows(plane), :] + planes[all_rows(plane + 1, 1), :]
 
 
 def clear(refs):
@@ -239,63 +290,59 @@
     ref[(LEAD + ROWS) * 8 :, :] = jnp.zeros(((PADDED - LEAD - ROWS) * 8, LANES), jnp.float32)
 
 
-def local_values(here, own, side_a, side_b):
-    out = []
-    for block in here.blocks:
-        col, slot = block >> 2, block & 3
-        back = (here.knot - slot) & 3
-        table = jnp.where(
-            col == here.tile,
-            own[...],
-            jnp.where(col == (here.tile ^ 1), side_a[...], side_b[...]),
-        )
-        out.append(
-            jnp.where(
-                back == 0,
-                table[0:1],
-                jnp.where(back == 1, table[1:2], jnp.where(back == 2, table[2:3], table[3:4])),
-            )
-        )
+def local_values(here, tables):
+    out = [jnp.zeros((1, BLOCK), jnp.float32) for _ in range(2)]
+    for table, col in zip(tables, (here.tile, here.tile ^ 1, here.side_b)):
+        for n in range(4):
+            held = (col * 4 + ((here.knot - n) & 3)).astype(jnp.float32)
+            for half in range(2):
+                out[half] = jnp.where(
+                    here.blocks[half][:, :BLOCK] == held, table[n : n + 1, :], out[half]
+                )
     return jnp.concatenate(out, axis=1)
+
+
+def scalar_copies(tables, scalars, sems):
+    copies = [
+        pltpu.make_async_copy(t, m, sems.at[n]) for n, (t, m) in enumerate(zip(tables, scalars))
+    ]
+    for c in copies:
+        c.start()
+    return copies
 
 
 def padded_copy(source, target, sem):
     return pltpu.make_async_copy(source, target.at[pl.ds(LEAD * 8, ROWS * 8)], sem)
 
 
-def cover(pair, count):
+def cover(pair, planes):
     lane = iota((8, LANES), 1)
     sub = iota((8, LANES), 0)
 
     def body(p, carry):
         off = pair(p, 3)
+        rows = window(planes, off >> 7)
+        counts = [rows[rows_at(8 * i, COUNT), :] for i in range(GROUPS)]
         for i in range(GROUPS):
             s = (sub + 8 * i) * LANES + lane - (off & 127)
             inside = (s >= 0) & (s < SLAB)
-            count[pl.ds((off >> 7) + (LEAD + 8 * i), 8), :] += jnp.where(inside, 1.0, 0.0)
+            rows[rows_at(8 * i, COUNT), :] = counts[i] + jnp.where(inside, 1.0, 0.0)
         return carry
 
     lax.fori_loop(0, live_count(pair), body, 0)
 
 
 def early_kernel(
-    meta, meta_a, grad_in, image_in, far_in,
-    cross, weight_out, value_out, own_out, side_out, count, near, image,
-    far, acc0, acc1, acc2, acc3, sems,
+    column, near, image, far_in,
+    cross, weight_out, value_out, own_out, side_out, count_out,
+    far, planes, scalars, sems,
 ):
-    copies = [
-        padded_copy(grad_in, near, sems.at[0]),
-        pltpu.make_async_copy(image_in, image, sems.at[1]),
-        padded_copy(far_in, far, sems.at[2]),
-    ]
-    for c in copies:
-        c.start()
-    for ref in (near, far):
-        clear_ends(ref)
-    clear((acc0, acc1, acc2, acc3, count))
+    reads = scalar_copies((column,), (scalars,), sems)
+    copy = padded_copy(far_in, far, sems.at[1])
+    copy.start()
+    clear_ends(far)
+    clear((planes,))
     here = Here()
-    cover(pair_reader(meta, 1), count)
-    cover(pair_reader(meta_a, 2 - here.to_a), count)
 
     def rows(g, carry):
         w = jnp.zeros((8, LANES), jnp.float32)
@@ -303,49 +350,61 @@
         for z in range(DEPTH):
             slope = near[pl.ds(64 * g + (LEAD * 8 + z), 8, stride=8), :]
             w = w + slope * slope
-            v = v + slope * image[pl.ds(64 * g + z, 8, stride=8), :]
+            v = v + slope * image[pl.ds(64 * g + (LEAD * 8 + z), 8, stride=8), :]
         at = pl.ds(pl.multiple_of(8 * g, 8), 8)
         weight_out[at, :] = w
         value_out[at, :] = v
         return carry
 
-    copies[0].wait()
-    copies[1].wait()
     lax.fori_loop(0, ROWS // 8, rows, 0)
-    slabs(pair_reader(meta, 1), 0, near, near, image, cross, (acc0, acc1))
-    copies[2].wait()
-    slabs(pair_reader(meta, here.to_a), CAP, far, near, image, cross, (acc2, acc3))
-    own_out[...] = collected((acc0, acc1))
-    side_out[...] = collected((acc2, acc3))
+    reads[0].wait()
+    cover(sent_reader(scalars, 1), planes)
+    slabs(sent_reader(scalars, 1), 0, near, near, image, cross, planes, 0, False)
+    copy.wait()
+    slabs(sent_reader(scalars, here.to_a), CAP, far, near, image, cross, planes, 2, False)
+    own_out[...] = collected(planes, 0)
+    side_out[...] = collected(planes, 2)
+    count_out[...] = planes[all_rows(COUNT), :]
 
 
 def late_kernel(
-    meta, meta_b, blocks, shifts, column, side_a, side_b,
+    blocks, shifts, column, side_a, side_b,
     near, image, cross_early, weight, value, own, side, counted, far_in,
     cross, weight_out, part_out,
-    far, field, count, acc0, acc1, acc2, acc3, acc4, acc5, sems,
+    far, planes, scalars_own, scalars_a, scalars_b, sems, scalar_sems,
 ):
+    reads = scalar_copies(
+        (column, side_a, side_b), (scalars_own, scalars_a, scalars_b), scalar_sems
+    )
     copy = padded_copy(far_in, far, sems.at[0])
     copy.start()
     here = Here(blocks, shifts)
     clear_ends(far)
-    clear((acc0, acc1, acc2, acc3, acc4, acc5))
-    count[...] = counted[...]
-    cover(pair_reader(meta_b, 2 - here.to_b), count)
+    clear((planes,))
     spline = Spline()
-    field[...] = spline.field(local_values(here, column, side_a, side_b)) + here.rigid
-    slab_steps(pair_reader(meta, 1), 0, field, cross_early, (acc0, acc1))
-    slab_steps(pair_reader(meta, here.to_a), CAP, field, cross_early, (acc2, acc3))
+    field = spline.field(local_values(here, (column, side_a, side_b))) + here.rigid
+    planes[all_rows(FIELD), :] = field
+    for c in reads:
+        c.wait()
+    cover(sent_reader(scalars_a, 2 - here.to_a), planes)
+    cover(sent_reader(scalars_b, 2 - here.to_b), planes)
+    slab_steps(
+        [
+            (sent_reader(scalars_own, 1), 0, cross_early, 0),
+            (sent_reader(scalars_own, here.to_a), CAP, cross_early, 2),
+        ],
+        planes,
+    )
     copy.wait()
-    slabs(pair_reader(meta, here.to_b), 0, far, near, image, cross, (acc4, acc5), field)
-    n = count[LEAD : LEAD + ROWS, :]
+    slabs(sent_reader(scalars_own, here.to_b), 0, far, near, image, cross, planes, 4, True)
+    n = counted[...] + planes[all_rows(COUNT), :]
     w = weight[...] * n
     weight_out[...] = w
     part_out[0:1, :] = spline.adjoint(
-        value[...] * n + w * field[...] - own[...] - collected((acc0, acc1))
-    )
-    part_out[1:2, :] = -spline.adjoint(side[...] + collected((acc2, acc3)))
-    part_out[2:3, :] = -spline.adjoint(collected((acc4, acc5)))
+        value[...] * n + w * planes[all_rows(FIELD), :] - own[...] - collected(planes, 0)
+    )
+    part_out[1:2, :] = -spline.adjoint(side[...] + collected(planes, 2))
+    part_out[2:3, :] = -spline.adjoint(collected(planes, 4))
     part_out[3:4, :] = here.block_row()
     for m, row in enumerate(spline.band(w)):
         part_out[4 + m : 5 + m, :] = row
@@ -413,17 +472,18 @@
 
 
 def step_kernel(
-    meta, blocks, both, ahead, third, behind, column, side_a, side_b, start, weight,
+    blocks, both, ahead, third, behind, column, side_a, side_b, start, weight,
     cross_early, cross_late,
     part_out, state, factor,
-    field, steps, work, acc0, acc1, acc2, acc3, acc4, acc5,
+    planes, steps, work, scalars, scalar_sems,
 ):
+    reads = scalar_copies((column,), (scalars,), scalar_sems)
     here = Here(blocks)
-    clear((acc0, acc1, acc2, acc3, acc4, acc5, steps))
+    clear((planes, steps))
     lane = iota((1, LANES), 1)
     zero = jnp.zeros((1, LANES), jnp.float32)
     tiles = near_tiles(both, ahead, third, behind)
-    knots = local_values(here, column, side_a, side_b)
+    knots = local_values(here, (column, side_a, side_b))
     coefs = [
         jnp.where(lane < BLOCK, knots, 0.0),
         jnp.where(lane < BLOCK, pltpu.roll(knots, BLOCK, 1), 0.0),
@@ -471,13 +531,21 @@
         [coefs[q] + change[q] for q in range(3)] + [zero] + sums + [zero], axis=0
     )
     spline = Spline()
-    field[...] = spline.field(joined(change))
-    slab_steps(pair_reader(meta, 1), 0, field, cross_early, (acc0, acc1))
-    slab_steps(pair_reader(meta, here.to_a), CAP, field, cross_early, (acc2, acc3))
-    slab_steps(pair_reader(meta, here.to_b), 0, field, cross_late, (acc4, acc5))
-    part_out[0:1, :] = spline.adjoint(weight[...] * field[...] - collected((acc0, acc1)))
-    part_out[1:2, :] = -spline.adjoint(collected((acc2, acc3)))
-    part_out[2:3, :] = -spline.adjoint(collected((acc4, acc5)))
+    planes[all_rows(FIELD), :] = spline.field(joined(change))
+    reads[0].wait()
+    slab_steps(
+        [
+            (sent_reader(scalars, 1), 0, cross_early, 0),
+            (sent_reader(scalars, here.to_a), CAP, cross_early, 2),
+            (sent_reader(scalars, here.to_b), 0, cross_late, 4),
+        ],
+        planes,
+    )
+    part_out[0:1, :] = spline.adjoint(
+        weight[...] * planes[all_rows(FIELD), :] - collected(planes, 0)
+    )
+    part_out[1:2, :] = -spline.adjoint(collected(planes, 2))
+    part_out[2:3, :] = -spline.adjoint(collected(planes, 4))
     part_out[3:4, :] = here.block_row()
     part_out[4:8, :] = jnp.zeros((4, LANES), jnp.float32)
 
@@ -532,9 +600,9 @@
         copy.wait()
 
 
-SMEM = pl.BlockSpec(memory_space=pltpu.SMEM)
 VMEM = pl.BlockSpec(memory_space=pltpu.VMEM)
 ANY = pl.BlockSpec(memory_space=pl.ANY)
+HBM = pl.BlockSpec(memory_space=pltpu.HBM)
 
 
 def f32(*shape):
@@ -549,16 +617,12 @@
         out_specs=out_specs,
         out_shape=out_shape,
         scratch_shapes=scratch,
-        compiler_params=pltpu.CompilerParams(vmem_limit_bytes=VMEM_LIMIT),
+        compiler_params=pltpu.CompilerParams(vmem_limit_bytes=24 * 1024 * 1024),
     )
 
 
 def whole():
     return pltpu.VMEM((PADDED * 8, LANES), jnp.float32)
-
-
-def acc():
-    return pltpu.VMEM((PADDED, LANES), jnp.float32)
 
 
 def square():
@@ -589,59 +653,59 @@
             for s in range(1, knots)
         ]
 
+    shifts = shifts.reshape(1, 1)
     far_b = move(gradient, swap_b)
     far_a = move(gradient, swap_a)
-    meta_a = move(intersections, swap_a)
-    meta_b = move(intersections, swap_b)
-    column = jnp.concatenate(over_knot(start_coefficients), axis=0)
-    tables = (column, move(column, swap_a), move(column, swap_b))
-
-    grad = viewed(gradient)
-    image = viewed(images)
-    cross_early, *sums, near, held = call(
+    sent = jnp.pad(intersections.reshape(1, -1).astype(jnp.float32), ((0, 0), (0, 8)))
+    column = jnp.concatenate(over_knot(start_coefficients) + [sent.reshape(2, BLOCK)], axis=0)
+    side_a, side_b = move(column, swap_a), move(column, swap_b)
+
+    grad, image = viewed(gradient), viewed(images)
+    ends = ((LEAD * 8, (PADDED - LEAD - ROWS) * 8), (0, 0))
+    near, held = jnp.pad(grad, ends), jnp.pad(image, ends)
+    cross_early, *sums = call(
         early_kernel, "early_pairs",
-        [SMEM] * 2 + [ANY] * 3,
-        [VMEM] * 8,
-        [f32(2 * CAP, SLAB_ROWS, LANES)]
-        + [f32(ROWS, LANES)] * 4
-        + [f32(PADDED, LANES), f32(PADDED * DEPTH, LANES), f32(ROWS * DEPTH, LANES)],
-        [whole()] + [acc()] * 4 + [pltpu.SemaphoreType.DMA((3,))],
-    )(intersections, meta_a, grad, image, viewed(far_a))
+        [VMEM] * 3 + [HBM],
+        [VMEM] * 6,
+        [f32(2 * CAP, SLAB_ROWS, LANES)] + [f32(ROWS, LANES)] * 5,
+        [whole()] * 2 + [pltpu.SMEM((6, BLOCK), jnp.float32), pltpu.SemaphoreType.DMA((2,))],
+    )(column, near, held, viewed(far_a))
     cross_late, weight, part = call(
         late_kernel, "late_pairs",
-        [SMEM] * 4 + [VMEM] * 11 + [ANY],
+        [VMEM] * 13 + [ANY],
         [VMEM] * 3,
         [f32(CAP, SLAB_ROWS, LANES), f32(ROWS, LANES), f32(8, LANES)],
-        [whole(), pltpu.VMEM((ROWS, LANES), jnp.float32)]
-        + [acc()] * 7
-        + [pltpu.SemaphoreType.DMA((1,))],
+        [whole()] * 2
+        + [pltpu.SMEM((6, BLOCK), jnp.float32)] * 3
+        + [pltpu.SemaphoreType.DMA((1,)), pltpu.SemaphoreType.DMA((3,))],
     )(
-        intersections, meta_b, tile_blocks, shifts, *tables, near, held, cross_early, *sums,
+        tile_blocks, shifts, column, side_a, side_b, near, held, cross_early, *sums,
         viewed(far_b),
     )
 
     def exchange(value):
         v = over_knot(value)
         me = (v[0] + v[1]) + (v[2] + v[3])
+        third = move(me, swap_c)
         both = jnp.concatenate([me, move(me, swap_a)], axis=0)
-        next_up = move(both, same_d)
-        third = move(me, swap_c)
-        next_up, third = lax.optimization_barrier((next_up, third))
-        return both, next_up, third, move(next_up, swap_a)
+        ahead = move(both, same_d)
+        third, ahead = lax.optimization_barrier((third, ahead))
+        return both, ahead, third, move(ahead, swap_a)
 
     part, state, factor = call(
         step_kernel, "first_step",
-        [SMEM] * 2 + [VMEM] * 11,
+        [VMEM] * 12,
         [VMEM] * 3,
         [f32(8, LANES), f32(8, LANES), f32(4 * BLOCK, LANES)],
-        [pltpu.VMEM((ROWS, LANES), jnp.float32), square(), square()] + [acc()] * 6,
+        [whole(), square(), square()]
+        + [pltpu.SMEM((6, BLOCK), jnp.float32), pltpu.SemaphoreType.DMA((1,))],
     )(
-        intersections, tile_blocks, *exchange(part), *tables, start_coefficients, weight,
+        tile_blocks, *exchange(part), column, side_a, side_b, start_coefficients, weight,
         cross_early, cross_late,
     )
     coef, warped = call(
         final_kernel, "second_step",
-        [SMEM] * 2 + [VMEM] * 6 + [ANY] * 2,
+        [VMEM] * 8 + [ANY] * 2,
         [VMEM, ANY],
         [f32(1, BLOCK), f32(ROWS * DEPTH, LANES)],
         [pltpu.VMEM((ROWS * DEPTH, LANES), jnp.float32)] * 2

time: 93.1 us -> 88.5 us (0.951)
  Pallas kernels: 27.2 us -> 20.4 us
  waiting for transfers between devices: 20.4 us -> 24.6 us
  starting transfers between devices: 39 us -> 37 us
    pallas_call x4, Pallas kernels: 27.2 us -> 20.4 us  [the longest x1 6.18 us: per_device(): call(late_kernel, 'late_pairs', [VMEM] * 13 + [ANY], [VMEM] * 3, [f32(CAP...]
    ppermute x14 -> x12, starting transfers between devices: 24.6 us -> 19.3 us  [move(): return lax.ppermute(value, 'tile', route)]
    ppermute x14 -> x12, waiting for transfers between devices: 13.1 us -> 17.6 us  [move(): return lax.ppermute(value, 'tile', route)]
    unnamed x13 -> x8, local copies, waits for them, and re-layouts: 3.98 us -> 0.34 us
    ppermute x9, starting transfers between devices: 14.5 us -> 17.7 us  [over_knot(): lax.ppermute(value, 'knot', [(i, (i + s) % knots) for i in range(knots)])]
    pad x0 -> x3, local copies, waits for them, and re-layouts: none -> 2.05 us  [the longest x2 2.03 us: per_device(): near, held = (jnp.pad(grad, ends), jnp.pad(image, ends))]
  transfers between devices with their start and end apart: 23 -> 21, of which waited for: 12 -> 13; matrix products, arithmetic and copies ran while one was open for 2% -> 4% of each run, Pallas kernels for 7% -> 6%
where the time goes in v3:
time: 88.5 us; the launch traced here: 87.5 us
  starting transfers between devices  37 us (42%)
  waiting for transfers between devices  24.6 us (28%)
  Pallas kernels  20.4 us (23%)
  local copies, waits for them, and re-layouts  3.34 us (4%)
  between operations  1.44 us (2%)
    ppermute x12, starting transfers between devices, move(): return lax.ppermute(value, 'tile', route)  19.3 us
    ppermute x9, starting transfers between devices, over_knot(): lax.ppermute(value, 'knot', [(i, (i + s) % knots) for i in range(knots)])  17.7 us
    ppermute x12, waiting for transfers between devices, move(): return lax.ppermute(value, 'tile', route)  17.6 us
    ppermute x9, waiting for transfers between devices, over_knot(): lax.ppermute(value, 'knot', [(i, (i + s) % knots) for i in range(knots)])  7.05 us
    pallas_call x1, Pallas kernels, per_device(): call(late_kernel, 'late_pairs', [VMEM] * 13 + [ANY], [VMEM] * 3, [f32(CAP...  6.18 us
    pallas_call x1, Pallas kernels, per_device(): call(step_kernel, 'first_step', [VMEM] * 12, [VMEM] * 3, [f32(8, LANES),...  5.26 us
    pallas_call x1, Pallas kernels, per_device(): call(early_kernel, 'early_pairs', [VMEM] * 3 + [HBM], [VMEM] * 6, [f32(2...  4.87 us
    pallas_call x1, Pallas kernels, per_device(): call(final_kernel, 'second_step', [VMEM] * 8 + [ANY] * 2, [VMEM, ANY], [f...  4.08 us
  transfers between devices with their start and end apart: 21, of which 13 were waited for; matrix products, arithmetic and copies ran while one was open for 4% of the time, Pallas kernels for 6%

profile of v3, /device:TPU:24, one launch (start us, length us, event | category | flops | bytes accessed | tf_op | source)
XLA Modules:
  0.0 87.5 jit_solution(5279652988735493890)
XLA Ops:
  0.7 4.9 %collective-permute-start.6 = (f32[1,8,65536]{2,1,0:T(8,128)}, f32[1,8,65536]{2,1,0:T(8,128)S(1)}, u32[]{:S(2)}, u32[]{:S(2)}) collective-permute-start(f32[1,8,65536]{2,1,0:T(8,128)} %param.7), channel_id=1, source_target_pairs={{4,8},{8,4},{12,16},{16,12},{20,24},{24,20},{28,32},{32,28},{36,40... | collective-permute-start | bytes 6291464 | tf_op jit(solution)/shard_map/ppermute | solution.py:648
  5.7 2.0 %collective-permute-start = (f32[1,64]{1,0:T(1,128)}, f32[1,64]{1,0:T(1,128)S(1)}, u32[]{:S(2)}, u32[]{:S(2)}) collective-permute-start(f32[1,64]{1,0:T(1,128)} %start.1), channel_id=1, source_target_pairs={{0,1},{1,2},{2,3},{3,0},{4,5},{5,6},{6,7},{7,4},{8,9},{9,10},{10,1... | collective-permute-start | bytes 776 | tf_op jit(solution)/shard_map/ppermute | solution.py:652
  7.7 3.6 %collective-permute-start.1 = (f32[1,64]{1,0:T(1,128)}, f32[1,64]{1,0:T(1,128)S(1)}, u32[]{:S(2)}, u32[]{:S(2)}) collective-permute-start(f32[1,64]{1,0:T(1,128)} %start.1), channel_id=1, source_target_pairs={{0,2},{1,3},{2,0},{3,1},{4,6},{5,7},{6,4},{7,5},{8,10},{9,11},{10,... | collective-permute-start | bytes 776 | tf_op jit(solution)/shard_map/ppermute | solution.py:652
  11.2 1.0 %collective-permute-start.2 = (f32[1,64]{1,0:T(1,128)}, f32[1,64]{1,0:T(1,128)S(1)}, u32[]{:S(2)}, u32[]{:S(2)}) collective-permute-start(f32[1,64]{1,0:T(1,128)} %start.1), channel_id=1, source_target_pairs={{0,3},{1,0},{2,1},{3,2},{4,7},{5,4},{6,5},{7,6},{8,11},{9,8},{10,9... | collective-permute-start | bytes 776 | tf_op jit(solution)/shard_map/ppermute | solution.py:652
  12.2 0.7 convert_element_type.19
  13.3 1.7 %collective-permute-done.2 = f32[1,64]{1,0:T(1,128)S(1)} collective-permute-done((f32[1,64]{1,0:T(1,128)}, f32[1,64]{1,0:T(1,128)S(1)}, u32[]{:S(2)}, u32[]{:S(2)}) %collective-permute-start.2) | collective-permute-done | bytes 288 | tf_op jit(solution)/shard_map/ppermute | solution.py:652
  15.7 2.8 %collective-permute-start.4 = (f32[6,64]{1,0:T(8,128)S(1)}, f32[6,64]{1,0:T(8,128)S(1)}, u32[]{:S(2)}, u32[]{:S(2)}) collective-permute-start(f32[6,64]{1,0:T(8,128)S(1)} %concatenate.9.column), channel_id=1, source_target_pairs={{4,8},{8,4},{12,16},{16,12},{20,24},{24,20},{28,32},{32,28},{36,40... | collective-permute-start | bytes 4616 | tf_op jit(solution)/shard_map/ppermute | solution.py:648
  18.5 1.9 %pad.12.near = f32[4352,128]{1,0:T(8,128)S(1)} pad(f32[4096,128]{1,0:T(8,128)} %bitcast.30, f32[]{:T(128)} %constant.2.clone.1), padding=128_128x0_0 | pad | bytes 4325380 | tf_op jit(solution)/shard_map/jit(_pad)/pad | solution.py:665
  21.6 4.9 %early_pairs.1 = (f32[16,72,128]{2,1,0:T(8,128)S(1)}, f32[512,128]{1,0:T(8,128)S(1)}, f32[512,128]{1,0:T(8,128)S(1)}, f32[512,128]{1,0:T(8,128)S(1)}, f32[512,128]{1,0:T(8,128)S(1)}, /*index=5*/f32[512,128]{1,0:T(8,128)S(1)}) custom-call(f32[6,64]{1,0:T(8,128)S(1)} %concatenate.9.column, f32[4352,128]{1,0:T(8,128)S(1)} %pad.12.near, ...), custom_call_target="tpu_custom_call" | custom-call | tf_op jit(solution)/shard_map/early_pairs/pallas_call | solution.py:666
  26.4 4.0 %collective-permute-done.4.side_b = f32[6,64]{1,0:T(8,128)S(1)} collective-permute-done((f32[6,64]{1,0:T(8,128)S(1)}, f32[6,64]{1,0:T(8,128)S(1)}, u32[]{:S(2)}, u32[]{:S(2)}) %collective-permute-start.4) | collective-permute-done | bytes 1568 | tf_op jit(solution)/shard_map/ppermute | solution.py:648
  30.5 6.2 %late_pairs.1 = (f32[8,72,128]{2,1,0:T(8,128)S(1)}, f32[512,128]{1,0:T(8,128)S(1)}, f32[8,128]{1,0:T(8,128)S(1)}) custom-call(s32[1,2]{1,0:T(1,128)S(1)} %copy-done.2, s32[1,1]{1,0:T(1,128)} %bitcast.28.shifts, f32[6,64]{1,0:T(8,128)S(1)} %concatenate.9.column, f32[6,64]{1,0:T(8,128)S(1)} %collective-permute-done.3.side_a, ...), custom_call_target="tpu_custom_call" | custom-call | tf_op jit(solution)/shard_map/late_pairs/pallas_call | solution.py:673
  36.7 2.0 %collective-permute-start.7 = (f32[8,128]{1,0:T(8,128)S(1)}, f32[8,128]{1,0:T(8,128)S(1)}, u32[]{:S(2)}, u32[]{:S(2)}) collective-permute-start(f32[8,128]{1,0:T(8,128)S(1)} %get-tuple-element.26), channel_id=1, source_target_pairs={{0,1},{1,2},{2,3},{3,0},{4,5},{5,6},{6,7},{7,4},{8,9},{9,10},{10,1... | collective-permute-start | bytes 12296 | tf_op jit(solution)/shard_map/ppermute | solution.py:652
  38.6 3.6 %collective-permute-start.8 = (f32[8,128]{1,0:T(8,128)S(1)}, f32[8,128]{1,0:T(8,128)S(1)}, u32[]{:S(2)}, u32[]{:S(2)}) collective-permute-start(f32[8,128]{1,0:T(8,128)S(1)} %get-tuple-element.26), channel_id=1, source_target_pairs={{0,2},{1,3},{2,0},{3,1},{4,6},{5,7},{6,4},{7,5},{8,10},{9,11},{10,... | collective-permute-start | bytes 12296 | tf_op jit(solution)/shard_map/ppermute | solution.py:652
  42.2 1.0 %collective-permute-start.9 = (f32[8,128]{1,0:T(8,128)S(1)}, f32[8,128]{1,0:T(8,128)S(1)}, u32[]{:S(2)}, u32[]{:S(2)}) collective-permute-start(f32[8,128]{1,0:T(8,128)S(1)} %get-tuple-element.26), channel_id=1, source_target_pairs={{0,3},{1,0},{2,1},{3,2},{4,7},{5,4},{6,5},{7,6},{8,11},{9,8},{10,9... | collective-permute-start | bytes 12296 | tf_op jit(solution)/shard_map/ppermute | solution.py:652
  43.9 2.0 %collective-permute-done.9 = f32[8,128]{1,0:T(8,128)S(1)} collective-permute-done((f32[8,128]{1,0:T(8,128)S(1)}, f32[8,128]{1,0:T(8,128)S(1)}, u32[]{:S(2)}, u32[]{:S(2)}) %collective-permute-start.9) | collective-permute-done | bytes 4128 | tf_op jit(solution)/shard_map/ppermute | solution.py:652
  45.8 1.2 %collective-permute-done.10 = f32[8,128]{1,0:T(8,128)S(1)} collective-permute-done((f32[8,128]{1,0:T(8,128)S(1)}, f32[8,128]{1,0:T(8,128)S(1)}, u32[]{:S(2)}, u32[]{:S(2)}) %collective-permute-start.10) | collective-permute-done | bytes 4128 | tf_op jit(solution)/shard_map/ppermute | solution.py:648
  47.0 1.9 %collective-permute-start.12 = (f32[16,128]{1,0:T(8,128)S(1)}, f32[16,128]{1,0:T(8,128)S(1)}, u32[]{:S(2)}, u32[]{:S(2)}) collective-permute-start(f32[16,128]{1,0:T(8,128)S(1)} %pad_maximum_fusion.both), channel_id=1, source_target_pairs={{0,8},{8,16},{12,4},{16,24},{20,12},{24,32},{28,20},{32,40},{36,28... | collective-permute-start | bytes 24584 | tf_op jit(solution)/shard_map/ppermute | solution.py:648
  48.9 1.9 %collective-permute-start.11 = (f32[8,128]{1,0:T(8,128)S(1)}, f32[8,128]{1,0:T(8,128)S(1)}, u32[]{:S(2)}, u32[]{:S(2)}) collective-permute-start(f32[8,128]{1,0:T(8,128)S(1)} %add_add_fusion.1), channel_id=1, source_target_pairs={{4,16},{12,24},{16,4},{20,32},{24,12},{28,40},{32,20},{36,48},{40,... | collective-permute-start | bytes 12296 | tf_op jit(solution)/shard_map/ppermute | solution.py:648
  50.9 5.4 %collective-permute-done.11.third = f32[8,128]{1,0:T(8,128)S(1)} collective-permute-done((f32[8,128]{1,0:T(8,128)S(1)}, f32[8,128]{1,0:T(8,128)S(1)}, u32[]{:S(2)}, u32[]{:S(2)}) %collective-permute-start.11) | collective-permute-done | bytes 4128 | tf_op jit(solution)/shard_map/ppermute | solution.py:648
  56.3 0.9 %collective-permute-start.13 = (f32[16,128]{1,0:T(8,128)S(1)}, f32[16,128]{1,0:T(8,128)S(1)}, u32[]{:S(2)}, u32[]{:S(2)}) collective-permute-start(f32[16,128]{1,0:T(8,128)S(1)} %collective-permute-done.12.ahead), channel_id=1, source_target_pairs={{0,4},{4,0},{8,12},{12,8},{16,20},{20,16},{24,28},{28,24},{32,36},... | collective-permute-start | bytes 24584 | tf_op jit(solution)/shard_map/ppermute | solution.py:648
  57.2 0.8 collective-permute-done.13.behind
  58.0 5.3 %first_step.1 = (f32[8,128]{1,0:T(8,128)S(1)}, f32[8,128]{1,0:T(8,128)S(1)}, f32[256,128]{1,0:T(8,128)S(1)}) custom-call(s32[1,2]{1,0:T(1,128)S(1)} %copy-done.2, f32[16,128]{1,0:T(8,128)S(1)} %pad_maximum_fusion.both, f32[16,128]{1,0:T(8,128)S(1)} %collective-permute-done.12.ahead, f32[8,128]{1,0:T(8,128)S(1)} %collective-permute-done.11.third, ...), custom_call_target="tpu_custom_call" | custom-call | tf_op jit(solution)/shard_map/first_step/pallas_call | solution.py:695
  63.5 3.5 %collective-permute-start.15 = (f32[8,128]{1,0:T(8,128)S(1)}, f32[8,128]{1,0:T(8,128)S(1)}, u32[]{:S(2)}, u32[]{:S(2)}) collective-permute-start(f32[8,128]{1,0:T(8,128)S(1)} %get-tuple-element.31), channel_id=1, source_target_pairs={{0,2},{1,3},{2,0},{3,1},{4,6},{5,7},{6,4},{7,5},{8,10},{9,11},{10,... | collective-permute-start | bytes 12296 | tf_op jit(solution)/shard_map/ppermute | solution.py:652
  67.0 0.8 collective-permute-start.16
  68.6 2.0 %collective-permute-done.16 = f32[8,128]{1,0:T(8,128)S(1)} collective-permute-done((f32[8,128]{1,0:T(8,128)S(1)}, f32[8,128]{1,0:T(8,128)S(1)}, u32[]{:S(2)}, u32[]{:S(2)}) %collective-permute-start.16) | collective-permute-done | bytes 4128 | tf_op jit(solution)/shard_map/ppermute | solution.py:652
  70.6 1.2 %collective-permute-done.17 = f32[8,128]{1,0:T(8,128)S(1)} collective-permute-done((f32[8,128]{1,0:T(8,128)S(1)}, f32[8,128]{1,0:T(8,128)S(1)}, u32[]{:S(2)}, u32[]{:S(2)}) %collective-permute-start.17) | collective-permute-done | bytes 4128 | tf_op jit(solution)/shard_map/ppermute | solution.py:648
  71.8 1.9 %collective-permute-start.19 = (f32[16,128]{1,0:T(8,128)S(1)}, f32[16,128]{1,0:T(8,128)S(1)}, u32[]{:S(2)}, u32[]{:S(2)}) collective-permute-start(f32[16,128]{1,0:T(8,128)S(1)} %pad_maximum_fusion.1.both), channel_id=1, source_target_pairs={{0,8},{8,16},{12,4},{16,24},{20,12},{24,32},{28,20},{32,40},{36,28... | collective-permute-start | bytes 24584 | tf_op jit(solution)/shard_map/ppermute | solution.py:648
  73.7 3.2 %collective-permute-start.18 = (f32[8,128]{1,0:T(8,128)S(1)}, f32[8,128]{1,0:T(8,128)S(1)}, u32[]{:S(2)}, u32[]{:S(2)}) collective-permute-start(f32[8,128]{1,0:T(8,128)S(1)} %add_add_fusion), channel_id=1, source_target_pairs={{4,16},{12,24},{16,4},{20,32},{24,12},{28,40},{32,20},{36,48},{40,... | collective-permute-start | bytes 12296 | tf_op jit(solution)/shard_map/ppermute | solution.py:648
  76.9 4.2 %collective-permute-done.18.third = f32[8,128]{1,0:T(8,128)S(1)} collective-permute-done((f32[8,128]{1,0:T(8,128)S(1)}, f32[8,128]{1,0:T(8,128)S(1)}, u32[]{:S(2)}, u32[]{:S(2)}) %collective-permute-start.18) | collective-permute-done | bytes 4128 | tf_op jit(solution)/shard_map/ppermute | solution.py:648
  81.0 1.5 %collective-permute-start.20 = (f32[16,128]{1,0:T(8,128)S(1)}, f32[16,128]{1,0:T(8,128)S(1)}, u32[]{:S(2)}, u32[]{:S(2)}) collective-permute-start(f32[16,128]{1,0:T(8,128)S(1)} %collective-permute-done.19.ahead), channel_id=1, source_target_pairs={{0,4},{4,0},{8,12},{12,8},{16,20},{20,16},{24,28},{28,24},{32,36},... | collective-permute-start | bytes 24584 | tf_op jit(solution)/shard_map/ppermute | solution.py:648
  82.6 0.8 collective-permute-done.20.behind
  83.4 4.1 %second_step.1 = (f32[1,64]{1,0:T(1,128)}, f32[4096,128]{1,0:T(8,128)}) custom-call(s32[1,2]{1,0:T(1,128)S(1)} %copy-done.2, s32[1,1]{1,0:T(1,128)} %bitcast.29.shifts, f32[16,128]{1,0:T(8,128)S(1)} %pad_maximum_fusion.1.both, f32[16,128]{1,0:T(8,128)S(1)} %collective-permute-done.19.ahead, f32[8,128]{1,0:T(8,128)S(1)} %collective-permute-done.18.third, ...), custom_call_target="tpu_custom_call" | custom-call | tf_op jit(solution)/shard_map/second_step/pallas_call | solution.py:706
  (34 shorter events, 3.4 us)
Async XLA Ops:
  0.6 20.9 %collective-permute-start.5 = (f32[1,8,65536]{2,1,0:T(8,128)}, f32[1,8,65536]{2,1,0:T(8,128)}, u32[]{:S(2)}, u32[]{:S(2)}) collective-permute-start(f32[1,8,65536]{2,1,0:T(8,128)} %param.7), channel_id=1, source_target_pairs={{0,4},{4,0},{8,12},{12,8},{16,20},{20,16},{24,28},{28,24},{32,36},... | collective-permute-start | bytes 6291464 | tf_op jit(solution)/shard_map/ppermute | solution.py:648
  0.7 29.7 %collective-permute-start.6 = (f32[1,8,65536]{2,1,0:T(8,128)}, f32[1,8,65536]{2,1,0:T(8,128)S(1)}, u32[]{:S(2)}, u32[]{:S(2)}) collective-permute-start(f32[1,8,65536]{2,1,0:T(8,128)} %param.7), channel_id=1, source_target_pairs={{4,8},{8,4},{12,16},{16,12},{20,24},{24,20},{28,32},{32,28},{36,40... | collective-permute-start | bytes 6291464 | tf_op jit(solution)/shard_map/ppermute | solution.py:648
  5.7 7.6 %collective-permute-start = (f32[1,64]{1,0:T(1,128)}, f32[1,64]{1,0:T(1,128)S(1)}, u32[]{:S(2)}, u32[]{:S(2)}) collective-permute-start(f32[1,64]{1,0:T(1,128)} %start.1), channel_id=1, source_target_pairs={{0,1},{1,2},{2,3},{3,0},{4,5},{5,6},{6,7},{7,4},{8,9},{9,10},{10,1... | collective-permute-start | bytes 776 | tf_op jit(solution)/shard_map/ppermute | solution.py:652
  7.7 5.6 %collective-permute-start.1 = (f32[1,64]{1,0:T(1,128)}, f32[1,64]{1,0:T(1,128)S(1)}, u32[]{:S(2)}, u32[]{:S(2)}) collective-permute-start(f32[1,64]{1,0:T(1,128)} %start.1), channel_id=1, source_target_pairs={{0,2},{1,3},{2,0},{3,1},{4,6},{5,7},{6,4},{7,5},{8,10},{9,11},{10,... | collective-permute-start | bytes 776 | tf_op jit(solution)/shard_map/ppermute | solution.py:652
  11.2 3.7 %collective-permute-start.2 = (f32[1,64]{1,0:T(1,128)}, f32[1,64]{1,0:T(1,128)S(1)}, u32[]{:S(2)}, u32[]{:S(2)}) collective-permute-start(f32[1,64]{1,0:T(1,128)} %start.1), channel_id=1, source_target_pairs={{0,3},{1,0},{2,1},{3,2},{4,7},{5,4},{6,5},{7,6},{8,11},{9,8},{10,9... | collective-permute-start | bytes 776 | tf_op jit(solution)/shard_map/ppermute | solution.py:652
  15.6 10.8 %collective-permute-start.3 = (f32[6,64]{1,0:T(8,128)S(1)}, f32[6,64]{1,0:T(8,128)S(1)}, u32[]{:S(2)}, u32[]{:S(2)}) collective-permute-start(f32[6,64]{1,0:T(8,128)S(1)} %concatenate.9.column), channel_id=1, source_target_pairs={{0,4},{4,0},{8,12},{12,8},{16,20},{20,16},{24,28},{28,24},{32,36},... | collective-permute-start | bytes 4616 | tf_op jit(solution)/shard_map/ppermute | solution.py:648
  15.7 14.8 %collective-permute-start.4 = (f32[6,64]{1,0:T(8,128)S(1)}, f32[6,64]{1,0:T(8,128)S(1)}, u32[]{:S(2)}, u32[]{:S(2)}) collective-permute-start(f32[6,64]{1,0:T(8,128)S(1)} %concatenate.9.column), channel_id=1, source_target_pairs={{4,8},{8,4},{12,16},{16,12},{20,24},{24,20},{28,32},{32,28},{36,40... | collective-permute-start | bytes 4616 | tf_op jit(solution)/shard_map/ppermute | solution.py:648
  18.5 2.2 %copy-start.1 = (f32[1,8,65536]{2,1,0:T(8,128)S(1)}, f32[1,8,65536]{2,1,0:T(8,128)}, u32[]{:S(2)}) copy-start(f32[1,8,65536]{2,1,0:T(8,128)} %param.6) | copy-start | bytes 6291460
  21.5 8.9 %copy-start.2 = (s32[1,2]{1,0:T(1,128)S(1)}, s32[1,2]{1,0:T(1,128)}, u32[]{:S(2)}) copy-start(s32[1,2]{1,0:T(1,128)} %blocks.5) | copy-start | bytes 28
  30.5 27.5 %copy-start.3 = (f32[1,64]{1,0:T(1,128)S(1)}, f32[1,64]{1,0:T(1,128)}, u32[]{:S(2)}) copy-start(f32[1,64]{1,0:T(1,128)} %start.1) | copy-start | bytes 772
  30.5 52.9 %copy-start = (f32[1,8,65536]{2,1,0:T(8,128)S(1)}, f32[1,8,65536]{2,1,0:T(8,128)}, u32[]{:S(2)}) copy-start(f32[1,8,65536]{2,1,0:T(8,128)} %param.7) | copy-start | bytes 6291460
  36.7 6.6 %collective-permute-start.7 = (f32[8,128]{1,0:T(8,128)S(1)}, f32[8,128]{1,0:T(8,128)S(1)}, u32[]{:S(2)}, u32[]{:S(2)}) collective-permute-start(f32[8,128]{1,0:T(8,128)S(1)} %get-tuple-element.26), channel_id=1, source_target_pairs={{0,1},{1,2},{2,3},{3,0},{4,5},{5,6},{6,7},{7,4},{8,9},{9,10},{10,1... | collective-permute-start | bytes 12296 | tf_op jit(solution)/shard_map/ppermute | solution.py:652
  38.6 5.2 %collective-permute-start.8 = (f32[8,128]{1,0:T(8,128)S(1)}, f32[8,128]{1,0:T(8,128)S(1)}, u32[]{:S(2)}, u32[]{:S(2)}) collective-permute-start(f32[8,128]{1,0:T(8,128)S(1)} %get-tuple-element.26), channel_id=1, source_target_pairs={{0,2},{1,3},{2,0},{3,1},{4,6},{5,7},{6,4},{7,5},{8,10},{9,11},{10,... | collective-permute-start | bytes 12296 | tf_op jit(solution)/shard_map/ppermute | solution.py:652
  42.2 3.6 %collective-permute-start.9 = (f32[8,128]{1,0:T(8,128)S(1)}, f32[8,128]{1,0:T(8,128)S(1)}, u32[]{:S(2)}, u32[]{:S(2)}) collective-permute-start(f32[8,128]{1,0:T(8,128)S(1)} %get-tuple-element.26), channel_id=1, source_target_pairs={{0,3},{1,0},{2,1},{3,2},{4,7},{5,4},{6,5},{7,6},{8,11},{9,8},{10,9... | collective-permute-start | bytes 12296 | tf_op jit(solution)/shard_map/ppermute | solution.py:652
  45.8 1.2 %collective-permute-start.10 = (f32[8,128]{1,0:T(8,128)S(1)}, f32[8,128]{1,0:T(8,128)S(1)}, u32[]{:S(2)}, u32[]{:S(2)}) collective-permute-start(f32[8,128]{1,0:T(8,128)S(1)} %add_add_fusion.1), channel_id=1, source_target_pairs={{0,4},{4,0},{8,12},{12,8},{16,20},{20,16},{24,28},{28,24},{32,36},... | collective-permute-start | bytes 12296 | tf_op jit(solution)/shard_map/ppermute | solution.py:648
  47.0 9.2 %collective-permute-start.12 = (f32[16,128]{1,0:T(8,128)S(1)}, f32[16,128]{1,0:T(8,128)S(1)}, u32[]{:S(2)}, u32[]{:S(2)}) collective-permute-start(f32[16,128]{1,0:T(8,128)S(1)} %pad_maximum_fusion.both), channel_id=1, source_target_pairs={{0,8},{8,16},{12,4},{16,24},{20,12},{24,32},{28,20},{32,40},{36,28... | collective-permute-start | bytes 24584 | tf_op jit(solution)/shard_map/ppermute | solution.py:648
  48.9 7.3 %collective-permute-start.11 = (f32[8,128]{1,0:T(8,128)S(1)}, f32[8,128]{1,0:T(8,128)S(1)}, u32[]{:S(2)}, u32[]{:S(2)}) collective-permute-start(f32[8,128]{1,0:T(8,128)S(1)} %add_add_fusion.1), channel_id=1, source_target_pairs={{4,16},{12,24},{16,4},{20,32},{24,12},{28,40},{32,20},{36,48},{40,... | collective-permute-start | bytes 12296 | tf_op jit(solution)/shard_map/ppermute | solution.py:648
  56.3 1.7 %collective-permute-start.13 = (f32[16,128]{1,0:T(8,128)S(1)}, f32[16,128]{1,0:T(8,128)S(1)}, u32[]{:S(2)}, u32[]{:S(2)}) collective-permute-start(f32[16,128]{1,0:T(8,128)S(1)} %collective-permute-done.12.ahead), channel_id=1, source_target_pairs={{0,4},{4,0},{8,12},{12,8},{16,20},{20,16},{24,28},{28,24},{32,36},... | collective-permute-start | bytes 24584 | tf_op jit(solution)/shard_map/ppermute | solution.py:648
  63.3 4.9 %collective-permute-start.14 = (f32[8,128]{1,0:T(8,128)S(1)}, f32[8,128]{1,0:T(8,128)S(1)}, u32[]{:S(2)}, u32[]{:S(2)}) collective-permute-start(f32[8,128]{1,0:T(8,128)S(1)} %get-tuple-element.31), channel_id=1, source_target_pairs={{0,1},{1,2},{2,3},{3,0},{4,5},{5,6},{6,7},{7,4},{8,9},{9,10},{10,1... | collective-permute-start | bytes 12296 | tf_op jit(solution)/shard_map/ppermute | solution.py:652
  63.5 5.1 %collective-permute-start.15 = (f32[8,128]{1,0:T(8,128)S(1)}, f32[8,128]{1,0:T(8,128)S(1)}, u32[]{:S(2)}, u32[]{:S(2)}) collective-permute-start(f32[8,128]{1,0:T(8,128)S(1)} %get-tuple-element.31), channel_id=1, source_target_pairs={{0,2},{1,3},{2,0},{3,1},{4,6},{5,7},{6,4},{7,5},{8,10},{9,11},{10,... | collective-permute-start | bytes 12296 | tf_op jit(solution)/shard_map/ppermute | solution.py:652
  67.0 3.6 %collective-permute-start.16 = (f32[8,128]{1,0:T(8,128)S(1)}, f32[8,128]{1,0:T(8,128)S(1)}, u32[]{:S(2)}, u32[]{:S(2)}) collective-permute-start(f32[8,128]{1,0:T(8,128)S(1)} %get-tuple-element.31), channel_id=1, source_target_pairs={{0,3},{1,0},{2,1},{3,2},{4,7},{5,4},{6,5},{7,6},{8,11},{9,8},{10,9... | collective-permute-start | bytes 12296 | tf_op jit(solution)/shard_map/ppermute | solution.py:652
  70.6 1.2 %collective-permute-start.17 = (f32[8,128]{1,0:T(8,128)S(1)}, f32[8,128]{1,0:T(8,128)S(1)}, u32[]{:S(2)}, u32[]{:S(2)}) collective-permute-start(f32[8,128]{1,0:T(8,128)S(1)} %add_add_fusion), channel_id=1, source_target_pairs={{0,4},{4,0},{8,12},{12,8},{16,20},{20,16},{24,28},{28,24},{32,36},... | collective-permute-start | bytes 12296 | tf_op jit(solution)/shard_map/ppermute | solution.py:648
  71.8 9.2 %collective-permute-start.19 = (f32[16,128]{1,0:T(8,128)S(1)}, f32[16,128]{1,0:T(8,128)S(1)}, u32[]{:S(2)}, u32[]{:S(2)}) collective-permute-start(f32[16,128]{1,0:T(8,128)S(1)} %pad_maximum_fusion.1.both), channel_id=1, source_target_pairs={{0,8},{8,16},{12,4},{16,24},{20,12},{24,32},{28,20},{32,40},{36,28... | collective-permute-start | bytes 24584 | tf_op jit(solution)/shard_map/ppermute | solution.py:648
  73.7 7.3 %collective-permute-start.18 = (f32[8,128]{1,0:T(8,128)S(1)}, f32[8,128]{1,0:T(8,128)S(1)}, u32[]{:S(2)}, u32[]{:S(2)}) collective-permute-start(f32[8,128]{1,0:T(8,128)S(1)} %add_add_fusion), channel_id=1, source_target_pairs={{4,16},{12,24},{16,4},{20,32},{24,12},{28,40},{32,20},{36,48},{40,... | collective-permute-start | bytes 12296 | tf_op jit(solution)/shard_map/ppermute | solution.py:648
  81.0 2.3 %collective-permute-start.20 = (f32[16,128]{1,0:T(8,128)S(1)}, f32[16,128]{1,0:T(8,128)S(1)}, u32[]{:S(2)}, u32[]{:S(2)}) collective-permute-start(f32[16,128]{1,0:T(8,128)S(1)} %collective-permute-done.19.ahead), channel_id=1, source_target_pairs={{0,4},{4,0},{8,12},{12,8},{16,20},{20,16},{24,28},{28,24},{32,36},... | collective-permute-start | bytes 24584 | tf_op jit(solution)/shard_map/ppermute | solution.py:648

commit v4 on v3

--- a/solution.py
+++ b/solution.py
@@ -414,7 +414,7 @@
     me, a = both[0:8, :], both[8:16, :]
     d, b = ahead[0:8, :], ahead[8:16, :]
     sd, sb = behind[0:8, :], behind[8:16, :]
-    c = third[...]
+    c = third[0:8, :]
     return [
         (me, me[0:1] + a[1:2] + b[2:3]),
         (a, a[0:1] + me[1:2] + sb[2:3]),
@@ -686,7 +686,7 @@
     def exchange(value):
         v = over_knot(value)
         me = (v[0] + v[1]) + (v[2] + v[3])
-        third = move(me, swap_c)
+        third = move(jnp.pad(me, ((0, 24), (0, 0))), swap_c)
         both = jnp.concatenate([me, move(me, swap_a)], axis=0)
         ahead = move(both, same_d)
         third, ahead = lax.optimization_barrier((third, ahead))

time: 88.5 us -> 86.5 us (0.977)
  starting transfers between devices: 37 us -> 35.3 us
    ppermute x12, starting transfers between devices: 19.3 us -> 17.8 us  [move(): return lax.ppermute(value, 'tile', route)]
  transfers between devices with their start and end apart: 21 -> 21, of which waited for: 13 -> 11; matrix products, arithmetic and copies ran while one was open for 4% -> 4% of each run, Pallas kernels for 6% -> 6%
where the time goes in v4:
time: 86.5 us; the launch traced here: 86 us
  starting transfers between devices  35.3 us (41%)
  waiting for transfers between devices  24.1 us (28%)
  Pallas kernels  21.1 us (24%)
  local copies, waits for them, and re-layouts  3.35 us (4%)
  between operations  1.5 us (2%)
    ppermute x12, starting transfers between devices, move(): return lax.ppermute(value, 'tile', route)  17.8 us
    ppermute x9, starting transfers between devices, over_knot(): lax.ppermute(value, 'knot', [(i, (i + s) % knots) for i in range(knots)])  17.4 us
    ppermute x12, waiting for transfers between devices, move(): return lax.ppermute(value, 'tile', route)  16.8 us
    ppermute x9, waiting for transfers between devices, over_knot(): lax.ppermute(value, 'knot', [(i, (i + s) % knots) for i in range(knots)])  7.32 us
    pallas_call x1, Pallas kernels, per_device(): call(late_kernel, 'late_pairs', [VMEM] * 13 + [ANY], [VMEM] * 3, [f32(CAP...  6.42 us
    pallas_call x1, Pallas kernels, per_device(): call(early_kernel, 'early_pairs', [VMEM] * 3 + [HBM], [VMEM] * 6, [f32(2...  5.34 us
    pallas_call x1, Pallas kernels, per_device(): call(step_kernel, 'first_step', [VMEM] * 12, [VMEM] * 3, [f32(8, LANES),...  5.26 us
    pallas_call x1, Pallas kernels, per_device(): call(final_kernel, 'second_step', [VMEM] * 8 + [ANY] * 2, [VMEM, ANY], [f...  4.08 us
  transfers between devices with their start and end apart: 21, of which 11 were waited for; matrix products, arithmetic and copies ran while one was open for 4% of the time, Pallas kernels for 6%

profile of v4, /device:TPU:24, one launch (start us, length us, event | category | flops | bytes accessed | tf_op | source)
XLA Modules:
  0.0 86.0 jit_solution(4308497331722710281)
XLA Ops:
  0.7 4.9 %collective-permute-start.6 = (f32[1,8,65536]{2,1,0:T(8,128)}, f32[1,8,65536]{2,1,0:T(8,128)S(1)}, u32[]{:S(2)}, u32[]{:S(2)}) collective-permute-start(f32[1,8,65536]{2,1,0:T(8,128)} %param.7), channel_id=1, source_target_pairs={{4,8},{8,4},{12,16},{16,12},{20,24},{24,20},{28,32},{32,28},{36,40... | collective-permute-start | bytes 6291464 | tf_op jit(solution)/shard_map/ppermute | solution.py:648
  5.7 2.0 %collective-permute-start = (f32[1,64]{1,0:T(1,128)}, f32[1,64]{1,0:T(1,128)S(1)}, u32[]{:S(2)}, u32[]{:S(2)}) collective-permute-start(f32[1,64]{1,0:T(1,128)} %start.1), channel_id=1, source_target_pairs={{0,1},{1,2},{2,3},{3,0},{4,5},{5,6},{6,7},{7,4},{8,9},{9,10},{10,1... | collective-permute-start | bytes 776 | tf_op jit(solution)/shard_map/ppermute | solution.py:652
  7.7 3.6 %collective-permute-start.1 = (f32[1,64]{1,0:T(1,128)}, f32[1,64]{1,0:T(1,128)S(1)}, u32[]{:S(2)}, u32[]{:S(2)}) collective-permute-start(f32[1,64]{1,0:T(1,128)} %start.1), channel_id=1, source_target_pairs={{0,2},{1,3},{2,0},{3,1},{4,6},{5,7},{6,4},{7,5},{8,10},{9,11},{10,... | collective-permute-start | bytes 776 | tf_op jit(solution)/shard_map/ppermute | solution.py:652
  11.2 1.0 %collective-permute-start.2 = (f32[1,64]{1,0:T(1,128)}, f32[1,64]{1,0:T(1,128)S(1)}, u32[]{:S(2)}, u32[]{:S(2)}) collective-permute-start(f32[1,64]{1,0:T(1,128)} %start.1), channel_id=1, source_target_pairs={{0,3},{1,0},{2,1},{3,2},{4,7},{5,4},{6,5},{7,6},{8,11},{9,8},{10,9... | collective-permute-start | bytes 776 | tf_op jit(solution)/shard_map/ppermute | solution.py:652
  12.2 0.7 convert_element_type.22
  13.3 1.7 %collective-permute-done.2 = f32[1,64]{1,0:T(1,128)S(1)} collective-permute-done((f32[1,64]{1,0:T(1,128)}, f32[1,64]{1,0:T(1,128)S(1)}, u32[]{:S(2)}, u32[]{:S(2)}) %collective-permute-start.2) | collective-permute-done | bytes 288 | tf_op jit(solution)/shard_map/ppermute | solution.py:652
  14.9 0.7 concatenate.9.column
  15.7 2.8 %collective-permute-start.4 = (f32[6,64]{1,0:T(8,128)S(1)}, f32[6,64]{1,0:T(8,128)S(1)}, u32[]{:S(2)}, u32[]{:S(2)}) collective-permute-start(f32[6,64]{1,0:T(8,128)S(1)} %concatenate.9.column), channel_id=1, source_target_pairs={{4,8},{8,4},{12,16},{16,12},{20,24},{24,20},{28,32},{32,28},{36,40... | collective-permute-start | bytes 4616 | tf_op jit(solution)/shard_map/ppermute | solution.py:648
  18.5 1.9 %pad.19.near = f32[4352,128]{1,0:T(8,128)S(1)} pad(f32[4096,128]{1,0:T(8,128)} %bitcast.30, f32[]{:T(128)} %constant.2.clone.1), padding=128_128x0_0 | pad | bytes 4325380 | tf_op jit(solution)/shard_map/jit(_pad)/pad | solution.py:665
  21.6 5.3 %early_pairs.1 = (f32[16,72,128]{2,1,0:T(8,128)S(1)}, f32[512,128]{1,0:T(8,128)S(1)}, f32[512,128]{1,0:T(8,128)S(1)}, f32[512,128]{1,0:T(8,128)S(1)}, f32[512,128]{1,0:T(8,128)S(1)}, /*index=5*/f32[512,128]{1,0:T(8,128)S(1)}) custom-call(f32[6,64]{1,0:T(8,128)S(1)} %concatenate.9.column, f32[4352,128]{1,0:T(8,128)S(1)} %pad.19.near, ...), custom_call_target="tpu_custom_call" | custom-call | tf_op jit(solution)/shard_map/early_pairs/pallas_call | solution.py:666
  26.9 3.5 %collective-permute-done.4.side_b = f32[6,64]{1,0:T(8,128)S(1)} collective-permute-done((f32[6,64]{1,0:T(8,128)S(1)}, f32[6,64]{1,0:T(8,128)S(1)}, u32[]{:S(2)}, u32[]{:S(2)}) %collective-permute-start.4) | collective-permute-done | bytes 1568 | tf_op jit(solution)/shard_map/ppermute | solution.py:648
  30.5 6.4 %late_pairs.1 = (f32[8,72,128]{2,1,0:T(8,128)S(1)}, f32[512,128]{1,0:T(8,128)S(1)}, f32[8,128]{1,0:T(8,128)S(1)}) custom-call(s32[1,2]{1,0:T(1,128)S(1)} %copy-done.2, s32[1,1]{1,0:T(1,128)} %bitcast.28.shifts, f32[6,64]{1,0:T(8,128)S(1)} %concatenate.9.column, f32[6,64]{1,0:T(8,128)S(1)} %collective-permute-done.3.side_a, ...), custom_call_target="tpu_custom_call" | custom-call | tf_op jit(solution)/shard_map/late_pairs/pallas_call | solution.py:673
  36.9 2.0 %collective-permute-start.7 = (f32[8,128]{1,0:T(8,128)S(1)}, f32[8,128]{1,0:T(8,128)S(1)}, u32[]{:S(2)}, u32[]{:S(2)}) collective-permute-start(f32[8,128]{1,0:T(8,128)S(1)} %get-tuple-element.26), channel_id=1, source_target_pairs={{0,1},{1,2},{2,3},{3,0},{4,5},{5,6},{6,7},{7,4},{8,9},{9,10},{10,1... | collective-permute-start | bytes 12296 | tf_op jit(solution)/shard_map/ppermute | solution.py:652
  38.9 3.6 %collective-permute-start.8 = (f32[8,128]{1,0:T(8,128)S(1)}, f32[8,128]{1,0:T(8,128)S(1)}, u32[]{:S(2)}, u32[]{:S(2)}) collective-permute-start(f32[8,128]{1,0:T(8,128)S(1)} %get-tuple-element.26), channel_id=1, source_target_pairs={{0,2},{1,3},{2,0},{3,1},{4,6},{5,7},{6,4},{7,5},{8,10},{9,11},{10,... | collective-permute-start | bytes 12296 | tf_op jit(solution)/shard_map/ppermute | solution.py:652
  42.5 1.0 %collective-permute-start.9 = (f32[8,128]{1,0:T(8,128)S(1)}, f32[8,128]{1,0:T(8,128)S(1)}, u32[]{:S(2)}, u32[]{:S(2)}) collective-permute-start(f32[8,128]{1,0:T(8,128)S(1)} %get-tuple-element.26), channel_id=1, source_target_pairs={{0,3},{1,0},{2,1},{3,2},{4,7},{5,4},{6,5},{7,6},{8,11},{9,8},{10,9... | collective-permute-start | bytes 12296 | tf_op jit(solution)/shard_map/ppermute | solution.py:652
  43.5 0.6 collective-permute-done.8
  44.1 2.0 %collective-permute-done.9 = f32[8,128]{1,0:T(8,128)S(1)} collective-permute-done((f32[8,128]{1,0:T(8,128)S(1)}, f32[8,128]{1,0:T(8,128)S(1)}, u32[]{:S(2)}, u32[]{:S(2)}) %collective-permute-start.9) | collective-permute-done | bytes 4128 | tf_op jit(solution)/shard_map/ppermute | solution.py:652
  46.1 1.9 %collective-permute-start.11 = (f32[32,128]{1,0:T(8,128)S(1)}, f32[32,128]{1,0:T(8,128)S(1)}, u32[]{:S(2)}, u32[]{:S(2)}) collective-permute-start(f32[32,128]{1,0:T(8,128)S(1)} %pad.21), channel_id=1, source_target_pairs={{4,16},{12,24},{16,4},{20,32},{24,12},{28,40},{32,20},{36,48},{40,... | collective-permute-start | bytes 49160 | tf_op jit(solution)/shard_map/ppermute | solution.py:648
  48.0 2.3 %collective-permute-start.12 = (f32[16,128]{1,0:T(8,128)S(1)}, f32[16,128]{1,0:T(8,128)S(1)}, u32[]{:S(2)}, u32[]{:S(2)}) collective-permute-start(f32[16,128]{1,0:T(8,128)S(1)} %pad_maximum_fusion.both), channel_id=1, source_target_pairs={{0,8},{8,16},{12,4},{16,24},{20,12},{24,32},{28,20},{32,40},{36,28... | collective-permute-start | bytes 24584 | tf_op jit(solution)/shard_map/ppermute | solution.py:648
  50.3 5.4 %collective-permute-done.12.ahead = f32[16,128]{1,0:T(8,128)S(1)} collective-permute-done((f32[16,128]{1,0:T(8,128)S(1)}, f32[16,128]{1,0:T(8,128)S(1)}, u32[]{:S(2)}, u32[]{:S(2)}) %collective-permute-start.12) | collective-permute-done | bytes 8224 | tf_op jit(solution)/shard_map/ppermute | solution.py:648
  55.7 1.2 %collective-permute-done.13.behind = f32[16,128]{1,0:T(8,128)S(1)} collective-permute-done((f32[16,128]{1,0:T(8,128)S(1)}, f32[16,128]{1,0:T(8,128)S(1)}, u32[]{:S(2)}, u32[]{:S(2)}) %collective-permute-start.13) | collective-permute-done | bytes 8224 | tf_op jit(solution)/shard_map/ppermute | solution.py:648
  56.9 5.3 %first_step.1 = (f32[8,128]{1,0:T(8,128)S(1)}, f32[8,128]{1,0:T(8,128)S(1)}, f32[256,128]{1,0:T(8,128)S(1)}) custom-call(s32[1,2]{1,0:T(1,128)S(1)} %copy-done.2, f32[16,128]{1,0:T(8,128)S(1)} %pad_maximum_fusion.both, f32[16,128]{1,0:T(8,128)S(1)} %collective-permute-done.12.ahead, f32[32,128]{1,0:T(8,128)S(1)} %collective-permute-done.11.third, ...), custom_call_target="tpu_custom_call" | custom-call | tf_op jit(solution)/shard_map/first_step/pallas_call | solution.py:695
  62.2 3.7 %collective-permute-start.15 = (f32[8,128]{1,0:T(8,128)S(1)}, f32[8,128]{1,0:T(8,128)S(1)}, u32[]{:S(2)}, u32[]{:S(2)}) collective-permute-start(f32[8,128]{1,0:T(8,128)S(1)} %get-tuple-element.31), channel_id=1, source_target_pairs={{0,2},{1,3},{2,0},{3,1},{4,6},{5,7},{6,4},{7,5},{8,10},{9,11},{10,... | collective-permute-start | bytes 12296 | tf_op jit(solution)/shard_map/ppermute | solution.py:652
  65.9 0.5 collective-permute-start.16
  66.4 0.6 collective-permute-done.14
  67.0 0.5 collective-permute-done.15
  67.5 2.0 %collective-permute-done.16 = f32[8,128]{1,0:T(8,128)S(1)} collective-permute-done((f32[8,128]{1,0:T(8,128)S(1)}, f32[8,128]{1,0:T(8,128)S(1)}, u32[]{:S(2)}, u32[]{:S(2)}) %collective-permute-start.16) | collective-permute-done | bytes 4128 | tf_op jit(solution)/shard_map/ppermute | solution.py:652
  69.5 3.5 %collective-permute-start.18 = (f32[32,128]{1,0:T(8,128)S(1)}, f32[32,128]{1,0:T(8,128)S(1)}, u32[]{:S(2)}, u32[]{:S(2)}) collective-permute-start(f32[32,128]{1,0:T(8,128)S(1)} %pad.22), channel_id=1, source_target_pairs={{4,16},{12,24},{16,4},{20,32},{24,12},{28,40},{32,20},{36,48},{40,... | collective-permute-start | bytes 49160 | tf_op jit(solution)/shard_map/ppermute | solution.py:648
  73.1 2.2 %collective-permute-start.19 = (f32[16,128]{1,0:T(8,128)S(1)}, f32[16,128]{1,0:T(8,128)S(1)}, u32[]{:S(2)}, u32[]{:S(2)}) collective-permute-start(f32[16,128]{1,0:T(8,128)S(1)} %pad_maximum_fusion.1.both), channel_id=1, source_target_pairs={{0,8},{8,16},{12,4},{16,24},{20,12},{24,32},{28,20},{32,40},{36,28... | collective-permute-start | bytes 24584 | tf_op jit(solution)/shard_map/ppermute | solution.py:648
  75.3 5.5 %collective-permute-done.19.ahead = f32[16,128]{1,0:T(8,128)S(1)} collective-permute-done((f32[16,128]{1,0:T(8,128)S(1)}, f32[16,128]{1,0:T(8,128)S(1)}, u32[]{:S(2)}, u32[]{:S(2)}) %collective-permute-start.19) | collective-permute-done | bytes 8224 | tf_op jit(solution)/shard_map/ppermute | solution.py:648
  80.8 1.2 %collective-permute-done.20.behind = f32[16,128]{1,0:T(8,128)S(1)} collective-permute-done((f32[16,128]{1,0:T(8,128)S(1)}, f32[16,128]{1,0:T(8,128)S(1)}, u32[]{:S(2)}, u32[]{:S(2)}) %collective-permute-start.20) | collective-permute-done | bytes 8224 | tf_op jit(solution)/shard_map/ppermute | solution.py:648
  81.9 4.1 %second_step.1 = (f32[1,64]{1,0:T(1,128)}, f32[4096,128]{1,0:T(8,128)}) custom-call(s32[1,2]{1,0:T(1,128)S(1)} %copy-done.2, s32[1,1]{1,0:T(1,128)} %bitcast.29.shifts, f32[16,128]{1,0:T(8,128)S(1)} %pad_maximum_fusion.1.both, f32[16,128]{1,0:T(8,128)S(1)} %collective-permute-done.19.ahead, f32[32,128]{1,0:T(8,128)S(1)} %collective-permute-done.18.third, ...), custom_call_target="tpu_custom_call" | custom-call | tf_op jit(solution)/shard_map/second_step/pallas_call | solution.py:706
  (36 shorter events, 1.1 us)
Async XLA Ops:
  0.6 20.9 %collective-permute-start.5 = (f32[1,8,65536]{2,1,0:T(8,128)}, f32[1,8,65536]{2,1,0:T(8,128)}, u32[]{:S(2)}, u32[]{:S(2)}) collective-permute-start(f32[1,8,65536]{2,1,0:T(8,128)} %param.7), channel_id=1, source_target_pairs={{0,4},{4,0},{8,12},{12,8},{16,20},{20,16},{24,28},{28,24},{32,36},... | collective-permute-start | bytes 6291464 | tf_op jit(solution)/shard_map/ppermute | solution.py:648
  0.7 29.7 %collective-permute-start.6 = (f32[1,8,65536]{2,1,0:T(8,128)}, f32[1,8,65536]{2,1,0:T(8,128)S(1)}, u32[]{:S(2)}, u32[]{:S(2)}) collective-permute-start(f32[1,8,65536]{2,1,0:T(8,128)} %param.7), channel_id=1, source_target_pairs={{4,8},{8,4},{12,16},{16,12},{20,24},{24,20},{28,32},{32,28},{36,40... | collective-permute-start | bytes 6291464 | tf_op jit(solution)/shard_map/ppermute | solution.py:648
  5.7 7.6 %collective-permute-start = (f32[1,64]{1,0:T(1,128)}, f32[1,64]{1,0:T(1,128)S(1)}, u32[]{:S(2)}, u32[]{:S(2)}) collective-permute-start(f32[1,64]{1,0:T(1,128)} %start.1), channel_id=1, source_target_pairs={{0,1},{1,2},{2,3},{3,0},{4,5},{5,6},{6,7},{7,4},{8,9},{9,10},{10,1... | collective-permute-start | bytes 776 | tf_op jit(solution)/shard_map/ppermute | solution.py:652
  7.7 5.6 %collective-permute-start.1 = (f32[1,64]{1,0:T(1,128)}, f32[1,64]{1,0:T(1,128)S(1)}, u32[]{:S(2)}, u32[]{:S(2)}) collective-permute-start(f32[1,64]{1,0:T(1,128)} %start.1), channel_id=1, source_target_pairs={{0,2},{1,3},{2,0},{3,1},{4,6},{5,7},{6,4},{7,5},{8,10},{9,11},{10,... | collective-permute-start | bytes 776 | tf_op jit(solution)/shard_map/ppermute | solution.py:652
  11.2 3.7 %collective-permute-start.2 = (f32[1,64]{1,0:T(1,128)}, f32[1,64]{1,0:T(1,128)S(1)}, u32[]{:S(2)}, u32[]{:S(2)}) collective-permute-start(f32[1,64]{1,0:T(1,128)} %start.1), channel_id=1, source_target_pairs={{0,3},{1,0},{2,1},{3,2},{4,7},{5,4},{6,5},{7,6},{8,11},{9,8},{10,9... | collective-permute-start | bytes 776 | tf_op jit(solution)/shard_map/ppermute | solution.py:652
  15.6 11.3 %collective-permute-start.3 = (f32[6,64]{1,0:T(8,128)S(1)}, f32[6,64]{1,0:T(8,128)S(1)}, u32[]{:S(2)}, u32[]{:S(2)}) collective-permute-start(f32[6,64]{1,0:T(8,128)S(1)} %concatenate.9.column), channel_id=1, source_target_pairs={{0,4},{4,0},{8,12},{12,8},{16,20},{20,16},{24,28},{28,24},{32,36},... | collective-permute-start | bytes 4616 | tf_op jit(solution)/shard_map/ppermute | solution.py:648
  15.7 14.8 %collective-permute-start.4 = (f32[6,64]{1,0:T(8,128)S(1)}, f32[6,64]{1,0:T(8,128)S(1)}, u32[]{:S(2)}, u32[]{:S(2)}) collective-permute-start(f32[6,64]{1,0:T(8,128)S(1)} %concatenate.9.column), channel_id=1, source_target_pairs={{4,8},{8,4},{12,16},{16,12},{20,24},{24,20},{28,32},{32,28},{36,40... | collective-permute-start | bytes 4616 | tf_op jit(solution)/shard_map/ppermute | solution.py:648
  18.5 2.2 %copy-start.1 = (f32[1,8,65536]{2,1,0:T(8,128)S(1)}, f32[1,8,65536]{2,1,0:T(8,128)}, u32[]{:S(2)}) copy-start(f32[1,8,65536]{2,1,0:T(8,128)} %param.6) | copy-start | bytes 6291460
  21.5 8.9 %copy-start.2 = (s32[1,2]{1,0:T(1,128)S(1)}, s32[1,2]{1,0:T(1,128)}, u32[]{:S(2)}) copy-start(s32[1,2]{1,0:T(1,128)} %blocks.5) | copy-start | bytes 28
  30.5 26.4 %copy-start.3 = (f32[1,64]{1,0:T(1,128)S(1)}, f32[1,64]{1,0:T(1,128)}, u32[]{:S(2)}) copy-start(f32[1,64]{1,0:T(1,128)} %start.1) | copy-start | bytes 772
  30.5 51.5 %copy-start = (f32[1,8,65536]{2,1,0:T(8,128)S(1)}, f32[1,8,65536]{2,1,0:T(8,128)}, u32[]{:S(2)}) copy-start(f32[1,8,65536]{2,1,0:T(8,128)} %param.7) | copy-start | bytes 6291460
  36.9 6.6 %collective-permute-start.7 = (f32[8,128]{1,0:T(8,128)S(1)}, f32[8,128]{1,0:T(8,128)S(1)}, u32[]{:S(2)}, u32[]{:S(2)}) collective-permute-start(f32[8,128]{1,0:T(8,128)S(1)} %get-tuple-element.26), channel_id=1, source_target_pairs={{0,1},{1,2},{2,3},{3,0},{4,5},{5,6},{6,7},{7,4},{8,9},{9,10},{10,1... | collective-permute-start | bytes 12296 | tf_op jit(solution)/shard_map/ppermute | solution.py:652
  38.9 5.2 %collective-permute-start.8 = (f32[8,128]{1,0:T(8,128)S(1)}, f32[8,128]{1,0:T(8,128)S(1)}, u32[]{:S(2)}, u32[]{:S(2)}) collective-permute-start(f32[8,128]{1,0:T(8,128)S(1)} %get-tuple-element.26), channel_id=1, source_target_pairs={{0,2},{1,3},{2,0},{3,1},{4,6},{5,7},{6,4},{7,5},{8,10},{9,11},{10,... | collective-permute-start | bytes 12296 | tf_op jit(solution)/shard_map/ppermute | solution.py:652
  42.5 3.6 %collective-permute-start.9 = (f32[8,128]{1,0:T(8,128)S(1)}, f32[8,128]{1,0:T(8,128)S(1)}, u32[]{:S(2)}, u32[]{:S(2)}) collective-permute-start(f32[8,128]{1,0:T(8,128)S(1)} %get-tuple-element.26), channel_id=1, source_target_pairs={{0,3},{1,0},{2,1},{3,2},{4,7},{5,4},{6,5},{7,6},{8,11},{9,8},{10,9... | collective-permute-start | bytes 12296 | tf_op jit(solution)/shard_map/ppermute | solution.py:652
  46.1 1.9 %collective-permute-start.10 = (f32[8,128]{1,0:T(8,128)S(1)}, f32[8,128]{1,0:T(8,128)S(1)}, u32[]{:S(2)}, u32[]{:S(2)}) collective-permute-start(f32[8,128]{1,0:T(8,128)S(1)} %add_add_fusion.1), channel_id=1, source_target_pairs={{0,4},{4,0},{8,12},{12,8},{16,20},{20,16},{24,28},{28,24},{32,36},... | collective-permute-start | bytes 12296 | tf_op jit(solution)/shard_map/ppermute | solution.py:648
  46.1 9.6 %collective-permute-start.11 = (f32[32,128]{1,0:T(8,128)S(1)}, f32[32,128]{1,0:T(8,128)S(1)}, u32[]{:S(2)}, u32[]{:S(2)}) collective-permute-start(f32[32,128]{1,0:T(8,128)S(1)} %pad.21), channel_id=1, source_target_pairs={{4,16},{12,24},{16,4},{20,32},{24,12},{28,40},{32,20},{36,48},{40,... | collective-permute-start | bytes 49160 | tf_op jit(solution)/shard_map/ppermute | solution.py:648
  48.0 7.7 %collective-permute-start.12 = (f32[16,128]{1,0:T(8,128)S(1)}, f32[16,128]{1,0:T(8,128)S(1)}, u32[]{:S(2)}, u32[]{:S(2)}) collective-permute-start(f32[16,128]{1,0:T(8,128)S(1)} %pad_maximum_fusion.both), channel_id=1, source_target_pairs={{0,8},{8,16},{12,4},{16,24},{20,12},{24,32},{28,20},{32,40},{36,28... | collective-permute-start | bytes 24584 | tf_op jit(solution)/shard_map/ppermute | solution.py:648
  55.7 1.2 %collective-permute-start.13 = (f32[16,128]{1,0:T(8,128)S(1)}, f32[16,128]{1,0:T(8,128)S(1)}, u32[]{:S(2)}, u32[]{:S(2)}) collective-permute-start(f32[16,128]{1,0:T(8,128)S(1)} %collective-permute-done.12.ahead), channel_id=1, source_target_pairs={{0,4},{4,0},{8,12},{12,8},{16,20},{20,16},{24,28},{28,24},{32,36},... | collective-permute-start | bytes 24584 | tf_op jit(solution)/shard_map/ppermute | solution.py:648
  62.1 4.9 %collective-permute-start.14 = (f32[8,128]{1,0:T(8,128)S(1)}, f32[8,128]{1,0:T(8,128)S(1)}, u32[]{:S(2)}, u32[]{:S(2)}) collective-permute-start(f32[8,128]{1,0:T(8,128)S(1)} %get-tuple-element.31), channel_id=1, source_target_pairs={{0,1},{1,2},{2,3},{3,0},{4,5},{5,6},{6,7},{7,4},{8,9},{9,10},{10,1... | collective-permute-start | bytes 12296 | tf_op jit(solution)/shard_map/ppermute | solution.py:652
  62.2 5.3 %collective-permute-start.15 = (f32[8,128]{1,0:T(8,128)S(1)}, f32[8,128]{1,0:T(8,128)S(1)}, u32[]{:S(2)}, u32[]{:S(2)}) collective-permute-start(f32[8,128]{1,0:T(8,128)S(1)} %get-tuple-element.31), channel_id=1, source_target_pairs={{0,2},{1,3},{2,0},{3,1},{4,6},{5,7},{6,4},{7,5},{8,10},{9,11},{10,... | collective-permute-start | bytes 12296 | tf_op jit(solution)/shard_map/ppermute | solution.py:652
  65.9 3.6 %collective-permute-start.16 = (f32[8,128]{1,0:T(8,128)S(1)}, f32[8,128]{1,0:T(8,128)S(1)}, u32[]{:S(2)}, u32[]{:S(2)}) collective-permute-start(f32[8,128]{1,0:T(8,128)S(1)} %get-tuple-element.31), channel_id=1, source_target_pairs={{0,3},{1,0},{2,1},{3,2},{4,7},{5,4},{6,5},{7,6},{8,11},{9,8},{10,9... | collective-permute-start | bytes 12296 | tf_op jit(solution)/shard_map/ppermute | solution.py:652
  69.5 3.6 %collective-permute-start.17 = (f32[8,128]{1,0:T(8,128)S(1)}, f32[8,128]{1,0:T(8,128)S(1)}, u32[]{:S(2)}, u32[]{:S(2)}) collective-permute-start(f32[8,128]{1,0:T(8,128)S(1)} %add_add_fusion), channel_id=1, source_target_pairs={{0,4},{4,0},{8,12},{12,8},{16,20},{20,16},{24,28},{28,24},{32,36},... | collective-permute-start | bytes 12296 | tf_op jit(solution)/shard_map/ppermute | solution.py:648
  69.5 11.2 %collective-permute-start.18 = (f32[32,128]{1,0:T(8,128)S(1)}, f32[32,128]{1,0:T(8,128)S(1)}, u32[]{:S(2)}, u32[]{:S(2)}) collective-permute-start(f32[32,128]{1,0:T(8,128)S(1)} %pad.22), channel_id=1, source_target_pairs={{4,16},{12,24},{16,4},{20,32},{24,12},{28,40},{32,20},{36,48},{40,... | collective-permute-start | bytes 49160 | tf_op jit(solution)/shard_map/ppermute | solution.py:648
  73.1 7.7 %collective-permute-start.19 = (f32[16,128]{1,0:T(8,128)S(1)}, f32[16,128]{1,0:T(8,128)S(1)}, u32[]{:S(2)}, u32[]{:S(2)}) collective-permute-start(f32[16,128]{1,0:T(8,128)S(1)} %pad_maximum_fusion.1.both), channel_id=1, source_target_pairs={{0,8},{8,16},{12,4},{16,24},{20,12},{24,32},{28,20},{32,40},{36,28... | collective-permute-start | bytes 24584 | tf_op jit(solution)/shard_map/ppermute | solution.py:648
  80.7 1.2 %collective-permute-start.20 = (f32[16,128]{1,0:T(8,128)S(1)}, f32[16,128]{1,0:T(8,128)S(1)}, u32[]{:S(2)}, u32[]{:S(2)}) collective-permute-start(f32[16,128]{1,0:T(8,128)S(1)} %collective-permute-done.19.ahead), channel_id=1, source_target_pairs={{0,4},{4,0},{8,12},{12,8},{16,20},{20,16},{24,28},{28,24},{32,36},... | collective-permute-start | bytes 24584 | tf_op jit(solution)/shard_map/ppermute | solution.py:648

commit v5 on v4

--- a/solution.py
+++ b/solution.py
@@ -107,12 +107,18 @@
             total = total + pltpu.roll(rows[4 + s : 5 + s], s + 1, 1)
         return total
 
-    def adjoint(self, value):
+    def sums(self, value):
         part = self.moments(value)
-        rows = sum(self.cubic[n] * part(n) for n in range(4))
-        return self.gather(dot(rows, self.hot))
-
-    def band(self, value):
+        return sum(self.cubic[n] * part(n) for n in range(4))
+
+    def adjoints(self, values, weight=None):
+        stack = [self.sums(v) for v in values]
+        if weight is not None:
+            stack += self.bands(weight)
+        rows = dot(jnp.concatenate(stack, axis=0), self.hot)
+        return [self.gather(rows[8 * n : 8 * n + 8]) for n in range(len(stack))]
+
+    def bands(self, value):
         part = self.moments(value)
         parts = [part(n) for n in range(7)]
         y = [sum(self.cubic[j] * parts[i + j] for j in range(4)) for i in range(4)]
@@ -121,8 +127,7 @@
             moved = [pltpu.roll(v, 8 - m, 0) if m else v for v in y]
             rows = sum(self.cubic[i] * moved[i] for i in range(4))
             stack.append(jnp.where((self.sub & 3) + m < 4, rows, 0.0))
-        rows = dot(jnp.concatenate(stack, axis=0), self.hot)
-        return [self.gather(rows[8 * m : 8 * m + 8]) for m in range(4)]
+        return stack
 
 
 LAST_ROW = ROWS - SLAB_ROWS
@@ -400,14 +405,15 @@
     n = counted[...] + planes[all_rows(COUNT), :]
     w = weight[...] * n
     weight_out[...] = w
-    part_out[0:1, :] = spline.adjoint(
-        value[...] * n + w * planes[all_rows(FIELD), :] - own[...] - collected(planes, 0)
-    )
-    part_out[1:2, :] = -spline.adjoint(side[...] + collected(planes, 2))
-    part_out[2:3, :] = -spline.adjoint(collected(planes, 4))
+    mine = value[...] * n + w * planes[all_rows(FIELD), :] - own[...] - collected(planes, 0)
+    others = [side[...] + collected(planes, 2), collected(planes, 4)]
+    rows = spline.adjoints([mine] + others, w)
+    part_out[0:1, :] = rows[0]
+    part_out[1:2, :] = -rows[1]
+    part_out[2:3, :] = -rows[2]
     part_out[3:4, :] = here.block_row()
-    for m, row in enumerate(spline.band(w)):
-        part_out[4 + m : 5 + m, :] = row
+    for m in range(4):
+        part_out[4 + m : 5 + m, :] = rows[3 + m]
 
 
 def near_tiles(both, ahead, third, behind):
@@ -541,11 +547,11 @@
         ],
         planes,
     )
-    part_out[0:1, :] = spline.adjoint(
-        weight[...] * planes[all_rows(FIELD), :] - collected(planes, 0)
-    )
-    part_out[1:2, :] = -spline.adjoint(collected(planes, 2))
-    part_out[2:3, :] = -spline.adjoint(collected(planes, 4))
+    mine = weight[...] * planes[all_rows(FIELD), :] - collected(planes, 0)
+    rows = spline.adjoints([mine, collected(planes, 2), collected(planes, 4)])
+    part_out[0:1, :] = rows[0]
+    part_out[1:2, :] = -rows[1]
+    part_out[2:3, :] = -rows[2]
     part_out[3:4, :] = here.block_row()
     part_out[4:8, :] = jnp.zeros((4, LANES), jnp.float32)
 

time: 86.5 us -> 85.6 us (0.990)
  Pallas kernels: 21.1 us -> 18.4 us
  waiting for transfers between devices: 24.1 us -> 25.1 us
    pallas_call x1, Pallas kernels: 5.34 us -> 3.66 us  [per_device(): call(early_kernel, 'early_pairs', [VMEM] * 3 + [HBM], [VMEM] * 6, [f32(2...]
    ppermute x12, waiting for transfers between devices: 16.8 us -> 17.8 us  [move(): return lax.ppermute(value, 'tile', route)]
  transfers between devices with their start and end apart: 21 -> 21, of which waited for: 11 -> 11; matrix products, arithmetic and copies ran while one was open for 4% -> 4% of each run, Pallas kernels for 6% -> 4%
where the time goes in v5:
time: 85.6 us; the launch traced here: 85 us
  starting transfers between devices  35.9 us (42%)
  waiting for transfers between devices  25.1 us (29%)
  Pallas kernels  18.4 us (21%)
  local copies, waits for them, and re-layouts  3.35 us (4%)
  between operations  1.5 us (2%)
    ppermute x12, starting transfers between devices, move(): return lax.ppermute(value, 'tile', route)  18.5 us
    ppermute x12, waiting for transfers between devices, move(): return lax.ppermute(value, 'tile', route)  17.8 us
    ppermute x9, starting transfers between devices, over_knot(): lax.ppermute(value, 'knot', [(i, (i + s) % knots) for i in range(knots)])  17.4 us
    ppermute x9, waiting for transfers between devices, over_knot(): lax.ppermute(value, 'knot', [(i, (i + s) % knots) for i in range(knots)])  7.33 us
    pallas_call x1, Pallas kernels, per_device(): call(late_kernel, 'late_pairs', [VMEM] * 13 + [ANY], [VMEM] * 3, [f32(CAP...  5.74 us
    pallas_call x1, Pallas kernels, per_device(): call(step_kernel, 'first_step', [VMEM] * 12, [VMEM] * 3, [f32(8, LANES),...  4.88 us
    pallas_call x1, Pallas kernels, per_device(): call(final_kernel, 'second_step', [VMEM] * 8 + [ANY] * 2, [VMEM, ANY], [f...  4.08 us
    pallas_call x1, Pallas kernels, per_device(): call(early_kernel, 'early_pairs', [VMEM] * 3 + [HBM], [VMEM] * 6, [f32(2...  3.66 us
  transfers between devices with their start and end apart: 21, of which 11 were waited for; matrix products, arithmetic and copies ran while one was open for 4% of the time, Pallas kernels for 4%

profile of v5, /device:TPU:24, one launch (start us, length us, event | category | flops | bytes accessed | tf_op | source)
XLA Modules:
  0.0 85.0 jit_solution(16142959764529643144)
XLA Ops:
  0.7 4.9 %collective-permute-start.6 = (f32[1,8,65536]{2,1,0:T(8,128)}, f32[1,8,65536]{2,1,0:T(8,128)S(1)}, u32[]{:S(2)}, u32[]{:S(2)}) collective-permute-start(f32[1,8,65536]{2,1,0:T(8,128)} %param.7), channel_id=1, source_target_pairs={{4,8},{8,4},{12,16},{16,12},{20,24},{24,20},{28,32},{32,28},{36,40... | collective-permute-start | bytes 6291464 | tf_op jit(solution)/shard_map/ppermute | solution.py:654
  5.7 2.0 %collective-permute-start = (f32[1,64]{1,0:T(1,128)}, f32[1,64]{1,0:T(1,128)S(1)}, u32[]{:S(2)}, u32[]{:S(2)}) collective-permute-start(f32[1,64]{1,0:T(1,128)} %start.1), channel_id=1, source_target_pairs={{0,1},{1,2},{2,3},{3,0},{4,5},{5,6},{6,7},{7,4},{8,9},{9,10},{10,1... | collective-permute-start | bytes 776 | tf_op jit(solution)/shard_map/ppermute | solution.py:658
  7.7 3.6 %collective-permute-start.1 = (f32[1,64]{1,0:T(1,128)}, f32[1,64]{1,0:T(1,128)S(1)}, u32[]{:S(2)}, u32[]{:S(2)}) collective-permute-start(f32[1,64]{1,0:T(1,128)} %start.1), channel_id=1, source_target_pairs={{0,2},{1,3},{2,0},{3,1},{4,6},{5,7},{6,4},{7,5},{8,10},{9,11},{10,... | collective-permute-start | bytes 776 | tf_op jit(solution)/shard_map/ppermute | solution.py:658
  11.2 1.0 %collective-permute-start.2 = (f32[1,64]{1,0:T(1,128)}, f32[1,64]{1,0:T(1,128)S(1)}, u32[]{:S(2)}, u32[]{:S(2)}) collective-permute-start(f32[1,64]{1,0:T(1,128)} %start.1), channel_id=1, source_target_pairs={{0,3},{1,0},{2,1},{3,2},{4,7},{5,4},{6,5},{7,6},{8,11},{9,8},{10,9... | collective-permute-start | bytes 776 | tf_op jit(solution)/shard_map/ppermute | solution.py:658
  12.2 0.7 convert_element_type.22
  13.3 1.7 %collective-permute-done.2 = f32[1,64]{1,0:T(1,128)S(1)} collective-permute-done((f32[1,64]{1,0:T(1,128)}, f32[1,64]{1,0:T(1,128)S(1)}, u32[]{:S(2)}, u32[]{:S(2)}) %collective-permute-start.2) | collective-permute-done | bytes 288 | tf_op jit(solution)/shard_map/ppermute | solution.py:658
  14.9 0.7 concatenate.9.column
  15.7 2.8 %collective-permute-start.4 = (f32[6,64]{1,0:T(8,128)S(1)}, f32[6,64]{1,0:T(8,128)S(1)}, u32[]{:S(2)}, u32[]{:S(2)}) collective-permute-start(f32[6,64]{1,0:T(8,128)S(1)} %concatenate.9.column), channel_id=1, source_target_pairs={{4,8},{8,4},{12,16},{16,12},{20,24},{24,20},{28,32},{32,28},{36,40... | collective-permute-start | bytes 4616 | tf_op jit(solution)/shard_map/ppermute | solution.py:654
  18.5 1.9 %pad.19.near = f32[4352,128]{1,0:T(8,128)S(1)} pad(f32[4096,128]{1,0:T(8,128)} %bitcast.30, f32[]{:T(128)} %constant.2.clone.1), padding=128_128x0_0 | pad | bytes 4325380 | tf_op jit(solution)/shard_map/jit(_pad)/pad | solution.py:671
  21.6 3.7 %early_pairs.1 = (f32[16,72,128]{2,1,0:T(8,128)S(1)}, f32[512,128]{1,0:T(8,128)S(1)}, f32[512,128]{1,0:T(8,128)S(1)}, f32[512,128]{1,0:T(8,128)S(1)}, f32[512,128]{1,0:T(8,128)S(1)}, /*index=5*/f32[512,128]{1,0:T(8,128)S(1)}) custom-call(f32[6,64]{1,0:T(8,128)S(1)} %concatenate.9.column, f32[4352,128]{1,0:T(8,128)S(1)} %pad.19.near, ...), custom_call_target="tpu_custom_call" | custom-call | tf_op jit(solution)/shard_map/early_pairs/pallas_call | solution.py:672
  25.2 5.2 %collective-permute-done.4.side_b = f32[6,64]{1,0:T(8,128)S(1)} collective-permute-done((f32[6,64]{1,0:T(8,128)S(1)}, f32[6,64]{1,0:T(8,128)S(1)}, u32[]{:S(2)}, u32[]{:S(2)}) %collective-permute-start.4) | collective-permute-done | bytes 1568 | tf_op jit(solution)/shard_map/ppermute | solution.py:654
  30.5 5.7 %late_pairs.1 = (f32[8,72,128]{2,1,0:T(8,128)S(1)}, f32[512,128]{1,0:T(8,128)S(1)}, f32[8,128]{1,0:T(8,128)S(1)}) custom-call(s32[1,2]{1,0:T(1,128)S(1)} %copy-done.2, s32[1,1]{1,0:T(1,128)} %bitcast.28.shifts, f32[6,64]{1,0:T(8,128)S(1)} %concatenate.9.column, f32[6,64]{1,0:T(8,128)S(1)} %collective-permute-done.3.side_a, ...), custom_call_target="tpu_custom_call" | custom-call | tf_op jit(solution)/shard_map/late_pairs/pallas_call | solution.py:679
  36.2 2.0 %collective-permute-start.7 = (f32[8,128]{1,0:T(8,128)S(1)}, f32[8,128]{1,0:T(8,128)S(1)}, u32[]{:S(2)}, u32[]{:S(2)}) collective-permute-start(f32[8,128]{1,0:T(8,128)S(1)} %get-tuple-element.26), channel_id=1, source_target_pairs={{0,1},{1,2},{2,3},{3,0},{4,5},{5,6},{6,7},{7,4},{8,9},{9,10},{10,1... | collective-permute-start | bytes 12296 | tf_op jit(solution)/shard_map/ppermute | solution.py:658
  38.2 3.6 %collective-permute-start.8 = (f32[8,128]{1,0:T(8,128)S(1)}, f32[8,128]{1,0:T(8,128)S(1)}, u32[]{:S(2)}, u32[]{:S(2)}) collective-permute-start(f32[8,128]{1,0:T(8,128)S(1)} %get-tuple-element.26), channel_id=1, source_target_pairs={{0,2},{1,3},{2,0},{3,1},{4,6},{5,7},{6,4},{7,5},{8,10},{9,11},{10,... | collective-permute-start | bytes 12296 | tf_op jit(solution)/shard_map/ppermute | solution.py:658
  41.8 1.0 %collective-permute-start.9 = (f32[8,128]{1,0:T(8,128)S(1)}, f32[8,128]{1,0:T(8,128)S(1)}, u32[]{:S(2)}, u32[]{:S(2)}) collective-permute-start(f32[8,128]{1,0:T(8,128)S(1)} %get-tuple-element.26), channel_id=1, source_target_pairs={{0,3},{1,0},{2,1},{3,2},{4,7},{5,4},{6,5},{7,6},{8,11},{9,8},{10,9... | collective-permute-start | bytes 12296 | tf_op jit(solution)/shard_map/ppermute | solution.py:658
  42.8 0.6 collective-permute-done.8
  43.4 2.0 %collective-permute-done.9 = f32[8,128]{1,0:T(8,128)S(1)} collective-permute-done((f32[8,128]{1,0:T(8,128)S(1)}, f32[8,128]{1,0:T(8,128)S(1)}, u32[]{:S(2)}, u32[]{:S(2)}) %collective-permute-start.9) | collective-permute-done | bytes 4128 | tf_op jit(solution)/shard_map/ppermute | solution.py:658
  45.4 2.4 %collective-permute-start.11 = (f32[32,128]{1,0:T(8,128)S(1)}, f32[32,128]{1,0:T(8,128)S(1)}, u32[]{:S(2)}, u32[]{:S(2)}) collective-permute-start(f32[32,128]{1,0:T(8,128)S(1)} %pad.21), channel_id=1, source_target_pairs={{4,16},{12,24},{16,4},{20,32},{24,12},{28,40},{32,20},{36,48},{40,... | collective-permute-start | bytes 49160 | tf_op jit(solution)/shard_map/ppermute | solution.py:654
  47.9 2.6 %collective-permute-start.12 = (f32[16,128]{1,0:T(8,128)S(1)}, f32[16,128]{1,0:T(8,128)S(1)}, u32[]{:S(2)}, u32[]{:S(2)}) collective-permute-start(f32[16,128]{1,0:T(8,128)S(1)} %pad_maximum_fusion.both), channel_id=1, source_target_pairs={{0,8},{8,16},{12,4},{16,24},{20,12},{24,32},{28,20},{32,40},{36,28... | collective-permute-start | bytes 24584 | tf_op jit(solution)/shard_map/ppermute | solution.py:654
  50.5 5.0 %collective-permute-done.12.ahead = f32[16,128]{1,0:T(8,128)S(1)} collective-permute-done((f32[16,128]{1,0:T(8,128)S(1)}, f32[16,128]{1,0:T(8,128)S(1)}, u32[]{:S(2)}, u32[]{:S(2)}) %collective-permute-start.12) | collective-permute-done | bytes 8224 | tf_op jit(solution)/shard_map/ppermute | solution.py:654
  55.5 1.2 %collective-permute-done.13.behind = f32[16,128]{1,0:T(8,128)S(1)} collective-permute-done((f32[16,128]{1,0:T(8,128)S(1)}, f32[16,128]{1,0:T(8,128)S(1)}, u32[]{:S(2)}, u32[]{:S(2)}) %collective-permute-start.13) | collective-permute-done | bytes 8224 | tf_op jit(solution)/shard_map/ppermute | solution.py:654
  56.7 4.9 %first_step.1 = (f32[8,128]{1,0:T(8,128)S(1)}, f32[8,128]{1,0:T(8,128)S(1)}, f32[256,128]{1,0:T(8,128)S(1)}) custom-call(s32[1,2]{1,0:T(1,128)S(1)} %copy-done.2, f32[16,128]{1,0:T(8,128)S(1)} %pad_maximum_fusion.both, f32[16,128]{1,0:T(8,128)S(1)} %collective-permute-done.12.ahead, f32[32,128]{1,0:T(8,128)S(1)} %collective-permute-done.11.third, ...), custom_call_target="tpu_custom_call" | custom-call | tf_op jit(solution)/shard_map/first_step/pallas_call | solution.py:701
  61.7 3.7 %collective-permute-start.15 = (f32[8,128]{1,0:T(8,128)S(1)}, f32[8,128]{1,0:T(8,128)S(1)}, u32[]{:S(2)}, u32[]{:S(2)}) collective-permute-start(f32[8,128]{1,0:T(8,128)S(1)} %get-tuple-element.31), channel_id=1, source_target_pairs={{0,2},{1,3},{2,0},{3,1},{4,6},{5,7},{6,4},{7,5},{8,10},{9,11},{10,... | collective-permute-start | bytes 12296 | tf_op jit(solution)/shard_map/ppermute | solution.py:658
  65.3 0.5 collective-permute-start.16
  65.9 0.6 collective-permute-done.14
  66.5 0.5 collective-permute-done.15
  67.0 2.0 %collective-permute-done.16 = f32[8,128]{1,0:T(8,128)S(1)} collective-permute-done((f32[8,128]{1,0:T(8,128)S(1)}, f32[8,128]{1,0:T(8,128)S(1)}, u32[]{:S(2)}, u32[]{:S(2)}) %collective-permute-start.16) | collective-permute-done | bytes 4128 | tf_op jit(solution)/shard_map/ppermute | solution.py:658
  69.0 3.1 %collective-permute-start.18 = (f32[32,128]{1,0:T(8,128)S(1)}, f32[32,128]{1,0:T(8,128)S(1)}, u32[]{:S(2)}, u32[]{:S(2)}) collective-permute-start(f32[32,128]{1,0:T(8,128)S(1)} %pad.22), channel_id=1, source_target_pairs={{4,16},{12,24},{16,4},{20,32},{24,12},{28,40},{32,20},{36,48},{40,... | collective-permute-start | bytes 49160 | tf_op jit(solution)/shard_map/ppermute | solution.py:654
  72.1 2.4 %collective-permute-start.19 = (f32[16,128]{1,0:T(8,128)S(1)}, f32[16,128]{1,0:T(8,128)S(1)}, u32[]{:S(2)}, u32[]{:S(2)}) collective-permute-start(f32[16,128]{1,0:T(8,128)S(1)} %pad_maximum_fusion.1.both), channel_id=1, source_target_pairs={{0,8},{8,16},{12,4},{16,24},{20,12},{24,32},{28,20},{32,40},{36,28... | collective-permute-start | bytes 24584 | tf_op jit(solution)/shard_map/ppermute | solution.py:654
  74.5 5.2 %collective-permute-done.19.ahead = f32[16,128]{1,0:T(8,128)S(1)} collective-permute-done((f32[16,128]{1,0:T(8,128)S(1)}, f32[16,128]{1,0:T(8,128)S(1)}, u32[]{:S(2)}, u32[]{:S(2)}) %collective-permute-start.19) | collective-permute-done | bytes 8224 | tf_op jit(solution)/shard_map/ppermute | solution.py:654
  79.8 1.2 %collective-permute-done.20.behind = f32[16,128]{1,0:T(8,128)S(1)} collective-permute-done((f32[16,128]{1,0:T(8,128)S(1)}, f32[16,128]{1,0:T(8,128)S(1)}, u32[]{:S(2)}, u32[]{:S(2)}) %collective-permute-start.20) | collective-permute-done | bytes 8224 | tf_op jit(solution)/shard_map/ppermute | solution.py:654
  80.9 4.1 %second_step.1 = (f32[1,64]{1,0:T(1,128)}, f32[4096,128]{1,0:T(8,128)}) custom-call(s32[1,2]{1,0:T(1,128)S(1)} %copy-done.2, s32[1,1]{1,0:T(1,128)} %bitcast.29.shifts, f32[16,128]{1,0:T(8,128)S(1)} %pad_maximum_fusion.1.both, f32[16,128]{1,0:T(8,128)S(1)} %collective-permute-done.19.ahead, f32[32,128]{1,0:T(8,128)S(1)} %collective-permute-done.18.third, ...), custom_call_target="tpu_custom_call" | custom-call | tf_op jit(solution)/shard_map/second_step/pallas_call | solution.py:712
  (36 shorter events, 1.1 us)
Async XLA Ops:
  0.6 20.9 %collective-permute-start.5 = (f32[1,8,65536]{2,1,0:T(8,128)}, f32[1,8,65536]{2,1,0:T(8,128)}, u32[]{:S(2)}, u32[]{:S(2)}) collective-permute-start(f32[1,8,65536]{2,1,0:T(8,128)} %param.7), channel_id=1, source_target_pairs={{0,4},{4,0},{8,12},{12,8},{16,20},{20,16},{24,28},{28,24},{32,36},... | collective-permute-start | bytes 6291464 | tf_op jit(solution)/shard_map/ppermute | solution.py:654
  0.7 29.7 %collective-permute-start.6 = (f32[1,8,65536]{2,1,0:T(8,128)}, f32[1,8,65536]{2,1,0:T(8,128)S(1)}, u32[]{:S(2)}, u32[]{:S(2)}) collective-permute-start(f32[1,8,65536]{2,1,0:T(8,128)} %param.7), channel_id=1, source_target_pairs={{4,8},{8,4},{12,16},{16,12},{20,24},{24,20},{28,32},{32,28},{36,40... | collective-permute-start | bytes 6291464 | tf_op jit(solution)/shard_map/ppermute | solution.py:654
  5.7 7.6 %collective-permute-start = (f32[1,64]{1,0:T(1,128)}, f32[1,64]{1,0:T(1,128)S(1)}, u32[]{:S(2)}, u32[]{:S(2)}) collective-permute-start(f32[1,64]{1,0:T(1,128)} %start.1), channel_id=1, source_target_pairs={{0,1},{1,2},{2,3},{3,0},{4,5},{5,6},{6,7},{7,4},{8,9},{9,10},{10,1... | collective-permute-start | bytes 776 | tf_op jit(solution)/shard_map/ppermute | solution.py:658
  7.7 5.6 %collective-permute-start.1 = (f32[1,64]{1,0:T(1,128)}, f32[1,64]{1,0:T(1,128)S(1)}, u32[]{:S(2)}, u32[]{:S(2)}) collective-permute-start(f32[1,64]{1,0:T(1,128)} %start.1), channel_id=1, source_target_pairs={{0,2},{1,3},{2,0},{3,1},{4,6},{5,7},{6,4},{7,5},{8,10},{9,11},{10,... | collective-permute-start | bytes 776 | tf_op jit(solution)/shard_map/ppermute | solution.py:658
  11.2 3.7 %collective-permute-start.2 = (f32[1,64]{1,0:T(1,128)}, f32[1,64]{1,0:T(1,128)S(1)}, u32[]{:S(2)}, u32[]{:S(2)}) collective-permute-start(f32[1,64]{1,0:T(1,128)} %start.1), channel_id=1, source_target_pairs={{0,3},{1,0},{2,1},{3,2},{4,7},{5,4},{6,5},{7,6},{8,11},{9,8},{10,9... | collective-permute-start | bytes 776 | tf_op jit(solution)/shard_map/ppermute | solution.py:658
  15.6 9.6 %collective-permute-start.3 = (f32[6,64]{1,0:T(8,128)S(1)}, f32[6,64]{1,0:T(8,128)S(1)}, u32[]{:S(2)}, u32[]{:S(2)}) collective-permute-start(f32[6,64]{1,0:T(8,128)S(1)} %concatenate.9.column), channel_id=1, source_target_pairs={{0,4},{4,0},{8,12},{12,8},{16,20},{20,16},{24,28},{28,24},{32,36},... | collective-permute-start | bytes 4616 | tf_op jit(solution)/shard_map/ppermute | solution.py:654
  15.7 14.8 %collective-permute-start.4 = (f32[6,64]{1,0:T(8,128)S(1)}, f32[6,64]{1,0:T(8,128)S(1)}, u32[]{:S(2)}, u32[]{:S(2)}) collective-permute-start(f32[6,64]{1,0:T(8,128)S(1)} %concatenate.9.column), channel_id=1, source_target_pairs={{4,8},{8,4},{12,16},{16,12},{20,24},{24,20},{28,32},{32,28},{36,40... | collective-permute-start | bytes 4616 | tf_op jit(solution)/shard_map/ppermute | solution.py:654
  18.5 2.2 %copy-start.1 = (f32[1,8,65536]{2,1,0:T(8,128)S(1)}, f32[1,8,65536]{2,1,0:T(8,128)}, u32[]{:S(2)}) copy-start(f32[1,8,65536]{2,1,0:T(8,128)} %param.6) | copy-start | bytes 6291460
  21.5 8.9 %copy-start.2 = (s32[1,2]{1,0:T(1,128)S(1)}, s32[1,2]{1,0:T(1,128)}, u32[]{:S(2)}) copy-start(s32[1,2]{1,0:T(1,128)} %blocks.5) | copy-start | bytes 28
  30.5 26.3 %copy-start.3 = (f32[1,64]{1,0:T(1,128)S(1)}, f32[1,64]{1,0:T(1,128)}, u32[]{:S(2)}) copy-start(f32[1,64]{1,0:T(1,128)} %start.1) | copy-start | bytes 772
  30.5 50.5 %copy-start = (f32[1,8,65536]{2,1,0:T(8,128)S(1)}, f32[1,8,65536]{2,1,0:T(8,128)}, u32[]{:S(2)}) copy-start(f32[1,8,65536]{2,1,0:T(8,128)} %param.7) | copy-start | bytes 6291460
  36.2 6.6 %collective-permute-start.7 = (f32[8,128]{1,0:T(8,128)S(1)}, f32[8,128]{1,0:T(8,128)S(1)}, u32[]{:S(2)}, u32[]{:S(2)}) collective-permute-start(f32[8,128]{1,0:T(8,128)S(1)} %get-tuple-element.26), channel_id=1, source_target_pairs={{0,1},{1,2},{2,3},{3,0},{4,5},{5,6},{6,7},{7,4},{8,9},{9,10},{10,1... | collective-permute-start | bytes 12296 | tf_op jit(solution)/shard_map/ppermute | solution.py:658
  38.2 5.2 %collective-permute-start.8 = (f32[8,128]{1,0:T(8,128)S(1)}, f32[8,128]{1,0:T(8,128)S(1)}, u32[]{:S(2)}, u32[]{:S(2)}) collective-permute-start(f32[8,128]{1,0:T(8,128)S(1)} %get-tuple-element.26), channel_id=1, source_target_pairs={{0,2},{1,3},{2,0},{3,1},{4,6},{5,7},{6,4},{7,5},{8,10},{9,11},{10,... | collective-permute-start | bytes 12296 | tf_op jit(solution)/shard_map/ppermute | solution.py:658
  41.8 3.6 %collective-permute-start.9 = (f32[8,128]{1,0:T(8,128)S(1)}, f32[8,128]{1,0:T(8,128)S(1)}, u32[]{:S(2)}, u32[]{:S(2)}) collective-permute-start(f32[8,128]{1,0:T(8,128)S(1)} %get-tuple-element.26), channel_id=1, source_target_pairs={{0,3},{1,0},{2,1},{3,2},{4,7},{5,4},{6,5},{7,6},{8,11},{9,8},{10,9... | collective-permute-start | bytes 12296 | tf_op jit(solution)/shard_map/ppermute | solution.py:658
  45.4 2.4 %collective-permute-start.10 = (f32[8,128]{1,0:T(8,128)S(1)}, f32[8,128]{1,0:T(8,128)S(1)}, u32[]{:S(2)}, u32[]{:S(2)}) collective-permute-start(f32[8,128]{1,0:T(8,128)S(1)} %add_add_fusion.1), channel_id=1, source_target_pairs={{0,4},{4,0},{8,12},{12,8},{16,20},{20,16},{24,28},{28,24},{32,36},... | collective-permute-start | bytes 12296 | tf_op jit(solution)/shard_map/ppermute | solution.py:654
  45.4 10.1 %collective-permute-start.11 = (f32[32,128]{1,0:T(8,128)S(1)}, f32[32,128]{1,0:T(8,128)S(1)}, u32[]{:S(2)}, u32[]{:S(2)}) collective-permute-start(f32[32,128]{1,0:T(8,128)S(1)} %pad.21), channel_id=1, source_target_pairs={{4,16},{12,24},{16,4},{20,32},{24,12},{28,40},{32,20},{36,48},{40,... | collective-permute-start | bytes 49160 | tf_op jit(solution)/shard_map/ppermute | solution.py:654
  47.9 7.7 %collective-permute-start.12 = (f32[16,128]{1,0:T(8,128)S(1)}, f32[16,128]{1,0:T(8,128)S(1)}, u32[]{:S(2)}, u32[]{:S(2)}) collective-permute-start(f32[16,128]{1,0:T(8,128)S(1)} %pad_maximum_fusion.both), channel_id=1, source_target_pairs={{0,8},{8,16},{12,4},{16,24},{20,12},{24,32},{28,20},{32,40},{36,28... | collective-permute-start | bytes 24584 | tf_op jit(solution)/shard_map/ppermute | solution.py:654
  55.5 1.2 %collective-permute-start.13 = (f32[16,128]{1,0:T(8,128)S(1)}, f32[16,128]{1,0:T(8,128)S(1)}, u32[]{:S(2)}, u32[]{:S(2)}) collective-permute-start(f32[16,128]{1,0:T(8,128)S(1)} %collective-permute-done.12.ahead), channel_id=1, source_target_pairs={{0,4},{4,0},{8,12},{12,8},{16,20},{20,16},{24,28},{28,24},{32,36},... | collective-permute-start | bytes 24584 | tf_op jit(solution)/shard_map/ppermute | solution.py:654
  61.6 4.9 %collective-permute-start.14 = (f32[8,128]{1,0:T(8,128)S(1)}, f32[8,128]{1,0:T(8,128)S(1)}, u32[]{:S(2)}, u32[]{:S(2)}) collective-permute-start(f32[8,128]{1,0:T(8,128)S(1)} %get-tuple-element.31), channel_id=1, source_target_pairs={{0,1},{1,2},{2,3},{3,0},{4,5},{5,6},{6,7},{7,4},{8,9},{9,10},{10,1... | collective-permute-start | bytes 12296 | tf_op jit(solution)/shard_map/ppermute | solution.py:658
  61.7 5.3 %collective-permute-start.15 = (f32[8,128]{1,0:T(8,128)S(1)}, f32[8,128]{1,0:T(8,128)S(1)}, u32[]{:S(2)}, u32[]{:S(2)}) collective-permute-start(f32[8,128]{1,0:T(8,128)S(1)} %get-tuple-element.31), channel_id=1, source_target_pairs={{0,2},{1,3},{2,0},{3,1},{4,6},{5,7},{6,4},{7,5},{8,10},{9,11},{10,... | collective-permute-start | bytes 12296 | tf_op jit(solution)/shard_map/ppermute | solution.py:658
  65.3 3.6 %collective-permute-start.16 = (f32[8,128]{1,0:T(8,128)S(1)}, f32[8,128]{1,0:T(8,128)S(1)}, u32[]{:S(2)}, u32[]{:S(2)}) collective-permute-start(f32[8,128]{1,0:T(8,128)S(1)} %get-tuple-element.31), channel_id=1, source_target_pairs={{0,3},{1,0},{2,1},{3,2},{4,7},{5,4},{6,5},{7,6},{8,11},{9,8},{10,9... | collective-permute-start | bytes 12296 | tf_op jit(solution)/shard_map/ppermute | solution.py:658
  69.0 3.1 %collective-permute-start.17 = (f32[8,128]{1,0:T(8,128)S(1)}, f32[8,128]{1,0:T(8,128)S(1)}, u32[]{:S(2)}, u32[]{:S(2)}) collective-permute-start(f32[8,128]{1,0:T(8,128)S(1)} %add_add_fusion), channel_id=1, source_target_pairs={{0,4},{4,0},{8,12},{12,8},{16,20},{20,16},{24,28},{28,24},{32,36},... | collective-permute-start | bytes 12296 | tf_op jit(solution)/shard_map/ppermute | solution.py:654
  69.0 10.8 %collective-permute-start.18 = (f32[32,128]{1,0:T(8,128)S(1)}, f32[32,128]{1,0:T(8,128)S(1)}, u32[]{:S(2)}, u32[]{:S(2)}) collective-permute-start(f32[32,128]{1,0:T(8,128)S(1)} %pad.22), channel_id=1, source_target_pairs={{4,16},{12,24},{16,4},{20,32},{24,12},{28,40},{32,20},{36,48},{40,... | collective-permute-start | bytes 49160 | tf_op jit(solution)/shard_map/ppermute | solution.py:654
  72.1 7.7 %collective-permute-start.19 = (f32[16,128]{1,0:T(8,128)S(1)}, f32[16,128]{1,0:T(8,128)S(1)}, u32[]{:S(2)}, u32[]{:S(2)}) collective-permute-start(f32[16,128]{1,0:T(8,128)S(1)} %pad_maximum_fusion.1.both), channel_id=1, source_target_pairs={{0,8},{8,16},{12,4},{16,24},{20,12},{24,32},{28,20},{32,40},{36,28... | collective-permute-start | bytes 24584 | tf_op jit(solution)/shard_map/ppermute | solution.py:654
  79.8 1.2 %collective-permute-start.20 = (f32[16,128]{1,0:T(8,128)S(1)}, f32[16,128]{1,0:T(8,128)S(1)}, u32[]{:S(2)}, u32[]{:S(2)}) collective-permute-start(f32[16,128]{1,0:T(8,128)S(1)} %collective-permute-done.19.ahead), channel_id=1, source_target_pairs={{0,4},{4,0},{8,12},{12,8},{16,20},{20,16},{24,28},{28,24},{32,36},... | collective-permute-start | bytes 24584 | tf_op jit(solution)/shard_map/ppermute | solution.py:654

commit v6 on v5

--- a/solution.py
+++ b/solution.py
@@ -560,18 +560,12 @@
 
 
 def final_kernel(
-    blocks, shifts, both, ahead, third, behind, state, factor, grad_in, image_in,
+    blocks, shifts, both, ahead, third, behind, state, factor, grad, image,
     coef_out, warped_out,
-    grad, image, field, steps, sems, out_sems,
+    moved_image, field, steps, out_sems,
 ):
     size = ROWS * 8 // CHUNKS
     at = [pl.ds(n * size, size) for n in range(CHUNKS)]
-    loads = []
-    for n in range(CHUNKS):
-        loads.append(pltpu.make_async_copy(grad_in.at[at[n]], grad.at[at[n]], sems.at[0, n]))
-        loads.append(pltpu.make_async_copy(image_in.at[at[n]], image.at[at[n]], sems.at[1, n]))
-    for copy in loads:
-        copy.start()
     here = Here(blocks, shifts)
     steps[...] = jnp.zeros((LANES, LANES), jnp.float32)
     tiles = near_tiles(both, ahead, third, behind)
@@ -589,18 +583,16 @@
     field[...] = spline.field(joined(coefs)) + here.rigid
     stores = []
     for n in range(CHUNKS):
-        loads[2 * n].wait()
-        loads[2 * n + 1].wait()
 
         def body(g, carry):
             for r in range(8):
                 row = g * 8 + r
                 rows = pl.ds(pl.multiple_of(row * 8, 8), 8)
-                image[rows, :] = image[rows, :] + grad[rows, :] * field[pl.ds(row, 1), :]
+                moved_image[rows, :] = image[rows, :] + grad[rows, :] * field[pl.ds(row, 1), :]
             return carry
 
         lax.fori_loop(n * size // 64, (n + 1) * size // 64, body, 0)
-        stores.append(pltpu.make_async_copy(image.at[at[n]], warped_out.at[at[n]], out_sems.at[n]))
+        stores.append(pltpu.make_async_copy(moved_image.at[at[n]], warped_out.at[at[n]], out_sems.at[n]))
         stores[-1].start()
     for copy in stores:
         copy.wait()
@@ -711,12 +703,12 @@
     )
     coef, warped = call(
         final_kernel, "second_step",
-        [VMEM] * 8 + [ANY] * 2,
+        [VMEM] * 10,
         [VMEM, ANY],
         [f32(1, BLOCK), f32(ROWS * DEPTH, LANES)],
-        [pltpu.VMEM((ROWS * DEPTH, LANES), jnp.float32)] * 2
+        [pltpu.VMEM((ROWS * DEPTH, LANES), jnp.float32)]
         + [pltpu.VMEM((ROWS, LANES), jnp.float32), square()]
-        + [pltpu.SemaphoreType.DMA((2, CHUNKS)), pltpu.SemaphoreType.DMA((CHUNKS,))],
+        + [pltpu.SemaphoreType.DMA((CHUNKS,))],
     )(tile_blocks, shifts, *exchange(part), state, factor, grad, image)
     warped = warped.reshape(ROWS, DEPTH, LANES).transpose(1, 0, 2).reshape(1, DEPTH, ROWS * LANES)
     return coef, warped

time: 85.6 us -> 85.4 us (level); the launches traced: 85 us -> 83.8 us
  waiting for transfers between devices: 25.1 us -> 21 us
  starting transfers between devices: 35.9 us -> 38.1 us
    ppermute x12, waiting for transfers between devices: 17.8 us -> 13.9 us  [move(): return lax.ppermute(value, 'tile', route)]
    ppermute x12, starting transfers between devices: 18.5 us -> 20.3 us  [move(): return lax.ppermute(value, 'tile', route)]
    pallas_call x1, Pallas kernels: 3.66 us -> 5.05 us  [per_device(): call(early_kernel, 'early_pairs', [VMEM] * 3 + [HBM], [VMEM] * 6, [f32(2...]
  transfers between devices with their start and end apart: 21 -> 21, of which waited for: 11 -> 11; matrix products, arithmetic and copies ran while one was open for 4% -> 4% of each run, Pallas kernels for 4% -> 6%
where the time goes in v6:
time: 85.4 us; the launch traced here: 83.8 us
  starting transfers between devices  38.1 us (45%)
  waiting for transfers between devices  21 us (25%)
  Pallas kernels  19.2 us (22%)
  local copies, waits for them, and re-layouts  3.35 us (4%)
  between operations  1.49 us (2%)
    ppermute x12, starting transfers between devices, move(): return lax.ppermute(value, 'tile', route)  20.3 us
    ppermute x9, starting transfers between devices, over_knot(): lax.ppermute(value, 'knot', [(i, (i + s) % knots) for i in range(knots)])  17.7 us
    ppermute x12, waiting for transfers between devices, move(): return lax.ppermute(value, 'tile', route)  13.9 us
    ppermute x9, waiting for transfers between devices, over_knot(): lax.ppermute(value, 'knot', [(i, (i + s) % knots) for i in range(knots)])  7.04 us
    pallas_call x1, Pallas kernels, per_device(): call(late_kernel, 'late_pairs', [VMEM] * 13 + [ANY], [VMEM] * 3, [f32(CAP...  5.52 us
    pallas_call x1, Pallas kernels, per_device(): call(early_kernel, 'early_pairs', [VMEM] * 3 + [HBM], [VMEM] * 6, [f32(2...  5.05 us
    pallas_call x1, Pallas kernels, per_device(): call(step_kernel, 'first_step', [VMEM] * 12, [VMEM] * 3, [f32(8, LANES),...  5.01 us
    pallas_call x1, Pallas kernels, per_device(): call(final_kernel, 'second_step', [VMEM] * 10, [VMEM, ANY], [f32(1, BLOCK...  3.64 us
  transfers between devices with their start and end apart: 21, of which 11 were waited for; matrix products, arithmetic and copies ran while one was open for 4% of the time, Pallas kernels for 6%

profile of v6, /device:TPU:24, one launch (start us, length us, event | category | flops | bytes accessed | tf_op | source)
XLA Modules:
  0.0 83.8 jit_solution(9287020673392722195)
XLA Ops:
  0.7 4.9 %collective-permute-start.6 = (f32[1,8,65536]{2,1,0:T(8,128)}, f32[1,8,65536]{2,1,0:T(8,128)S(1)}, u32[]{:S(2)}, u32[]{:S(2)}) collective-permute-start(f32[1,8,65536]{2,1,0:T(8,128)} %param.7), channel_id=1, source_target_pairs={{4,8},{8,4},{12,16},{16,12},{20,24},{24,20},{28,32},{32,28},{36,40... | collective-permute-start | bytes 6291464 | tf_op jit(solution)/shard_map/ppermute | solution.py:646
  5.7 2.0 %collective-permute-start = (f32[1,64]{1,0:T(1,128)}, f32[1,64]{1,0:T(1,128)S(1)}, u32[]{:S(2)}, u32[]{:S(2)}) collective-permute-start(f32[1,64]{1,0:T(1,128)} %start.1), channel_id=1, source_target_pairs={{0,1},{1,2},{2,3},{3,0},{4,5},{5,6},{6,7},{7,4},{8,9},{9,10},{10,1... | collective-permute-start | bytes 776 | tf_op jit(solution)/shard_map/ppermute | solution.py:650
  7.7 3.6 %collective-permute-start.1 = (f32[1,64]{1,0:T(1,128)}, f32[1,64]{1,0:T(1,128)S(1)}, u32[]{:S(2)}, u32[]{:S(2)}) collective-permute-start(f32[1,64]{1,0:T(1,128)} %start.1), channel_id=1, source_target_pairs={{0,2},{1,3},{2,0},{3,1},{4,6},{5,7},{6,4},{7,5},{8,10},{9,11},{10,... | collective-permute-start | bytes 776 | tf_op jit(solution)/shard_map/ppermute | solution.py:650
  11.2 1.0 %collective-permute-start.2 = (f32[1,64]{1,0:T(1,128)}, f32[1,64]{1,0:T(1,128)S(1)}, u32[]{:S(2)}, u32[]{:S(2)}) collective-permute-start(f32[1,64]{1,0:T(1,128)} %start.1), channel_id=1, source_target_pairs={{0,3},{1,0},{2,1},{3,2},{4,7},{5,4},{6,5},{7,6},{8,11},{9,8},{10,9... | collective-permute-start | bytes 776 | tf_op jit(solution)/shard_map/ppermute | solution.py:650
  12.2 0.7 convert_element_type.22
  13.3 1.7 %collective-permute-done.2 = f32[1,64]{1,0:T(1,128)S(1)} collective-permute-done((f32[1,64]{1,0:T(1,128)}, f32[1,64]{1,0:T(1,128)S(1)}, u32[]{:S(2)}, u32[]{:S(2)}) %collective-permute-start.2) | collective-permute-done | bytes 288 | tf_op jit(solution)/shard_map/ppermute | solution.py:650
  14.9 0.7 concatenate.9.column
  15.7 2.8 %collective-permute-start.4 = (f32[6,64]{1,0:T(8,128)S(1)}, f32[6,64]{1,0:T(8,128)S(1)}, u32[]{:S(2)}, u32[]{:S(2)}) collective-permute-start(f32[6,64]{1,0:T(8,128)S(1)} %concatenate.9.column), channel_id=1, source_target_pairs={{4,8},{8,4},{12,16},{16,12},{20,24},{24,20},{28,32},{32,28},{36,40... | collective-permute-start | bytes 4616 | tf_op jit(solution)/shard_map/ppermute | solution.py:646
  18.5 1.9 %pad.19.near = f32[4352,128]{1,0:T(8,128)S(1)} pad(f32[4096,128]{1,0:T(8,128)} %bitcast.30, f32[]{:T(128)} %constant.2.clone.1), padding=128_128x0_0 | pad | bytes 4325380 | tf_op jit(solution)/shard_map/jit(_pad)/pad | solution.py:663
  20.4 0.3 copy-done.1
  21.6 5.0 %early_pairs.1 = (f32[16,72,128]{2,1,0:T(8,128)S(1)}, f32[512,128]{1,0:T(8,128)S(1)}, f32[512,128]{1,0:T(8,128)S(1)}, f32[512,128]{1,0:T(8,128)S(1)}, f32[512,128]{1,0:T(8,128)S(1)}, /*index=5*/f32[512,128]{1,0:T(8,128)S(1)}) custom-call(f32[6,64]{1,0:T(8,128)S(1)} %concatenate.9.column, f32[4352,128]{1,0:T(8,128)S(1)} %pad.19.near, ...), custom_call_target="tpu_custom_call" | custom-call | tf_op jit(solution)/shard_map/early_pairs/pallas_call | solution.py:664
  26.6 3.8 %collective-permute-done.4.side_b = f32[6,64]{1,0:T(8,128)S(1)} collective-permute-done((f32[6,64]{1,0:T(8,128)S(1)}, f32[6,64]{1,0:T(8,128)S(1)}, u32[]{:S(2)}, u32[]{:S(2)}) %collective-permute-start.4) | collective-permute-done | bytes 1568 | tf_op jit(solution)/shard_map/ppermute | solution.py:646
  30.5 5.5 %late_pairs.1 = (f32[8,72,128]{2,1,0:T(8,128)S(1)}, f32[512,128]{1,0:T(8,128)S(1)}, f32[8,128]{1,0:T(8,128)S(1)}) custom-call(s32[1,2]{1,0:T(1,128)S(1)} %copy-done.2, s32[1,1]{1,0:T(1,128)} %bitcast.28.shifts, f32[6,64]{1,0:T(8,128)S(1)} %concatenate.9.column, f32[6,64]{1,0:T(8,128)S(1)} %collective-permute-done.3.side_a, ...), custom_call_target="tpu_custom_call" | custom-call | tf_op jit(solution)/shard_map/late_pairs/pallas_call | solution.py:671
  36.0 2.0 %collective-permute-start.7 = (f32[8,128]{1,0:T(8,128)S(1)}, f32[8,128]{1,0:T(8,128)S(1)}, u32[]{:S(2)}, u32[]{:S(2)}) collective-permute-start(f32[8,128]{1,0:T(8,128)S(1)} %get-tuple-element.26), channel_id=1, source_target_pairs={{0,1},{1,2},{2,3},{3,0},{4,5},{5,6},{6,7},{7,4},{8,9},{9,10},{10,1... | collective-permute-start | bytes 12296 | tf_op jit(solution)/shard_map/ppermute | solution.py:650
  38.0 3.6 %collective-permute-start.8 = (f32[8,128]{1,0:T(8,128)S(1)}, f32[8,128]{1,0:T(8,128)S(1)}, u32[]{:S(2)}, u32[]{:S(2)}) collective-permute-start(f32[8,128]{1,0:T(8,128)S(1)} %get-tuple-element.26), channel_id=1, source_target_pairs={{0,2},{1,3},{2,0},{3,1},{4,6},{5,7},{6,4},{7,5},{8,10},{9,11},{10,... | collective-permute-start | bytes 12296 | tf_op jit(solution)/shard_map/ppermute | solution.py:650
  41.6 1.0 %collective-permute-start.9 = (f32[8,128]{1,0:T(8,128)S(1)}, f32[8,128]{1,0:T(8,128)S(1)}, u32[]{:S(2)}, u32[]{:S(2)}) collective-permute-start(f32[8,128]{1,0:T(8,128)S(1)} %get-tuple-element.26), channel_id=1, source_target_pairs={{0,3},{1,0},{2,1},{3,2},{4,7},{5,4},{6,5},{7,6},{8,11},{9,8},{10,9... | collective-permute-start | bytes 12296 | tf_op jit(solution)/shard_map/ppermute | solution.py:650
  42.6 0.6 collective-permute-done.8
  43.2 2.0 %collective-permute-done.9 = f32[8,128]{1,0:T(8,128)S(1)} collective-permute-done((f32[8,128]{1,0:T(8,128)S(1)}, f32[8,128]{1,0:T(8,128)S(1)}, u32[]{:S(2)}, u32[]{:S(2)}) %collective-permute-start.9) | collective-permute-done | bytes 4128 | tf_op jit(solution)/shard_map/ppermute | solution.py:650
  45.2 2.3 %collective-permute-start.11 = (f32[32,128]{1,0:T(8,128)S(1)}, f32[32,128]{1,0:T(8,128)S(1)}, u32[]{:S(2)}, u32[]{:S(2)}) collective-permute-start(f32[32,128]{1,0:T(8,128)S(1)} %pad.21), channel_id=1, source_target_pairs={{4,16},{12,24},{16,4},{20,32},{24,12},{28,40},{32,20},{36,48},{40,... | collective-permute-start | bytes 49160 | tf_op jit(solution)/shard_map/ppermute | solution.py:646
  47.6 3.2 %collective-permute-start.12 = (f32[16,128]{1,0:T(8,128)S(1)}, f32[16,128]{1,0:T(8,128)S(1)}, u32[]{:S(2)}, u32[]{:S(2)}) collective-permute-start(f32[16,128]{1,0:T(8,128)S(1)} %pad_maximum_fusion.both), channel_id=1, source_target_pairs={{0,8},{8,16},{12,4},{16,24},{20,12},{24,32},{28,20},{32,40},{36,28... | collective-permute-start | bytes 24584 | tf_op jit(solution)/shard_map/ppermute | solution.py:646
  50.8 4.5 %collective-permute-done.12.ahead = f32[16,128]{1,0:T(8,128)S(1)} collective-permute-done((f32[16,128]{1,0:T(8,128)S(1)}, f32[16,128]{1,0:T(8,128)S(1)}, u32[]{:S(2)}, u32[]{:S(2)}) %collective-permute-start.12) | collective-permute-done | bytes 8224 | tf_op jit(solution)/shard_map/ppermute | solution.py:646
  55.2 1.2 %collective-permute-done.13.behind = f32[16,128]{1,0:T(8,128)S(1)} collective-permute-done((f32[16,128]{1,0:T(8,128)S(1)}, f32[16,128]{1,0:T(8,128)S(1)}, u32[]{:S(2)}, u32[]{:S(2)}) %collective-permute-start.13) | collective-permute-done | bytes 8224 | tf_op jit(solution)/shard_map/ppermute | solution.py:646
  56.4 5.0 %first_step.1 = (f32[8,128]{1,0:T(8,128)S(1)}, f32[8,128]{1,0:T(8,128)S(1)}, f32[256,128]{1,0:T(8,128)S(1)}) custom-call(s32[1,2]{1,0:T(1,128)S(1)} %copy-done.2, f32[16,128]{1,0:T(8,128)S(1)} %pad_maximum_fusion.both, f32[16,128]{1,0:T(8,128)S(1)} %collective-permute-done.12.ahead, f32[32,128]{1,0:T(8,128)S(1)} %collective-permute-done.11.third, ...), custom_call_target="tpu_custom_call" | custom-call | tf_op jit(solution)/shard_map/first_step/pallas_call | solution.py:693
  61.7 3.5 %collective-permute-start.15 = (f32[8,128]{1,0:T(8,128)S(1)}, f32[8,128]{1,0:T(8,128)S(1)}, u32[]{:S(2)}, u32[]{:S(2)}) collective-permute-start(f32[8,128]{1,0:T(8,128)S(1)} %get-tuple-element.31), channel_id=1, source_target_pairs={{0,2},{1,3},{2,0},{3,1},{4,6},{5,7},{6,4},{7,5},{8,10},{9,11},{10,... | collective-permute-start | bytes 12296 | tf_op jit(solution)/shard_map/ppermute | solution.py:650
  65.2 0.8 collective-permute-start.16
  66.3 0.5 collective-permute-done.15
  66.8 2.0 %collective-permute-done.16 = f32[8,128]{1,0:T(8,128)S(1)} collective-permute-done((f32[8,128]{1,0:T(8,128)S(1)}, f32[8,128]{1,0:T(8,128)S(1)}, u32[]{:S(2)}, u32[]{:S(2)}) %collective-permute-start.16) | collective-permute-done | bytes 4128 | tf_op jit(solution)/shard_map/ppermute | solution.py:650
  68.8 2.5 %collective-permute-start.18 = (f32[32,128]{1,0:T(8,128)S(1)}, f32[32,128]{1,0:T(8,128)S(1)}, u32[]{:S(2)}, u32[]{:S(2)}) collective-permute-start(f32[32,128]{1,0:T(8,128)S(1)} %pad.22), channel_id=1, source_target_pairs={{4,16},{12,24},{16,4},{20,32},{24,12},{28,40},{32,20},{36,48},{40,... | collective-permute-start | bytes 49160 | tf_op jit(solution)/shard_map/ppermute | solution.py:646
  71.3 4.4 %collective-permute-start.19 = (f32[16,128]{1,0:T(8,128)S(1)}, f32[16,128]{1,0:T(8,128)S(1)}, u32[]{:S(2)}, u32[]{:S(2)}) collective-permute-start(f32[16,128]{1,0:T(8,128)S(1)} %pad_maximum_fusion.1.both), channel_id=1, source_target_pairs={{0,8},{8,16},{12,4},{16,24},{20,12},{24,32},{28,20},{32,40},{36,28... | collective-permute-start | bytes 24584 | tf_op jit(solution)/shard_map/ppermute | solution.py:646
  75.7 3.3 %collective-permute-done.19.ahead = f32[16,128]{1,0:T(8,128)S(1)} collective-permute-done((f32[16,128]{1,0:T(8,128)S(1)}, f32[16,128]{1,0:T(8,128)S(1)}, u32[]{:S(2)}, u32[]{:S(2)}) %collective-permute-start.19) | collective-permute-done | bytes 8224 | tf_op jit(solution)/shard_map/ppermute | solution.py:646
  79.0 1.2 %collective-permute-done.20.behind = f32[16,128]{1,0:T(8,128)S(1)} collective-permute-done((f32[16,128]{1,0:T(8,128)S(1)}, f32[16,128]{1,0:T(8,128)S(1)}, u32[]{:S(2)}, u32[]{:S(2)}) %collective-permute-start.20) | collective-permute-done | bytes 8224 | tf_op jit(solution)/shard_map/ppermute | solution.py:646
  80.2 3.6 %second_step.1 = (f32[1,64]{1,0:T(1,128)}, f32[4096,128]{1,0:T(8,128)}) custom-call(s32[1,2]{1,0:T(1,128)S(1)} %copy-done.2, s32[1,1]{1,0:T(1,128)} %bitcast.29.shifts, f32[16,128]{1,0:T(8,128)S(1)} %pad_maximum_fusion.1.both, f32[16,128]{1,0:T(8,128)S(1)} %collective-permute-done.19.ahead, f32[32,128]{1,0:T(8,128)S(1)} %collective-permute-done.18.third, ...), custom_call_target="tpu_custom_call" | custom-call | tf_op jit(solution)/shard_map/second_step/pallas_call | solution.py:704
  (36 shorter events, 1.3 us)
Async XLA Ops:
  0.6 20.9 %collective-permute-start.5 = (f32[1,8,65536]{2,1,0:T(8,128)}, f32[1,8,65536]{2,1,0:T(8,128)}, u32[]{:S(2)}, u32[]{:S(2)}) collective-permute-start(f32[1,8,65536]{2,1,0:T(8,128)} %param.7), channel_id=1, source_target_pairs={{0,4},{4,0},{8,12},{12,8},{16,20},{20,16},{24,28},{28,24},{32,36},... | collective-permute-start | bytes 6291464 | tf_op jit(solution)/shard_map/ppermute | solution.py:646
  0.7 29.7 %collective-permute-start.6 = (f32[1,8,65536]{2,1,0:T(8,128)}, f32[1,8,65536]{2,1,0:T(8,128)S(1)}, u32[]{:S(2)}, u32[]{:S(2)}) collective-permute-start(f32[1,8,65536]{2,1,0:T(8,128)} %param.7), channel_id=1, source_target_pairs={{4,8},{8,4},{12,16},{16,12},{20,24},{24,20},{28,32},{32,28},{36,40... | collective-permute-start | bytes 6291464 | tf_op jit(solution)/shard_map/ppermute | solution.py:646
  5.7 7.6 %collective-permute-start = (f32[1,64]{1,0:T(1,128)}, f32[1,64]{1,0:T(1,128)S(1)}, u32[]{:S(2)}, u32[]{:S(2)}) collective-permute-start(f32[1,64]{1,0:T(1,128)} %start.1), channel_id=1, source_target_pairs={{0,1},{1,2},{2,3},{3,0},{4,5},{5,6},{6,7},{7,4},{8,9},{9,10},{10,1... | collective-permute-start | bytes 776 | tf_op jit(solution)/shard_map/ppermute | solution.py:650
  7.7 5.6 %collective-permute-start.1 = (f32[1,64]{1,0:T(1,128)}, f32[1,64]{1,0:T(1,128)S(1)}, u32[]{:S(2)}, u32[]{:S(2)}) collective-permute-start(f32[1,64]{1,0:T(1,128)} %start.1), channel_id=1, source_target_pairs={{0,2},{1,3},{2,0},{3,1},{4,6},{5,7},{6,4},{7,5},{8,10},{9,11},{10,... | collective-permute-start | bytes 776 | tf_op jit(solution)/shard_map/ppermute | solution.py:650
  11.2 3.7 %collective-permute-start.2 = (f32[1,64]{1,0:T(1,128)}, f32[1,64]{1,0:T(1,128)S(1)}, u32[]{:S(2)}, u32[]{:S(2)}) collective-permute-start(f32[1,64]{1,0:T(1,128)} %start.1), channel_id=1, source_target_pairs={{0,3},{1,0},{2,1},{3,2},{4,7},{5,4},{6,5},{7,6},{8,11},{9,8},{10,9... | collective-permute-start | bytes 776 | tf_op jit(solution)/shard_map/ppermute | solution.py:650
  15.6 11.0 %collective-permute-start.3 = (f32[6,64]{1,0:T(8,128)S(1)}, f32[6,64]{1,0:T(8,128)S(1)}, u32[]{:S(2)}, u32[]{:S(2)}) collective-permute-start(f32[6,64]{1,0:T(8,128)S(1)} %concatenate.9.column), channel_id=1, source_target_pairs={{0,4},{4,0},{8,12},{12,8},{16,20},{20,16},{24,28},{28,24},{32,36},... | collective-permute-start | bytes 4616 | tf_op jit(solution)/shard_map/ppermute | solution.py:646
  15.7 14.8 %collective-permute-start.4 = (f32[6,64]{1,0:T(8,128)S(1)}, f32[6,64]{1,0:T(8,128)S(1)}, u32[]{:S(2)}, u32[]{:S(2)}) collective-permute-start(f32[6,64]{1,0:T(8,128)S(1)} %concatenate.9.column), channel_id=1, source_target_pairs={{4,8},{8,4},{12,16},{16,12},{20,24},{24,20},{28,32},{32,28},{36,40... | collective-permute-start | bytes 4616 | tf_op jit(solution)/shard_map/ppermute | solution.py:646
  18.5 2.2 %copy-start.1 = (f32[1,8,65536]{2,1,0:T(8,128)S(1)}, f32[1,8,65536]{2,1,0:T(8,128)}, u32[]{:S(2)}) copy-start(f32[1,8,65536]{2,1,0:T(8,128)} %param.6) | copy-start | bytes 6291460
  21.5 8.9 %copy-start.2 = (s32[1,2]{1,0:T(1,128)S(1)}, s32[1,2]{1,0:T(1,128)}, u32[]{:S(2)}) copy-start(s32[1,2]{1,0:T(1,128)} %blocks.5) | copy-start | bytes 28
  30.5 25.9 %copy-start.3 = (f32[1,64]{1,0:T(1,128)S(1)}, f32[1,64]{1,0:T(1,128)}, u32[]{:S(2)}) copy-start(f32[1,64]{1,0:T(1,128)} %start.1) | copy-start | bytes 772
  30.5 49.7 %copy-start = (f32[1,8,65536]{2,1,0:T(8,128)S(1)}, f32[1,8,65536]{2,1,0:T(8,128)}, u32[]{:S(2)}) copy-start(f32[1,8,65536]{2,1,0:T(8,128)} %param.7) | copy-start | bytes 6291460
  36.0 6.6 %collective-permute-start.7 = (f32[8,128]{1,0:T(8,128)S(1)}, f32[8,128]{1,0:T(8,128)S(1)}, u32[]{:S(2)}, u32[]{:S(2)}) collective-permute-start(f32[8,128]{1,0:T(8,128)S(1)} %get-tuple-element.26), channel_id=1, source_target_pairs={{0,1},{1,2},{2,3},{3,0},{4,5},{5,6},{6,7},{7,4},{8,9},{9,10},{10,1... | collective-permute-start | bytes 12296 | tf_op jit(solution)/shard_map/ppermute | solution.py:650
  38.0 5.2 %collective-permute-start.8 = (f32[8,128]{1,0:T(8,128)S(1)}, f32[8,128]{1,0:T(8,128)S(1)}, u32[]{:S(2)}, u32[]{:S(2)}) collective-permute-start(f32[8,128]{1,0:T(8,128)S(1)} %get-tuple-element.26), channel_id=1, source_target_pairs={{0,2},{1,3},{2,0},{3,1},{4,6},{5,7},{6,4},{7,5},{8,10},{9,11},{10,... | collective-permute-start | bytes 12296 | tf_op jit(solution)/shard_map/ppermute | solution.py:650
  41.6 3.6 %collective-permute-start.9 = (f32[8,128]{1,0:T(8,128)S(1)}, f32[8,128]{1,0:T(8,128)S(1)}, u32[]{:S(2)}, u32[]{:S(2)}) collective-permute-start(f32[8,128]{1,0:T(8,128)S(1)} %get-tuple-element.26), channel_id=1, source_target_pairs={{0,3},{1,0},{2,1},{3,2},{4,7},{5,4},{6,5},{7,6},{8,11},{9,8},{10,9... | collective-permute-start | bytes 12296 | tf_op jit(solution)/shard_map/ppermute | solution.py:650
  45.2 2.4 %collective-permute-start.10 = (f32[8,128]{1,0:T(8,128)S(1)}, f32[8,128]{1,0:T(8,128)S(1)}, u32[]{:S(2)}, u32[]{:S(2)}) collective-permute-start(f32[8,128]{1,0:T(8,128)S(1)} %add_add_fusion.1), channel_id=1, source_target_pairs={{0,4},{4,0},{8,12},{12,8},{16,20},{20,16},{24,28},{28,24},{32,36},... | collective-permute-start | bytes 12296 | tf_op jit(solution)/shard_map/ppermute | solution.py:646
  45.2 10.0 %collective-permute-start.11 = (f32[32,128]{1,0:T(8,128)S(1)}, f32[32,128]{1,0:T(8,128)S(1)}, u32[]{:S(2)}, u32[]{:S(2)}) collective-permute-start(f32[32,128]{1,0:T(8,128)S(1)} %pad.21), channel_id=1, source_target_pairs={{4,16},{12,24},{16,4},{20,32},{24,12},{28,40},{32,20},{36,48},{40,... | collective-permute-start | bytes 49160 | tf_op jit(solution)/shard_map/ppermute | solution.py:646
  47.6 7.7 %collective-permute-start.12 = (f32[16,128]{1,0:T(8,128)S(1)}, f32[16,128]{1,0:T(8,128)S(1)}, u32[]{:S(2)}, u32[]{:S(2)}) collective-permute-start(f32[16,128]{1,0:T(8,128)S(1)} %pad_maximum_fusion.both), channel_id=1, source_target_pairs={{0,8},{8,16},{12,4},{16,24},{20,12},{24,32},{28,20},{32,40},{36,28... | collective-permute-start | bytes 24584 | tf_op jit(solution)/shard_map/ppermute | solution.py:646
  55.2 1.2 %collective-permute-start.13 = (f32[16,128]{1,0:T(8,128)S(1)}, f32[16,128]{1,0:T(8,128)S(1)}, u32[]{:S(2)}, u32[]{:S(2)}) collective-permute-start(f32[16,128]{1,0:T(8,128)S(1)} %collective-permute-done.12.ahead), channel_id=1, source_target_pairs={{0,4},{4,0},{8,12},{12,8},{16,20},{20,16},{24,28},{28,24},{32,36},... | collective-permute-start | bytes 24584 | tf_op jit(solution)/shard_map/ppermute | solution.py:646
  61.4 4.9 %collective-permute-start.14 = (f32[8,128]{1,0:T(8,128)S(1)}, f32[8,128]{1,0:T(8,128)S(1)}, u32[]{:S(2)}, u32[]{:S(2)}) collective-permute-start(f32[8,128]{1,0:T(8,128)S(1)} %get-tuple-element.31), channel_id=1, source_target_pairs={{0,1},{1,2},{2,3},{3,0},{4,5},{5,6},{6,7},{7,4},{8,9},{9,10},{10,1... | collective-permute-start | bytes 12296 | tf_op jit(solution)/shard_map/ppermute | solution.py:650
  61.7 5.1 %collective-permute-start.15 = (f32[8,128]{1,0:T(8,128)S(1)}, f32[8,128]{1,0:T(8,128)S(1)}, u32[]{:S(2)}, u32[]{:S(2)}) collective-permute-start(f32[8,128]{1,0:T(8,128)S(1)} %get-tuple-element.31), channel_id=1, source_target_pairs={{0,2},{1,3},{2,0},{3,1},{4,6},{5,7},{6,4},{7,5},{8,10},{9,11},{10,... | collective-permute-start | bytes 12296 | tf_op jit(solution)/shard_map/ppermute | solution.py:650
  65.2 3.6 %collective-permute-start.16 = (f32[8,128]{1,0:T(8,128)S(1)}, f32[8,128]{1,0:T(8,128)S(1)}, u32[]{:S(2)}, u32[]{:S(2)}) collective-permute-start(f32[8,128]{1,0:T(8,128)S(1)} %get-tuple-element.31), channel_id=1, source_target_pairs={{0,3},{1,0},{2,1},{3,2},{4,7},{5,4},{6,5},{7,6},{8,11},{9,8},{10,9... | collective-permute-start | bytes 12296 | tf_op jit(solution)/shard_map/ppermute | solution.py:650
  68.8 2.5 %collective-permute-start.17 = (f32[8,128]{1,0:T(8,128)S(1)}, f32[8,128]{1,0:T(8,128)S(1)}, u32[]{:S(2)}, u32[]{:S(2)}) collective-permute-start(f32[8,128]{1,0:T(8,128)S(1)} %add_add_fusion), channel_id=1, source_target_pairs={{0,4},{4,0},{8,12},{12,8},{16,20},{20,16},{24,28},{28,24},{32,36},... | collective-permute-start | bytes 12296 | tf_op jit(solution)/shard_map/ppermute | solution.py:646
  68.8 10.2 %collective-permute-start.18 = (f32[32,128]{1,0:T(8,128)S(1)}, f32[32,128]{1,0:T(8,128)S(1)}, u32[]{:S(2)}, u32[]{:S(2)}) collective-permute-start(f32[32,128]{1,0:T(8,128)S(1)} %pad.22), channel_id=1, source_target_pairs={{4,16},{12,24},{16,4},{20,32},{24,12},{28,40},{32,20},{36,48},{40,... | collective-permute-start | bytes 49160 | tf_op jit(solution)/shard_map/ppermute | solution.py:646
  71.3 7.7 %collective-permute-start.19 = (f32[16,128]{1,0:T(8,128)S(1)}, f32[16,128]{1,0:T(8,128)S(1)}, u32[]{:S(2)}, u32[]{:S(2)}) collective-permute-start(f32[16,128]{1,0:T(8,128)S(1)} %pad_maximum_fusion.1.both), channel_id=1, source_target_pairs={{0,8},{8,16},{12,4},{16,24},{20,12},{24,32},{28,20},{32,40},{36,28... | collective-permute-start | bytes 24584 | tf_op jit(solution)/shard_map/ppermute | solution.py:646
  79.0 1.2 %collective-permute-start.20 = (f32[16,128]{1,0:T(8,128)S(1)}, f32[16,128]{1,0:T(8,128)S(1)}, u32[]{:S(2)}, u32[]{:S(2)}) collective-permute-start(f32[16,128]{1,0:T(8,128)S(1)} %collective-permute-done.19.ahead), channel_id=1, source_target_pairs={{0,4},{4,0},{8,12},{12,8},{16,20},{20,16},{24,28},{28,24},{32,36},... | collective-permute-start | bytes 24584 | tf_op jit(solution)/shard_map/ppermute | solution.py:646
